TPU v7x, 256 devices: a whole 4x4x8 slice. The times are simulated.
256 devices in a mesh: dp: 4 (over x), fsdp: 64 (over z, y, core).
Axes of the slice: x: 4, y: 4, z: 8, core: 2. Of those that a mesh axis runs over, the one named last changes fastest.
Arguments:
- grad_query: bfloat16 [4, 4, 64, 192, 1536], P('dp', None, None, 'fsdp'), may hold values from -60 to 60
- grad_kv: bfloat16 [4, 4, 64, 256, 512], P('dp', None, None, 'fsdp'), may hold values from -60 to 60
- momentum_query: bfloat16 [4, 64, 2, 192, 1536], P('dp', 'fsdp'), may hold values from -120 to 120, as said below
- momentum_kv: bfloat16 [4, 64, 2, 256, 512], P('dp', 'fsdp'), may hold values from -120 to 120, as said below
- weight_query: float32 [4, 64, 192, 1536], P(None, 'dp', 'fsdp'), may hold values from -6 to 6
- weight_kv: float32 [4, 64, 256, 512], P(None, 'dp', 'fsdp'), may hold values from -6 to 6
- owner_query: int32 [4, 4, 16, 1], replicated, may hold values from 0 to 63; in each aligned block of 64 rows (0 to 63, 64 to 127, ..., all dimensions but the last counted through in order) at most 2 rows name the same one
- owner_kv: int32 [4, 4, 16, 1], replicated, may hold values from 0 to 63; in each aligned block of 64 rows (0 to 63, 64 to 127, ..., all dimensions but the last counted through in order) at most 2 rows name the same one
- max_logits: float32 [256, 4, 64], P(('dp', 'fsdp')), may hold values from 1 to 1500
Outputs:
- query_update: bfloat16 [4, 64, 192, 1536], P(None, 'dp', 'fsdp')
- kv_update: bfloat16 [4, 64, 256, 512], P(None, 'dp', 'fsdp')
- query_weight_new: float32 [4, 64, 192, 1536], P(None, 'dp', 'fsdp')
- kv_weight_new: float32 [4, 64, 256, 512], P(None, 'dp', 'fsdp')
- query_momentum_new: bfloat16 [4, 64, 2, 192, 1536], P('dp', 'fsdp')
- kv_momentum_new: bfloat16 [4, 64, 2, 256, 512], P('dp', 'fsdp')
Inputs may be any that keep to these rules, and one draw needn't show every extreme that they name: `owner_query`: within one group's 4 * 16 blocks no owner has more than 2; in some group one owner has exactly 2. `owner_kv`: within one group's 4 * 16 blocks no owner has more than 2; in some group one owner has exactly 2. `momentum_query`: slots at or past an owner's number of blocks in the group are not read. `momentum_kv`: slots at or past an owner's number of blocks in the group are not read.
All inputs are finite; a program needn't handle non-finite values.
Results may differ from a plain program's by a relative error of at most 0.019.
Values may be sent and summed in bfloat16 or wider, within the bound.
No kernel may reach another device: no remote copies, remote signals or barrier semaphores. Data moves between devices by JAX's collectives and lax.ppermute only.
A program may use at most 64 MiB of HBM per device.

v0:
```python
import math

import jax
import jax.numpy as jnp
from jax import lax
from jax.sharding import PartitionSpec as P

QN = 128
KN = 128
STEPS = 5


MOMENTUM_RATE = 0.95
LEARN_RATE = 0.02
DECAY_RATE = 0.1
CLIP_LEVEL = 100.0
NEWTON_FIRST = 3.4445
NEWTON_SECOND = -4.775
NEWTON_THIRD = 2.0315
EPSILON = 1e-07


def owner_slots(owners, node_count):
    hits = (owners[:, None] == jnp.arange(node_count, dtype=jnp.int32)[None, :]).astype(jnp.int32)
    before = jnp.cumsum(hits, axis=0) - hits
    return (jnp.sum(before * hits, axis=1), jnp.sum(hits, axis=0))


def dispatch_table(owners, node_count, capacity):
    slot_index, filled = owner_slots(owners, node_count)
    target = slot_index * node_count + owners
    dispatch = (
        jnp.arange(capacity * node_count, dtype=jnp.int32)[:, None] == target[None, :]
    ).astype(jnp.bfloat16)
    return (dispatch, filled)


def pack_slots(dispatch, grouped, node_count):
    matrices, row_count, col_count = grouped.shape
    packed = jnp.dot(
        dispatch,
        grouped.reshape(matrices, row_count * col_count),
        preferred_element_type=jnp.float32,
    )
    return packed.astype(jnp.bfloat16).reshape(
        dispatch.shape[0] // node_count, node_count * row_count, col_count
    )


def unpack_slots(dispatch, returned, node_count):
    capacity, total_rows, col_count = returned.shape
    row_count = total_rows // node_count
    flattened = returned.reshape(capacity * node_count, row_count * col_count)
    own_rows = lax.dot_general(
        dispatch, flattened, (((0,), (0,)), ((), ())), preferred_element_type=jnp.float32
    )
    return own_rows.astype(jnp.bfloat16).reshape(dispatch.shape[1], row_count, col_count)


def batched_newton(direction):
    frobenius = jnp.sqrt(jnp.sum(direction * direction, axis=(1, 2), keepdims=True))
    scaled = direction / (frobenius + EPSILON)
    for iteration in range(STEPS):
        square = jnp.einsum("sij,skj->sik", scaled, scaled, precision=lax.Precision.HIGHEST)
        polynomial = NEWTON_SECOND * square + NEWTON_THIRD * jnp.einsum(
            "sij,sjk->sik", square, square, precision=lax.Precision.HIGHEST
        )
        scaled = NEWTON_FIRST * scaled + jnp.einsum(
            "sij,sjk->sik", polynomial, scaled, precision=lax.Precision.HIGHEST
        )
    return scaled


def owner_step(arrived, previous, filled_here):
    capacity, row_count, col_count = arrived.shape
    in_use = (jnp.arange(capacity, dtype=jnp.int32) < filled_here)[:, None, None]
    gradient = arrived.astype(jnp.float32)
    carried = MOMENTUM_RATE * previous.astype(jnp.float32) + gradient
    direction = jnp.where(in_use, gradient + MOMENTUM_RATE * carried, 0.0)
    orthogonal = batched_newton(direction)
    scale_factor = 0.2 * math.sqrt(max(row_count, col_count))
    renewed = jnp.where(in_use, carried, 0.0).astype(jnp.bfloat16)
    return (renewed, (orthogonal * scale_factor).astype(jnp.bfloat16))


def step_weights(weight, update, factor):
    stepped = weight - LEARN_RATE * (update.astype(jnp.float32) + DECAY_RATE * weight)
    return stepped * factor


def on_device(
    grad_query,
    grad_kv,
    momentum_query,
    momentum_kv,
    weight_query,
    weight_kv,
    owner_query,
    owner_kv,
    max_logits,
):
    node_count = lax.axis_size("fsdp")
    group_count = lax.axis_size("dp")
    my_group = lax.axis_index("dp")
    my_node = lax.axis_index("fsdp")
    layers = grad_query.shape[1]
    head_count = grad_query.shape[2]
    per_group = head_count // group_count
    matrices = layers * per_group
    capacity = momentum_query.shape[2]
    query_rows = grad_query.shape[3]
    kv_rows = grad_kv.shape[3]
    query_cols = grad_query.shape[4]
    kv_cols = grad_kv.shape[4]
    all_query = owner_query.reshape(group_count, matrices)
    all_kv = owner_kv.reshape(group_count, matrices)
    query_owned = lax.dynamic_index_in_dim(all_query, my_group, 0, keepdims=False)
    kv_owned = lax.dynamic_index_in_dim(all_kv, my_group, 0, keepdims=False)
    query_dispatch, query_filled = dispatch_table(query_owned, node_count, capacity)
    kv_dispatch, kv_filled = dispatch_table(kv_owned, node_count, capacity)
    query_summed, kv_summed = (
        lax.psum_scatter(
            grad_query[0].astype(jnp.float32).astype(jnp.bfloat16),
            "dp",
            scatter_dimension=1,
            tiled=True,
        ).astype(jnp.float32),
        lax.psum_scatter(
            grad_kv[0].astype(jnp.float32).astype(jnp.bfloat16),
            "dp",
            scatter_dimension=1,
            tiled=True,
        ).astype(jnp.float32),
    )
    query_reduced = query_summed.astype(jnp.bfloat16).reshape(matrices, query_rows, query_cols)
    kv_reduced = kv_summed.astype(jnp.bfloat16).reshape(matrices, kv_rows, kv_cols)
    query_buckets = pack_slots(query_dispatch, query_reduced, node_count)
    kv_buckets = pack_slots(kv_dispatch, kv_reduced, node_count)
    query_arrived, kv_arrived = (
        lax.all_to_all(query_buckets, "fsdp", split_axis=1, concat_axis=1, tiled=True),
        lax.all_to_all(kv_buckets, "fsdp", split_axis=1, concat_axis=1, tiled=True),
    )
    query_count = lax.dynamic_index_in_dim(query_filled, my_node, 0, keepdims=False)
    kv_count = lax.dynamic_index_in_dim(kv_filled, my_node, 0, keepdims=False)
    query_renewed, query_outgoing = owner_step(query_arrived, momentum_query[0, 0], query_count)
    kv_renewed, kv_outgoing = owner_step(kv_arrived, momentum_kv[0, 0], kv_count)
    query_back, kv_back = (
        lax.all_to_all(query_outgoing, "fsdp", split_axis=1, concat_axis=1, tiled=True),
        lax.all_to_all(kv_outgoing, "fsdp", split_axis=1, concat_axis=1, tiled=True),
    )
    query_update = unpack_slots(query_dispatch, query_back, node_count).reshape(
        layers, per_group, query_rows, query_cols
    )
    kv_update = unpack_slots(kv_dispatch, kv_back, node_count).reshape(
        layers, per_group, kv_rows, kv_cols
    )
    merged = lax.pmax(max_logits, ("dp", "fsdp"))[0]
    group_peak = lax.dynamic_slice_in_dim(merged, my_group * per_group, per_group, 1)
    shrink = jnp.minimum(1.0, CLIP_LEVEL / group_peak)
    root_shrink = jnp.sqrt(shrink)
    query_index = my_node * query_rows + jnp.arange(query_rows, dtype=jnp.int32)
    kv_index = my_node * kv_rows + jnp.arange(kv_rows, dtype=jnp.int32)
    query_factor = jnp.where(
        query_index[None, None, :, None] < QN,
        root_shrink[:, :, None, None],
        shrink[:, :, None, None],
    )
    kv_factor = jnp.where(kv_index[None, None, :, None] < KN, root_shrink[:, :, None, None], 1.0)
    query_weight_new = step_weights(weight_query, query_update, query_factor)
    kv_weight_new = step_weights(weight_kv, kv_update, kv_factor)
    return (
        query_update,
        kv_update,
        query_weight_new,
        kv_weight_new,
        query_renewed[None, None],
        kv_renewed[None, None],
    )


def solution(mesh):
    return jax.shard_map(
        on_device,
        mesh=mesh,
        in_specs=(
            P("dp", None, None, "fsdp", None),
            P("dp", None, None, "fsdp", None),
            P("dp", "fsdp", None, None, None),
            P("dp", "fsdp", None, None, None),
            P(None, "dp", "fsdp", None),
            P(None, "dp", "fsdp", None),
            P(),
            P(),
            P(("dp", "fsdp"), None, None),
        ),
        out_specs=(
            P(None, "dp", "fsdp", None),
            P(None, "dp", "fsdp", None),
            P(None, "dp", "fsdp", None),
            P(None, "dp", "fsdp", None),
            P("dp", "fsdp", None, None, None),
            P("dp", "fsdp", None, None, None),
        ),
        check_vma=False,
    )
```

profile of v0, /device:TPU:2, one launch (start us, length us, event | category | flops | bytes accessed | tf_op | source)
XLA Modules:
  0.0 272.0 jit_solution(6532126027700873748)
XLA Ops:
  14.2 24.1 %reduce-scatter.8.cloned.1.call-done = bf16[16,8192]{1,0:T(8,128)(2,1)} async-done(((bf16[64,8192]{1,0:T(8,128)(2,1)}), bf16[16,8192]{1,0:T(8,128)(2,1)}) %reduce-scatter.8.cloned.1.call-update) | async-done | bytes 262160
  41.5 10.7 %all-to-all-start.2 = ((bf16[2,256,512]{2,0,1:T(2,128)(2,1)}), bf16[2,256,512]{2,0,1:T(2,128)(2,1)S(1)}, u32[]{:S(2)}, u32[]{:S(2)}) async-start(bf16[2,256,512]{2,0,1:T(2,128)(2,1)} %copy.38), calls=%async_computation.3 | async-start | bytes 1048576 | tf_op jit(solution)/shard_map/all_to_all | solution.py:141
  54.7 15.1 %all-to-all-done.2 = bf16[2,256,512]{2,0,1:T(2,128)(2,1)S(1)} async-done(((bf16[2,256,512]{2,0,1:T(2,128)(2,1)}), bf16[2,256,512]{2,0,1:T(2,128)(2,1)S(1)}, u32[]{:S(2)}, u32[]{:S(2)}) %all-to-all-start.2) | async-done | bytes 524320 | tf_op jit(solution)/shard_map/all_to_all | solution.py:141
  71.0 1.7 fusion.35
  81.5 3.5 %copy.34 = bf16[2,192,1536]{2,0,1:T(2,128)(2,1)} copy(bf16[2,192,1536]{2,1,0:T(8,128)(2,1)} %reshape.120) | data formatting | bytes 2359296 | tf_op jit(solution)/shard_map/reshape | solution.py:45
  85.0 8.7 %all-to-all-start = ((bf16[2,192,1536]{2,0,1:T(2,128)(2,1)}), bf16[2,192,1536]{2,0,1:T(2,128)(2,1)S(1)}, u32[]{:S(2)}, u32[]{:S(2)}) async-start(bf16[2,192,1536]{2,0,1:T(2,128)(2,1)} %copy.34), calls=%async_computation.1 | async-start | bytes 2359296 | tf_op jit(solution)/shard_map/all_to_all | solution.py:140
  103.9 21.5 %all-to-all-done = bf16[2,192,1536]{2,0,1:T(2,128)(2,1)S(1)} async-done(((bf16[2,192,1536]{2,0,1:T(2,128)(2,1)}), bf16[2,192,1536]{2,0,1:T(2,128)(2,1)S(1)}, u32[]{:S(2)}, u32[]{:S(2)}) %all-to-all-start) | async-done | bytes 1179680 | tf_op jit(solution)/shard_map/all_to_all | solution.py:140
  125.5 5.7 %all-to-all-start.3 = ((bf16[2,256,512]{2,0,1:T(2,128)(2,1)}), bf16[2,256,512]{2,0,1:T(2,128)(2,1)S(1)}, u32[]{:S(2)}, u32[]{:S(2)}) async-start(bf16[2,256,512]{2,0,1:T(2,128)(2,1)} %copy.40), calls=%async_computation.4 | async-start | bytes 1048576 | tf_op jit(solution)/shard_map/all_to_all | solution.py:149
  131.2 3.2 %fusion.19 = (bf16[1,1,2,192,1536]{4,3,2,1,0:T(8,128)(2,1)}, f32[2]{0:T(128)S(1)}) fusion(bf16[1,1,2,192,1536]{4,3,2,1,0:T(8,128)(2,1)} %param.11, pred[2]{0:T(512)(128)(4,1)S(1)} %iota_compare_fusion.9, bf16[2,192,1536]{2,0,1:T(2,128)(2,1)S(1)} %all-to-all-done), kind=kLoop, calls=%fused_computation.51 | loop fusion | flops 6488062 | bytes 3538954 | tf_op jit(solution)/shard_map/broadcast_in_dim | solution.py:176
  134.4 3.5 %fusion.38 = f32[2,192,192]{2,1,0:T(8,128)S(1)} fusion(bf16[1,1,2,192,1536]{4,3,2,1,0:T(8,128)(2,1)S(1)} %copy-done.1, f32[2]{0:T(128)S(1)} %sqrt_add_fusion.1, pred[2]{0:T(512)(128)(4,1)S(1)} %iota_compare_fusion.9, bf16[2,192,1536]{2,0,1:T(2,128)(2,1)S(1)} %all-to-all-done), kind=kOutput, calls=%fused_computation.91 | convolution fusion | flops 1363673088 | bytes 2654218 | tf_op jit(solution)/shard_map/sij,skj->sik/dot_general | solution.py:64
  138.5 3.4 %convolution_add_fusion.4 = f32[2,192,1536]{2,1,0:T(8,128)S(1)} fusion(f32[2,192,192]{2,1,0:T(8,128)S(1)} %fusion.18, f32[2]{0:T(128)S(1)} %sqrt_add_fusion.1, bf16[1,1,2,192,1536]{4,3,2,1,0:T(8,128)(2,1)S(1)} %copy-done.1, bf16[2,192,1536]{2,0,1:T(2,128)(2,1)S(1)} %all-to-all-done, pred[2]{0:T(512)(128)(4,1)S(1)} %iota_compare_fusion.9), kind=kOutput, calls=%fused_computation.7 | convolution fusion | flops 1369571328 | bytes 5013514 | tf_op jit(solution)/shard_map/sij,sjk->sik/dot_general | solution.py:68
  141.9 2.3 fusion.42
  144.7 2.6 convolution_add_fusion.3
  147.4 2.3 fusion.43
  150.2 2.4 convolution_add_fusion.2
  152.6 2.3 fusion.44
  155.4 2.4 convolution_add_fusion.1
  157.8 2.5 fusion.45
  160.9 2.3 fusion.1
  163.3 2.2 copy.36
  165.5 10.3 %all-to-all-start.1 = ((bf16[2,192,1536]{2,0,1:T(2,128)(2,1)}), bf16[2,192,1536]{2,0,1:T(2,128)(2,1)S(1)}, u32[]{:S(2)}, u32[]{:S(2)}) async-start(bf16[2,192,1536]{2,0,1:T(2,128)(2,1)} %copy.36), calls=%async_computation.2 | async-start | bytes 2359296 | tf_op jit(solution)/shard_map/all_to_all | solution.py:148
  175.8 78.9 %pmax.7 = f32[1,4,64]{2,1,0:T(4,128)S(1)} all-reduce(f32[1,4,64]{2,1,0:T(4,128)S(1)} %copy-done.6), channel_id=1, replica_groups=mesh['dp'=4,'fsdp'=64] {'dp','fsdp'}, use_global_device_ids=true, to_apply=%region_10.11 | all-reduce | flops 256 | bytes 2048 | tf_op jit(solution)/shard_map/pmax | solution.py:157
  255.8 2.2 subtract_multiply_fusion
  260.5 2.8 %fusion.4 = f32[4,16,3,1536]{3,2,1,0:T(4,128)S(1)} fusion(f32[4,16,3,1536]{3,1,2,0:T(8,128)} %param.13, bf16[4,16,3,1536]{3,2,1,0:T(4,128)(2,1)S(1)} %reshape_reshape.13, f32[4,16,3]{2,1,0:T(8,128)S(1)} %broadcast_select_fusion.1), kind=kLoop, calls=%fused_computation.19 | loop fusion | flops 1769472 | bytes 2949888 | tf_op jit(solution)/shard_map/mul | solution.py:88
  (89 shorter events, 40.4 us)
Async XLA Ops:
  7.2 1.2 copy-start
  7.2 31.1 %reduce-scatter.8.cloned.1.call-start = ((), (), s32[]{:S(2)}) async-start(), calls=%async_computation.7 | async-start | bytes 1310720
  9.0 2.9 %copy-start.4 = (s32[4,4,16,1]{2,3,1,0:T(1,128)S(1)}, s32[4,4,16,1]{2,3,1,0:T(1,128)}, u32[]{:S(2)}) copy-start(s32[4,4,16,1]{2,3,1,0:T(1,128)} %param.15) | copy-start | bytes 3076
  9.0 3.9 %copy-start.5 = (s32[4,4,16,1]{2,3,1,0:T(1,128)S(1)}, s32[4,4,16,1]{2,3,1,0:T(1,128)}, u32[]{:S(2)}) copy-start(s32[4,4,16,1]{2,3,1,0:T(1,128)} %param.16) | copy-start | bytes 3076
  10.6 67.4 %reduce-scatter.6.cloned.1.call-start = ((), (), s32[]{:S(2)}) async-start(), calls=%async_computation.6 | async-start | bytes 2949120 | tf_op jit(solution)/shard_map/reduce_scatter | solution.py:122
  39.5 30.3 %copy-start.3 = (bf16[1,1,2,256,512]{4,3,2,1,0:T(8,128)(2,1)S(1)}, bf16[1,1,2,256,512]{4,3,2,1,0:T(8,128)(2,1)}, u32[]{:S(2)}) copy-start(bf16[1,1,2,256,512]{4,3,2,1,0:T(8,128)(2,1)} %param.12) | copy-start | bytes 1572868
  41.5 28.3 %all-to-all-start.2 = ((bf16[2,256,512]{2,0,1:T(2,128)(2,1)}), bf16[2,256,512]{2,0,1:T(2,128)(2,1)S(1)}, u32[]{:S(2)}, u32[]{:S(2)}) async-start(bf16[2,256,512]{2,0,1:T(2,128)(2,1)} %copy.38), calls=%async_computation.3 | async-start | bytes 1048576 | tf_op jit(solution)/shard_map/all_to_all | solution.py:141
  85.0 40.4 %all-to-all-start = ((bf16[2,192,1536]{2,0,1:T(2,128)(2,1)}), bf16[2,192,1536]{2,0,1:T(2,128)(2,1)S(1)}, u32[]{:S(2)}, u32[]{:S(2)}) async-start(bf16[2,192,1536]{2,0,1:T(2,128)(2,1)} %copy.34), calls=%async_computation.1 | async-start | bytes 2359296 | tf_op jit(solution)/shard_map/all_to_all | solution.py:140
  125.5 40.1 %all-to-all-start.3 = ((bf16[2,256,512]{2,0,1:T(2,128)(2,1)}), bf16[2,256,512]{2,0,1:T(2,128)(2,1)S(1)}, u32[]{:S(2)}, u32[]{:S(2)}) async-start(bf16[2,256,512]{2,0,1:T(2,128)(2,1)} %copy.40), calls=%async_computation.4 | async-start | bytes 1048576 | tf_op jit(solution)/shard_map/all_to_all | solution.py:149
  131.2 3.2 %copy-start.1 = (bf16[1,1,2,192,1536]{4,3,2,1,0:T(8,128)(2,1)S(1)}, bf16[1,1,2,192,1536]{4,3,2,1,0:T(8,128)(2,1)}, u32[]{:S(2)}) copy-start(bf16[1,1,2,192,1536]{4,3,2,1,0:T(8,128)(2,1)} %param.11) | copy-start | bytes 3538948
  163.3 12.5 %copy-start.6 = (f32[1,4,64]{2,1,0:T(4,128)S(1)}, f32[1,4,64]{2,1,0:T(4,128)}, u32[]{:S(2)}) copy-start(f32[1,4,64]{2,1,0:T(4,128)} %param.17) | copy-start | bytes 3076
  165.5 92.5 %all-to-all-start.1 = ((bf16[2,192,1536]{2,0,1:T(2,128)(2,1)}), bf16[2,192,1536]{2,0,1:T(2,128)(2,1)S(1)}, u32[]{:S(2)}, u32[]{:S(2)}) async-start(bf16[2,192,1536]{2,0,1:T(2,128)(2,1)} %copy.36), calls=%async_computation.2 | async-start | bytes 2359296 | tf_op jit(solution)/shard_map/all_to_all | solution.py:148
  255.8 2.2 copy-start.2
Sparse Core Ops, SparseCore 0:
  11.1 27.1 reduce-scatter.7
  41.0 34.7 reduce-scatter.5
where the time goes:
time: 277 us; the launch traced here: 272 us
  blocking collectives  78.9 us (28%)
  waiting for transfers between devices  61.5 us (22%)
  matrix products  45.7 us (16%)
  starting transfers between devices  35.5 us (13%)
  local copies, waits for them, and re-layouts  22.4 us (8%)
  between operations  15 us (5%)
  other arithmetic  13.1 us (5%)
    pmax x1, blocking collectives, on_device(): merged = lax.pmax(max_logits, ('dp', 'fsdp'))[0]  78.9 us
    unnamed x3, waiting for transfers between devices  24.8 us
    all_to_all x1, waiting for transfers between devices, on_device(): lax.all_to_all(query_buckets, 'fsdp', split_axis=1, concat_axis=1, tiled=...  21.5 us
    dot_general x10, matrix products, batched_newton(): jnp.einsum('sij,skj->sik', scaled, scaled, precision=lax.Precision.HIGHEST)  19.2 us
    dot_general x10, matrix products, batched_newton(): jnp.einsum('sij,sjk->sik', polynomial, scaled, precision=lax.Precision.HI...  19 us
    all_to_all x1, waiting for transfers between devices, on_device(): lax.all_to_all(kv_buckets, 'fsdp', split_axis=1, concat_axis=1, tiled=True)  15.1 us
    all_to_all x1, starting transfers between devices, on_device(): lax.all_to_all(kv_buckets, 'fsdp', split_axis=1, concat_axis=1, tiled=True)  10.7 us
    all_to_all x1, starting transfers between devices, on_device(): lax.all_to_all(query_outgoing, 'fsdp', split_axis=1, concat_axis=1, tiled...  10.3 us
  transfers between devices with their start and end apart: 6, of which 3 were waited for; matrix products, arithmetic and copies ran while one was open for 24% of the time, Pallas kernels for 0%

commit v1 on v0

--- a/solution.py
+++ b/solution.py
@@ -154,8 +154,13 @@
     kv_update = unpack_slots(kv_dispatch, kv_back, node_count).reshape(
         layers, per_group, kv_rows, kv_cols
     )
-    merged = lax.pmax(max_logits, ("dp", "fsdp"))[0]
+    merged = lax.pmax(max_logits, "dp")[0]
     group_peak = lax.dynamic_slice_in_dim(merged, my_group * per_group, per_group, 1)
+    hop = 1
+    while hop < node_count:
+        pairs = [(i, (i + hop) % node_count) for i in range(node_count)]
+        group_peak = jnp.maximum(group_peak, lax.ppermute(group_peak, "fsdp", pairs))
+        hop *= 2
     shrink = jnp.minimum(1.0, CLIP_LEVEL / group_peak)
     root_shrink = jnp.sqrt(shrink)
     query_index = my_node * query_rows + jnp.arange(query_rows, dtype=jnp.int32)

time: 277 us -> 258 us (0.931)
  blocking collectives: 78.9 us -> 9.5 us
  waiting for transfers between devices: 61.5 us -> 107 us
  starting transfers between devices: 35.5 us -> 40.8 us
    pmax x1, blocking collectives: 78.9 us -> 9.5 us  [on_device(): merged = lax.pmax(max_logits, 'dp')[0]]
    ppermute x0 -> x6, waiting for transfers between devices: none -> 45.6 us  [on_device(): lax.ppermute(group_peak, 'fsdp', pairs)]
    ppermute x0 -> x6, starting transfers between devices: none -> 5.16 us  [on_device(): lax.ppermute(group_peak, 'fsdp', pairs)]
  transfers between devices with their start and end apart: 6 -> 12, of which waited for: 3 -> 9; matrix products, arithmetic and copies ran while one was open for 24% -> 25% of each run, Pallas kernels for 0% -> 0%
where the time goes in v1:
time: 258 us; the launch traced here: 253 us
  waiting for transfers between devices  107 us (41%)
  matrix products  45.9 us (18%)
  starting transfers between devices  40.8 us (16%)
  local copies, waits for them, and re-layouts  22.4 us (9%)
  between operations  14.8 us (6%)
  other arithmetic  13.1 us (5%)
  blocking collectives  9.5 us (4%)
    ppermute x6, waiting for transfers between devices, on_device(): lax.ppermute(group_peak, 'fsdp', pairs)  45.6 us
    unnamed x3, waiting for transfers between devices  24.8 us
    all_to_all x1, waiting for transfers between devices, on_device(): lax.all_to_all(query_buckets, 'fsdp', split_axis=1, concat_axis=1, tiled=...  21.5 us
    dot_general x10, matrix products, batched_newton(): jnp.einsum('sij,skj->sik', scaled, scaled, precision=lax.Precision.HIGHEST)  19.3 us
    dot_general x10, matrix products, batched_newton(): jnp.einsum('sij,sjk->sik', polynomial, scaled, precision=lax.Precision.HI...  19 us
    all_to_all x1, waiting for transfers between devices, on_device(): lax.all_to_all(kv_buckets, 'fsdp', split_axis=1, concat_axis=1, tiled=True)  15.1 us
    all_to_all x1, starting transfers between devices, on_device(): lax.all_to_all(kv_buckets, 'fsdp', split_axis=1, concat_axis=1, tiled=True)  10.7 us
    all_to_all x1, starting transfers between devices, on_device(): lax.all_to_all(query_outgoing, 'fsdp', split_axis=1, concat_axis=1, tiled...  10.3 us
  transfers between devices with their start and end apart: 12, of which 9 were waited for; matrix products, arithmetic and copies ran while one was open for 25% of the time, Pallas kernels for 0%

profile of v1, /device:TPU:2, one launch (start us, length us, event | category | flops | bytes accessed | tf_op | source)
XLA Modules:
  0.0 253.5 jit_solution(10182758150607750721)
XLA Ops:
  14.2 24.1 %reduce-scatter.8.cloned.1.call-done = bf16[16,8192]{1,0:T(8,128)(2,1)} async-done(((bf16[64,8192]{1,0:T(8,128)(2,1)}), bf16[16,8192]{1,0:T(8,128)(2,1)}) %reduce-scatter.8.cloned.1.call-update) | async-done | bytes 262160
  41.5 10.7 %all-to-all-start.2 = ((bf16[2,256,512]{2,0,1:T(2,128)(2,1)}), bf16[2,256,512]{2,0,1:T(2,128)(2,1)S(1)}, u32[]{:S(2)}, u32[]{:S(2)}) async-start(bf16[2,256,512]{2,0,1:T(2,128)(2,1)} %copy.38), calls=%async_computation.3 | async-start | bytes 1048576 | tf_op jit(solution)/shard_map/all_to_all | solution.py:141
  54.8 15.1 %all-to-all-done.2 = bf16[2,256,512]{2,0,1:T(2,128)(2,1)S(1)} async-done(((bf16[2,256,512]{2,0,1:T(2,128)(2,1)}), bf16[2,256,512]{2,0,1:T(2,128)(2,1)S(1)}, u32[]{:S(2)}, u32[]{:S(2)}) %all-to-all-start.2) | async-done | bytes 524320 | tf_op jit(solution)/shard_map/all_to_all | solution.py:141
  81.6 3.5 %copy.34 = bf16[2,192,1536]{2,0,1:T(2,128)(2,1)} copy(bf16[2,192,1536]{2,1,0:T(8,128)(2,1)} %reshape.108) | data formatting | bytes 2359296 | tf_op jit(solution)/shard_map/reshape | solution.py:45
  85.1 8.8 %all-to-all-start = ((bf16[2,192,1536]{2,0,1:T(2,128)(2,1)}), bf16[2,192,1536]{2,0,1:T(2,128)(2,1)S(1)}, u32[]{:S(2)}, u32[]{:S(2)}) async-start(bf16[2,192,1536]{2,0,1:T(2,128)(2,1)} %copy.34), calls=%async_computation.1 | async-start | bytes 2359296 | tf_op jit(solution)/shard_map/all_to_all | solution.py:140
  104.0 21.5 %all-to-all-done = bf16[2,192,1536]{2,0,1:T(2,128)(2,1)S(1)} async-done(((bf16[2,192,1536]{2,0,1:T(2,128)(2,1)}), bf16[2,192,1536]{2,0,1:T(2,128)(2,1)S(1)}, u32[]{:S(2)}, u32[]{:S(2)}) %all-to-all-start) | async-done | bytes 1179680 | tf_op jit(solution)/shard_map/all_to_all | solution.py:140
  125.6 5.7 %all-to-all-start.3 = ((bf16[2,256,512]{2,0,1:T(2,128)(2,1)}), bf16[2,256,512]{2,0,1:T(2,128)(2,1)S(1)}, u32[]{:S(2)}, u32[]{:S(2)}) async-start(bf16[2,256,512]{2,0,1:T(2,128)(2,1)} %copy.40), calls=%async_computation.4 | async-start | bytes 1048576 | tf_op jit(solution)/shard_map/all_to_all | solution.py:149
  131.3 3.2 %fusion.19 = (bf16[1,1,2,192,1536]{4,3,2,1,0:T(8,128)(2,1)}, f32[2]{0:T(128)S(1)}) fusion(bf16[1,1,2,192,1536]{4,3,2,1,0:T(8,128)(2,1)} %param.11, pred[2]{0:T(512)(128)(4,1)S(1)} %iota_compare_fusion.9, bf16[2,192,1536]{2,0,1:T(2,128)(2,1)S(1)} %all-to-all-done), kind=kLoop, calls=%fused_computation.51 | loop fusion | flops 6488062 | bytes 3538954 | tf_op jit(solution)/shard_map/broadcast_in_dim | solution.py:181
  134.5 3.5 %fusion.38 = f32[2,192,192]{2,1,0:T(8,128)S(1)} fusion(bf16[1,1,2,192,1536]{4,3,2,1,0:T(8,128)(2,1)S(1)} %copy-done.1, f32[2]{0:T(128)S(1)} %sqrt_add_fusion.1, pred[2]{0:T(512)(128)(4,1)S(1)} %iota_compare_fusion.9, bf16[2,192,1536]{2,0,1:T(2,128)(2,1)S(1)} %all-to-all-done), kind=kOutput, calls=%fused_computation.92 | convolution fusion | flops 1363673088 | bytes 2654218 | tf_op jit(solution)/shard_map/sij,skj->sik/dot_general | solution.py:64
  138.6 3.4 %convolution_add_fusion.4 = f32[2,192,1536]{2,1,0:T(8,128)S(1)} fusion(f32[2,192,192]{2,1,0:T(8,128)S(1)} %fusion.18, f32[2]{0:T(128)S(1)} %sqrt_add_fusion.1, bf16[1,1,2,192,1536]{4,3,2,1,0:T(8,128)(2,1)S(1)} %copy-done.1, bf16[2,192,1536]{2,0,1:T(2,128)(2,1)S(1)} %all-to-all-done, pred[2]{0:T(512)(128)(4,1)S(1)} %iota_compare_fusion.9), kind=kOutput, calls=%fused_computation.7 | convolution fusion | flops 1369571328 | bytes 5013514 | tf_op jit(solution)/shard_map/sij,sjk->sik/dot_general | solution.py:68
  144.9 2.6 %convolution_add_fusion.3 = f32[2,192,1536]{2,1,0:T(8,128)S(1)} fusion(f32[2,192,192]{2,1,0:T(8,128)S(1)} %fusion.17, f32[2,192,1536]{2,1,0:T(8,128)S(1)} %convolution_add_fusion.4), kind=kOutput, calls=%fused_computation.6 | convolution fusion | flops 1360134144 | bytes 5013504 | tf_op jit(solution)/shard_map/sij,sjk->sik/dot_general | solution.py:68
  150.3 2.4 convolution_add_fusion.2
  155.6 2.4 convolution_add_fusion.1
  157.9 2.7 %fusion.45 = f32[2,192,192]{2,1,0:T(8,128)S(1)} fusion(f32[2,192,1536]{2,1,0:T(8,128)S(1)} %convolution_add_fusion.1), kind=kOutput, calls=%fused_computation.97 | convolution fusion | flops 1358954496 | bytes 2654208 | tf_op jit(solution)/shard_map/sij,skj->sik/dot_general | solution.py:64
  165.8 10.3 %all-to-all-start.1 = ((bf16[2,192,1536]{2,0,1:T(2,128)(2,1)}), bf16[2,192,1536]{2,0,1:T(2,128)(2,1)S(1)}, u32[]{:S(2)}, u32[]{:S(2)}) async-start(bf16[2,192,1536]{2,0,1:T(2,128)(2,1)} %copy.36), calls=%async_computation.2 | async-start | bytes 2359296 | tf_op jit(solution)/shard_map/all_to_all | solution.py:148
  176.1 9.5 %pmax.7 = f32[1,4,64]{2,1,0:T(4,128)S(1)} all-reduce(f32[1,4,64]{2,1,0:T(4,128)S(1)} %copy-done.6), channel_id=1, replica_groups=mesh['dp'=4,'fsdp'=64] {'dp'}, use_global_device_ids=true, to_apply=%region_10.11 | all-reduce | flops 256 | bytes 2048 | tf_op jit(solution)/shard_map/pmax | solution.py:157
  185.7 18.5 %collective-permute-done = f32[4,16]{1,0:T(4,128)S(1)} collective-permute-done((f32[4,16]{1,0:T(4,128)S(1)}, f32[4,16]{1,0:T(4,128)S(1)}, u32[]{:S(2)}, u32[]{:S(2)}) %collective-permute-start) | collective-permute-done | bytes 288 | tf_op jit(solution)/shard_map/ppermute | solution.py:162
  204.3 6.9 %collective-permute-done.1 = f32[4,16]{1,0:T(4,128)S(1)} collective-permute-done((f32[4,16]{1,0:T(4,128)S(1)}, f32[4,16]{1,0:T(4,128)S(1)}, u32[]{:S(2)}, u32[]{:S(2)}) %collective-permute-start.1) | collective-permute-done | bytes 288 | tf_op jit(solution)/shard_map/ppermute | solution.py:162
  211.2 7.2 %collective-permute-done.2 = f32[4,16]{1,0:T(4,128)S(1)} collective-permute-done((f32[4,16]{1,0:T(4,128)S(1)}, f32[4,16]{1,0:T(4,128)S(1)}, u32[]{:S(2)}, u32[]{:S(2)}) %collective-permute-start.2) | collective-permute-done | bytes 288 | tf_op jit(solution)/shard_map/ppermute | solution.py:162
  218.4 4.8 %collective-permute-done.3 = f32[4,16]{1,0:T(4,128)S(1)} collective-permute-done((f32[4,16]{1,0:T(4,128)S(1)}, f32[4,16]{1,0:T(4,128)S(1)}, u32[]{:S(2)}, u32[]{:S(2)}) %collective-permute-start.3) | collective-permute-done | bytes 288 | tf_op jit(solution)/shard_map/ppermute | solution.py:162
  223.2 5.7 %collective-permute-done.4 = f32[4,16]{1,0:T(4,128)S(1)} collective-permute-done((f32[4,16]{1,0:T(4,128)S(1)}, f32[4,16]{1,0:T(4,128)S(1)}, u32[]{:S(2)}, u32[]{:S(2)}) %collective-permute-start.4) | collective-permute-done | bytes 288 | tf_op jit(solution)/shard_map/ppermute | solution.py:162
  228.9 5.1 %collective-permute-start.5 = (f32[4,16]{1,0:T(4,128)S(1)}, f32[4,16]{1,0:T(4,128)S(1)}, u32[]{:S(2)}, u32[]{:S(2)}) collective-permute-start(f32[4,16]{1,0:T(4,128)S(1)} %max.24), channel_id=1, source_target_pairs={{0,32},{1,33},{2,34},{3,35},{4,36},{5,37},{6,38},{7,39},{8,40},{9,... | collective-permute-start | bytes 776 | tf_op jit(solution)/shard_map/ppermute | solution.py:162
  234.0 2.5 collective-permute-done.5
  242.3 2.8 %fusion.4 = f32[4,16,3,1536]{3,2,1,0:T(4,128)S(1)} fusion(f32[4,16,3,1536]{3,1,2,0:T(8,128)} %param.13, bf16[4,16,3,1536]{3,2,1,0:T(4,128)(2,1)S(1)} %reshape_reshape.13, f32[4,16,3]{2,1,0:T(8,128)S(1)} %broadcast_select_fusion.1), kind=kLoop, calls=%fused_computation.19 | loop fusion | flops 1769472 | bytes 2949888 | tf_op jit(solution)/shard_map/mul | solution.py:88
  (107 shorter events, 55.8 us)
Async XLA Ops:
  7.2 1.2 copy-start
  7.2 31.1 %reduce-scatter.8.cloned.1.call-start = ((), (), s32[]{:S(2)}) async-start(), calls=%async_computation.7 | async-start | bytes 1310720
  9.0 2.9 %copy-start.4 = (s32[4,4,16,1]{2,3,1,0:T(1,128)S(1)}, s32[4,4,16,1]{2,3,1,0:T(1,128)}, u32[]{:S(2)}) copy-start(s32[4,4,16,1]{2,3,1,0:T(1,128)} %param.15) | copy-start | bytes 3076
  9.0 3.9 %copy-start.5 = (s32[4,4,16,1]{2,3,1,0:T(1,128)S(1)}, s32[4,4,16,1]{2,3,1,0:T(1,128)}, u32[]{:S(2)}) copy-start(s32[4,4,16,1]{2,3,1,0:T(1,128)} %param.16) | copy-start | bytes 3076
  10.6 67.4 %reduce-scatter.6.cloned.1.call-start = ((), (), s32[]{:S(2)}) async-start(), calls=%async_computation.6 | async-start | bytes 2949120 | tf_op jit(solution)/shard_map/reduce_scatter | solution.py:122
  39.5 30.4 %copy-start.3 = (bf16[1,1,2,256,512]{4,3,2,1,0:T(8,128)(2,1)S(1)}, bf16[1,1,2,256,512]{4,3,2,1,0:T(8,128)(2,1)}, u32[]{:S(2)}) copy-start(bf16[1,1,2,256,512]{4,3,2,1,0:T(8,128)(2,1)} %param.12) | copy-start | bytes 1572868
  41.5 28.4 %all-to-all-start.2 = ((bf16[2,256,512]{2,0,1:T(2,128)(2,1)}), bf16[2,256,512]{2,0,1:T(2,128)(2,1)S(1)}, u32[]{:S(2)}, u32[]{:S(2)}) async-start(bf16[2,256,512]{2,0,1:T(2,128)(2,1)} %copy.38), calls=%async_computation.3 | async-start | bytes 1048576 | tf_op jit(solution)/shard_map/all_to_all | solution.py:141
  85.1 40.5 %all-to-all-start = ((bf16[2,192,1536]{2,0,1:T(2,128)(2,1)}), bf16[2,192,1536]{2,0,1:T(2,128)(2,1)S(1)}, u32[]{:S(2)}, u32[]{:S(2)}) async-start(bf16[2,192,1536]{2,0,1:T(2,128)(2,1)} %copy.34), calls=%async_computation.1 | async-start | bytes 2359296 | tf_op jit(solution)/shard_map/all_to_all | solution.py:140
  125.6 40.2 %all-to-all-start.3 = ((bf16[2,256,512]{2,0,1:T(2,128)(2,1)}), bf16[2,256,512]{2,0,1:T(2,128)(2,1)S(1)}, u32[]{:S(2)}, u32[]{:S(2)}) async-start(bf16[2,256,512]{2,0,1:T(2,128)(2,1)} %copy.40), calls=%async_computation.4 | async-start | bytes 1048576 | tf_op jit(solution)/shard_map/all_to_all | solution.py:149
  131.3 3.2 %copy-start.1 = (bf16[1,1,2,192,1536]{4,3,2,1,0:T(8,128)(2,1)S(1)}, bf16[1,1,2,192,1536]{4,3,2,1,0:T(8,128)(2,1)}, u32[]{:S(2)}) copy-start(bf16[1,1,2,192,1536]{4,3,2,1,0:T(8,128)(2,1)} %param.11) | copy-start | bytes 3538948
  163.5 12.5 %copy-start.6 = (f32[1,4,64]{2,1,0:T(4,128)S(1)}, f32[1,4,64]{2,1,0:T(4,128)}, u32[]{:S(2)}) copy-start(f32[1,4,64]{2,1,0:T(4,128)} %param.17) | copy-start | bytes 3076
  165.8 74.0 %all-to-all-start.1 = ((bf16[2,192,1536]{2,0,1:T(2,128)(2,1)}), bf16[2,192,1536]{2,0,1:T(2,128)(2,1)S(1)}, u32[]{:S(2)}, u32[]{:S(2)}) async-start(bf16[2,192,1536]{2,0,1:T(2,128)(2,1)} %copy.36), calls=%async_computation.2 | async-start | bytes 2359296 | tf_op jit(solution)/shard_map/all_to_all | solution.py:148
  185.7 18.5 %collective-permute-start = (f32[4,16]{1,0:T(4,128)S(1)}, f32[4,16]{1,0:T(4,128)S(1)}, u32[]{:S(2)}, u32[]{:S(2)}) collective-permute-start(f32[4,16]{1,0:T(4,128)S(1)} %dynamic-slice_bitcast_fusion), channel_id=1, source_target_pairs={{0,1},{1,2},{2,3},{3,4},{4,5},{5,6},{6,7},{7,8},{8,9},{9,10},{10,1... | collective-permute-start | bytes 776 | tf_op jit(solution)/shard_map/ppermute | solution.py:162
  204.3 6.9 %collective-permute-start.1 = (f32[4,16]{1,0:T(4,128)S(1)}, f32[4,16]{1,0:T(4,128)S(1)}, u32[]{:S(2)}, u32[]{:S(2)}) collective-permute-start(f32[4,16]{1,0:T(4,128)S(1)} %fusion.108), channel_id=1, source_target_pairs={{0,2},{1,3},{2,4},{3,5},{4,6},{5,7},{6,8},{7,9},{8,10},{9,11},{10,... | collective-permute-start | bytes 776 | tf_op jit(solution)/shard_map/ppermute | solution.py:162
  211.2 7.2 %collective-permute-start.2 = (f32[4,16]{1,0:T(4,128)S(1)}, f32[4,16]{1,0:T(4,128)S(1)}, u32[]{:S(2)}, u32[]{:S(2)}) collective-permute-start(f32[4,16]{1,0:T(4,128)S(1)} %max.21), channel_id=1, source_target_pairs={{0,4},{1,5},{2,6},{3,7},{4,8},{5,9},{6,10},{7,11},{8,12},{9,13},{1... | collective-permute-start | bytes 776 | tf_op jit(solution)/shard_map/ppermute | solution.py:162
  218.4 4.8 %collective-permute-start.3 = (f32[4,16]{1,0:T(4,128)S(1)}, f32[4,16]{1,0:T(4,128)S(1)}, u32[]{:S(2)}, u32[]{:S(2)}) collective-permute-start(f32[4,16]{1,0:T(4,128)S(1)} %max.22), channel_id=1, source_target_pairs={{0,8},{1,9},{2,10},{3,11},{4,12},{5,13},{6,14},{7,15},{8,16},{9,17... | collective-permute-start | bytes 776 | tf_op jit(solution)/shard_map/ppermute | solution.py:162
  223.2 5.7 %collective-permute-start.4 = (f32[4,16]{1,0:T(4,128)S(1)}, f32[4,16]{1,0:T(4,128)S(1)}, u32[]{:S(2)}, u32[]{:S(2)}) collective-permute-start(f32[4,16]{1,0:T(4,128)S(1)} %max.23), channel_id=1, source_target_pairs={{0,16},{1,17},{2,18},{3,19},{4,20},{5,21},{6,22},{7,23},{8,24},{9,... | collective-permute-start | bytes 776 | tf_op jit(solution)/shard_map/ppermute | solution.py:162
  228.9 7.6 %collective-permute-start.5 = (f32[4,16]{1,0:T(4,128)S(1)}, f32[4,16]{1,0:T(4,128)S(1)}, u32[]{:S(2)}, u32[]{:S(2)}) collective-permute-start(f32[4,16]{1,0:T(4,128)S(1)} %max.24), channel_id=1, source_target_pairs={{0,32},{1,33},{2,34},{3,35},{4,36},{5,37},{6,38},{7,39},{8,40},{9,... | collective-permute-start | bytes 776 | tf_op jit(solution)/shard_map/ppermute | solution.py:162
  237.6 2.2 copy-start.2
Sparse Core Ops, SparseCore 0:
  11.1 27.1 reduce-scatter.7
  41.0 34.7 reduce-scatter.5

commit v2 on v0

v2 whole, which is shorter than its diff:
```python
import math

import jax
import jax.numpy as jnp
from jax import lax
from jax.experimental import pallas as pl
from jax.experimental.pallas import tpu as pltpu
from jax.sharding import PartitionSpec as P

QN = 128
KN = 128
STEPS = 5
LAYERS = 4
HEADS = 64
GROUPS = 4
PER_GROUP = 16
NODES = 64
BLOCKS = 64
Q_ROWS, Q_COLS = 192, 1536
KV_ROWS, KV_COLS = 256, 512
Q_OWN, KV_OWN = Q_ROWS // NODES, KV_ROWS // NODES
LANE = 128
Q_TILES, KV_TILES = Q_COLS // LANE, KV_COLS // LANE
SUB = 8
MSG_COLS = 7
MSG = MSG_COLS * LANE
ROWS = NODES * SUB
PEAK_TILE = Q_OWN * Q_TILES + KV_OWN * KV_TILES
SPLIT = Q_OWN * Q_TILES // SUB
SPLIT_SUB = Q_OWN * Q_TILES % SUB

MOMENTUM_RATE = 0.95
LEARN_RATE = 0.02
DECAY_RATE = 0.1
CLIP_LEVEL = 100.0
NEWTON_FIRST = 3.4445
NEWTON_SECOND = -4.775
NEWTON_THIRD = 2.0315
EPSILON = 1e-07
Q_SCALE = 0.2 * math.sqrt(max(Q_ROWS, Q_COLS))
KV_SCALE = 0.2 * math.sqrt(max(KV_ROWS, KV_COLS))

F32 = jnp.float32
BF16 = jnp.bfloat16
I32 = jnp.int32
PARAMS = pltpu.CompilerParams(vmem_limit_bytes=48 * 1024 * 1024)


def place(tile):
    col, sub = divmod(tile, SUB)
    return slice(sub * BLOCKS, (sub + 1) * BLOCKS), slice(col * LANE, (col + 1) * LANE)


def tiles_of(kind):
    if kind == "q":
        return [(r, ct, r * Q_TILES + ct) for r in range(Q_OWN) for ct in range(Q_TILES)]
    base = Q_OWN * Q_TILES
    return [(r, ct, base + r * KV_TILES + ct) for r in range(KV_OWN) for ct in range(KV_TILES)]


def iota(shape, dim):
    return lax.broadcasted_iota(I32, shape, dim)


def dot(a, b):
    return jnp.dot(a, b, preferred_element_type=F32)


def dot_nt(a, b):
    return lax.dot_general(a, b, (((1,), (1,)), ((), ())), preferred_element_type=F32)


def one(cond):
    return jnp.where(cond, 1.0, 0.0).astype(BF16)


def pack_matrix():
    row, col = iota((ROWS, ROWS), 0), iota((ROWS, ROWS), 1)
    return one(((row >> 3) == (col & 63)) & ((row & 7) == (col >> 6)))


def unpack_matrix():
    row, col = iota((ROWS, ROWS), 0), iota((ROWS, ROWS), 1)
    return one(((row & 63) == (col >> 3)) & ((row >> 6) == (col & 7)))


def natural_matrix(own):
    size = own * NODES
    row, col = iota((size, size), 0), iota((size, size), 1)
    return one(row == (col & 63) * own + (col >> 6))


def split_matrix(own):
    size = own * NODES
    row, col = iota((size, size), 0), iota((size, size), 1)
    return one(col == (row & 63) * own + (row >> 6))


def to_message(q_natural, kv_natural, tiles_ref):
    q_split = dot(split_matrix(Q_OWN), q_natural).astype(BF16)
    kv_split = dot(split_matrix(KV_OWN), kv_natural).astype(BF16)
    tiles_ref[:, SPLIT * LANE :] = jnp.zeros((ROWS, MSG - SPLIT * LANE), BF16)
    for r, ct, tile in tiles_of("q"):
        rows, cols = place(tile)
        tiles_ref[rows, cols] = q_split[r * NODES : (r + 1) * NODES, ct * LANE : (ct + 1) * LANE]
    for r, ct, tile in tiles_of("kv"):
        rows, cols = place(tile)
        tiles_ref[rows, cols] = kv_split[r * NODES : (r + 1) * NODES, ct * LANE : (ct + 1) * LANE]
    return dot(pack_matrix(), tiles_ref[...])


def from_tiles(tiles, q_ref, kv_ref):
    for r, ct, tile in tiles_of("q"):
        rows, cols = place(tile)
        q_ref[r * NODES : (r + 1) * NODES, ct * LANE : (ct + 1) * LANE] = tiles[rows, cols]
    for r, ct, tile in tiles_of("kv"):
        rows, cols = place(tile)
        kv_ref[r * NODES : (r + 1) * NODES, ct * LANE : (ct + 1) * LANE] = tiles[rows, cols]
    return dot(natural_matrix(Q_OWN), q_ref[...]), dot(natural_matrix(KV_OWN), kv_ref[...])


def by_kind(q_matrix, kv_matrix, source, q_rows):
    edge = SPLIT * LANE
    q_part = dot(q_matrix, source[:, : edge + LANE])
    kv_part = dot(kv_matrix, source[:, edge:])
    mixed = jnp.where(q_rows, q_part[:, edge:], kv_part[:, :LANE])
    return jnp.concatenate([q_part[:, :edge], mixed, kv_part[:, LANE:]], axis=1)


def call(kernel, out_shape, *operands, **options):
    return pl.pallas_call(kernel, out_shape=out_shape, compiler_params=PARAMS, **options)(*operands)


def shape(dims, dtype):
    return jax.ShapeDtypeStruct(dims, dtype)


def arrange_kernel(q_ref, kv_ref, out_ref):
    out_ref[:, SPLIT * LANE :] = jnp.zeros((ROWS, MSG - SPLIT * LANE), BF16)
    for kind, ref in (("q", q_ref), ("kv", kv_ref)):
        for r, ct, tile in tiles_of(kind):
            rows, cols = place(tile)
            for layer in range(LAYERS):
                start = rows.start + layer * PER_GROUP
                out_ref[start : start + PER_GROUP, cols] = ref[layer, r, :, ct * LANE : (ct + 1) * LANE]


def arrange(grad_query, grad_kv):
    return call(
        arrange_kernel,
        shape((GROUPS * ROWS, MSG), BF16),
        grad_query,
        grad_kv,
        grid=(GROUPS,),
        in_specs=[
            pl.BlockSpec((LAYERS, Q_OWN, PER_GROUP, Q_COLS), lambda g: (0, 0, g, 0)),
            pl.BlockSpec((LAYERS, KV_OWN, PER_GROUP, KV_COLS), lambda g: (0, 0, g, 0)),
        ],
        out_specs=pl.BlockSpec((ROWS, MSG), lambda g: (g, 0)),
    )


def table_kernel(row_ref, col_ref, send_ref, late_ref, late_back_ref, back_ref, over_ref):
    owner_row = row_ref[...]
    owner_col = col_ref[...]
    down, across = iota((NODES, BLOCKS), 0), iota((NODES, BLOCKS), 1)

    def count(cond, axis):
        return jnp.sum(jnp.where(cond, 1.0, 0.0), axis=axis, keepdims=True)

    same = owner_col == owner_row
    slot_col = count(same & (across < down), 1)
    slot_row = count(same & (down < across), 0)
    hits = down == owner_row
    hits_back = owner_col == across
    fill_col, fill_row = count(hits, 1), count(hits_back, 0)
    over_col, over_row = slot_col > 0.5, slot_row > 0.5
    free_col, free_row = fill_col < 0.5, fill_row < 0.5
    over_rank_col, over_rank_row = count(over_row & (across < down), 1), count(over_col & (down < across), 0)
    free_rank_col, free_rank_row = count(free_row & (across < down), 1), count(free_col & (down < across), 0)

    late = hits & over_row
    send = (hits & ~over_row) | (free_col & over_row & (free_rank_col == over_rank_row))
    late_back = hits_back & over_col
    send_back = (hits_back & ~over_col) | (free_row & over_col & (free_rank_row == over_rank_col))

    def spread_rows(count_rows, per):
        return one((iota((count_rows, NODES), 0) >> per) == iota((count_rows, NODES), 1))

    def spread_cols(count_cols):
        return one(iota((BLOCKS, count_cols), 0) == (iota((BLOCKS, count_cols), 1) & 63))

    def to_peers(table):
        wide = dot(dot(spread_rows(ROWS, 3), one(table)).astype(BF16), spread_cols(ROWS))
        row, col = iota((ROWS, ROWS), 0), iota((ROWS, ROWS), 1)
        return jnp.where((row & 7) == (col >> 6), wide, 0.0).astype(BF16)

    def to_tiles(table, per):
        width = NODES << per
        mine = one((iota((ROWS, BLOCKS), 0) & 63) == iota((ROWS, BLOCKS), 1))
        peers = one(iota((NODES, width), 0) == (iota((NODES, width), 1) >> per))
        wide = dot(dot(mine, one(table)).astype(BF16), peers)
        row, col = iota((ROWS, width), 0), iota((ROWS, width), 1)
        return jnp.where((row >> 6) == (col & ((1 << per) - 1)), wide, 0.0).astype(BF16)

    send_ref[...] = to_peers(send)
    late_ref[...] = to_peers(late)
    late_back_ref[...] = to_tiles(late_back, 3)
    back_ref[...] = to_tiles(send_back, 4)
    over = jnp.where(over_col, 1.0, 0.0)
    for sub in range(SUB):
        over_ref[sub * BLOCKS : (sub + 1) * BLOCKS, :] = jnp.broadcast_to(over, (BLOCKS, LANE))


def tables(owners):
    return call(
        table_kernel,
        (
            shape((ROWS, ROWS), BF16),
            shape((ROWS, ROWS), BF16),
            shape((ROWS, ROWS), BF16),
            shape((ROWS, 2 * ROWS), BF16),
            shape((ROWS, LANE), F32),
        ),
        owners.reshape(1, BLOCKS),
        owners.reshape(BLOCKS, 1),
    )


def late_kernel(q_ref, kv_ref, out_ref, tiles_ref):
    out_ref[...] = to_message(q_ref[0, 0, 0], kv_ref[0, 0, 0], tiles_ref).astype(BF16)


def late_message(momentum_query, momentum_kv):
    return call(
        late_kernel,
        shape((ROWS, MSG), BF16),
        momentum_query,
        momentum_kv,
        grid=(1,),
        in_specs=[
            pl.BlockSpec((1, 1, 1, Q_ROWS, Q_COLS), lambda i: (0, 0, 1, 0, 0)),
            pl.BlockSpec((1, 1, 1, KV_ROWS, KV_COLS), lambda i: (0, 0, 1, 0, 0)),
        ],
        out_specs=pl.BlockSpec((ROWS, MSG), lambda i: (0, 0)),
        scratch_shapes=[pltpu.VMEM((ROWS, MSG), BF16)],
    )


def send_kernel(
    sum_ref, late_in_ref, q_send, q_late, q_late_back, q_over, kv_send, kv_late, kv_late_back, kv_over, peak_ref,
    out_ref, late_out_ref,
):
    row = iota((ROWS, LANE), 0)
    tile_rows = row < SPLIT_SUB * BLOCKS
    peer_rows = (row & 7) < SPLIT_SUB
    reduced = sum_ref[...].astype(F32)
    earlier = by_kind(q_late_back[...], kv_late_back[...], late_in_ref[...], tile_rows)
    carried = MOMENTUM_RATE * earlier + reduced
    direction = reduced + MOMENTUM_RATE * carried
    q_over_mask, kv_over_mask = q_over[...] > 0.5, kv_over[...] > 0.5
    columns = []
    for col in range(MSG_COLS):
        if col < SPLIT:
            mask = q_over_mask
        elif col == SPLIT:
            mask = jnp.where(tile_rows, q_over[...], kv_over[...]) > 0.5
        else:
            mask = kv_over_mask
        lanes = slice(col * LANE, (col + 1) * LANE)
        columns.append(jnp.where(mask, direction[:, lanes], reduced[:, lanes]))
    chosen = jnp.concatenate(columns, axis=1).astype(BF16)
    message = by_kind(q_send[...], kv_send[...], chosen, peer_rows)
    peak = peak_ref[...]
    high = peak.astype(BF16).astype(F32)
    middle = (peak - high).astype(BF16).astype(F32)
    low = (peak - high) - middle
    col, sub = divmod(PEAK_TILE, SUB)
    lane = iota((ROWS, LANE), 1)
    last = message[:, col * LANE :]
    first_half = lane < LANE // 2
    last = jnp.where((row & 7) == sub, jnp.where(first_half, high, middle), last)
    last = jnp.where((row & 7) == sub + 1, jnp.where(first_half, low, 0.0), last)
    out_ref[:, : col * LANE] = message[:, : col * LANE].astype(BF16)
    out_ref[:, col * LANE :] = last.astype(BF16)
    late_out_ref[...] = by_kind(q_late[...], kv_late[...], carried.astype(BF16), peer_rows).astype(BF16)


def halves(x):
    high = x.astype(BF16)
    return high, (x - high.astype(F32)).astype(BF16)


def product(a, b, op):
    return op(a[0], b[0]) + (op(a[0], b[1]) + op(a[1], b[0]))


def newton_step(x_ref):
    x = x_ref[...]
    parts = halves(x)
    square = product(parts, parts, dot_nt)
    square_parts = halves(square)
    polynomial = NEWTON_SECOND * square + NEWTON_THIRD * product(square_parts, square_parts, dot)
    x_ref[...] = NEWTON_FIRST * x + product(halves(polynomial), parts, dot)


def owner_kernel(
    used_ref, in_ref, q_mom, kv_mom, late_ref, out_ref, q_new, kv_new, factor_ref, q_x, kv_x, q_half, kv_half, tiles_ref,
    joined,
):
    received = dot(unpack_matrix(), in_ref[...])
    rows, cols = place(PEAK_TILE)
    top = received[rows, cols]
    rows, cols = place(PEAK_TILE + 1)
    bottom = received[rows, cols]
    peaks = jnp.max((top[:, :BLOCKS] + top[:, BLOCKS:]) + bottom[:, :BLOCKS], axis=0, keepdims=True)
    diagonal = iota((BLOCKS, BLOCKS), 0) == iota((BLOCKS, BLOCKS), 1)
    peak_col = jnp.sum(jnp.where(diagonal, jnp.broadcast_to(peaks, (BLOCKS, BLOCKS)), 0.0), axis=1, keepdims=True)
    shrink = jnp.minimum(1.0, CLIP_LEVEL / peak_col)
    factor_ref[0] = jnp.broadcast_to(jnp.sqrt(shrink), (BLOCKS, LANE))
    factor_ref[1] = jnp.broadcast_to(shrink, (BLOCKS, LANE))

    arrived = from_tiles(received.astype(BF16), q_half, kv_half)
    for kind, gradient, mom, new, x_ref in (
        (0, arrived[0], q_mom, q_new, q_x),
        (1, arrived[1], kv_mom, kv_new, kv_x),
    ):
        used = used_ref[kind] > 0
        carried = MOMENTUM_RATE * mom[0, 0, 0].astype(F32) + gradient
        new[0, 0, 0] = jnp.where(used, carried, 0.0).astype(BF16)
        direction = jnp.where(used, gradient + MOMENTUM_RATE * carried, gradient)
        norm = jnp.sqrt(jnp.sum(direction * direction)) + EPSILON
        x_ref[...] = direction / norm

    def body(_, carry):
        newton_step(q_x)
        newton_step(kv_x)
        return carry

    lax.fori_loop(0, STEPS, body, 0)
    outgoing = to_message((q_x[...] * Q_SCALE).astype(BF16), (kv_x[...] * KV_SCALE).astype(BF16), tiles_ref)
    joined[:, :SUB, :] = outgoing.reshape(NODES, SUB, MSG)
    joined[:, SUB:, :] = late_ref[...].astype(F32).reshape(NODES, SUB, MSG)
    out_ref[...] = joined[...].reshape(2 * ROWS, MSG).astype(BF16)


def owner_step(used, arrived, momentum_query, momentum_kv, late):
    whole = pl.BlockSpec((ROWS, MSG), lambda i: (0, 0))
    q_slot = pl.BlockSpec((1, 1, 1, Q_ROWS, Q_COLS), lambda i: (0, 0, 0, 0, 0))
    kv_slot = pl.BlockSpec((1, 1, 1, KV_ROWS, KV_COLS), lambda i: (0, 0, 0, 0, 0))
    return call(
        owner_kernel,
        (
            shape((2 * ROWS, MSG), BF16),
            shape((1, 1, 2, Q_ROWS, Q_COLS), BF16),
            shape((1, 1, 2, KV_ROWS, KV_COLS), BF16),
            shape((2, BLOCKS, LANE), F32),
        ),
        used,
        arrived,
        momentum_query,
        momentum_kv,
        late,
        grid=(1,),
        in_specs=[pl.BlockSpec(memory_space=pltpu.SMEM), whole, q_slot, kv_slot, whole],
        out_specs=[
            pl.BlockSpec((2 * ROWS, MSG), lambda i: (0, 0)),
            q_slot,
            kv_slot,
            pl.BlockSpec((2, BLOCKS, LANE), lambda i: (0, 0, 0)),
        ],
        scratch_shapes=[
            pltpu.VMEM((Q_ROWS, Q_COLS), F32),
            pltpu.VMEM((KV_ROWS, KV_COLS), F32),
            pltpu.VMEM((Q_ROWS, Q_COLS), BF16),
            pltpu.VMEM((KV_ROWS, KV_COLS), BF16),
            pltpu.VMEM((ROWS, MSG), BF16),
            pltpu.VMEM((NODES, 2 * SUB, MSG), F32),
        ],
    )


def finish_kernel(
    node_ref, in_ref, q_back, kv_back, factor_ref, weight_ref, q_old, kv_old,
    update_ref, weight_new, kv_update_ref, q_new, kv_new, q_half, kv_half,
):
    back = in_ref[...]
    row = iota((ROWS, LANE), 0)
    updates = by_kind(q_back[...], kv_back[...], back, row < SPLIT_SUB * BLOCKS)
    node = node_ref[0]
    for r in range(Q_OWN):
        factor = jnp.where(node * Q_OWN + r < QN, factor_ref[0], factor_ref[1]).reshape(LAYERS, PER_GROUP, LANE)
        for ct in range(Q_TILES):
            rows, cols = place(r * Q_TILES + ct)
            lanes = slice(ct * LANE, (ct + 1) * LANE)
            update = updates[rows, cols].reshape(LAYERS, PER_GROUP, LANE)
            update_ref[:, r, :, lanes] = update.astype(BF16)
            weight = weight_ref[:, r, :, lanes]
            weight_new[:, r, :, lanes] = (weight - LEARN_RATE * (update + DECAY_RATE * weight)) * factor
    for r, ct, tile in tiles_of("kv"):
        rows, cols = place(tile)
        kv_update_ref[r, :, ct * LANE : (ct + 1) * LANE] = updates[rows, cols].astype(BF16)
    wide_row, wide_col = iota((ROWS, 2 * ROWS), 0), iota((ROWS, 2 * ROWS), 1)
    late_matrix = one(((wide_row & 63) == (wide_col >> 4)) & ((wide_row >> 6) + SUB == (wide_col & 15)))
    late = dot(late_matrix, back).astype(BF16)
    q_late, kv_late = from_tiles(late, q_half, kv_half)
    q_new[0, 0, 0] = q_late.astype(BF16)
    kv_new[0, 0, 0] = kv_late.astype(BF16)


def finish(node, returned, q_back, kv_back, factors, weight_query, q_momentum, kv_momentum):
    def whole(*dims):
        return pl.BlockSpec(dims, lambda i: (0,) * len(dims))

    anywhere = pl.BlockSpec(memory_space=pl.ANY)
    q_dims = (LAYERS, Q_OWN, PER_GROUP, Q_COLS)
    kv_dims = (KV_OWN, BLOCKS, KV_COLS)
    return call(
        finish_kernel,
        (
            shape(q_dims, BF16),
            shape(q_dims, F32),
            shape(kv_dims, BF16),
            shape((1, 1, 2, Q_ROWS, Q_COLS), BF16),
            shape((1, 1, 2, KV_ROWS, KV_COLS), BF16),
        ),
        node,
        returned,
        q_back,
        kv_back,
        factors,
        weight_query,
        q_momentum,
        kv_momentum,
        grid=(1,),
        in_specs=[
            pl.BlockSpec(memory_space=pltpu.SMEM),
            whole(2 * ROWS, MSG),
            whole(ROWS, 2 * ROWS),
            whole(ROWS, 2 * ROWS),
            whole(2, BLOCKS, LANE),
            whole(*q_dims),
            anywhere,
            anywhere,
        ],
        out_specs=[
            whole(*q_dims),
            whole(*q_dims),
            whole(*kv_dims),
            pl.BlockSpec((1, 1, 1, Q_ROWS, Q_COLS), lambda i: (0, 0, 1, 0, 0)),
            pl.BlockSpec((1, 1, 1, KV_ROWS, KV_COLS), lambda i: (0, 0, 1, 0, 0)),
        ],
        scratch_shapes=[pltpu.VMEM((Q_ROWS, Q_COLS), BF16), pltpu.VMEM((KV_ROWS, KV_COLS), BF16)],
        input_output_aliases={6: 3, 7: 4},
    )


def exchange(message):
    return lax.all_to_all(message, "fsdp", split_axis=0, concat_axis=0, tiled=True)


def on_device(
    grad_query, grad_kv, momentum_query, momentum_kv, weight_query, weight_kv, owner_query, owner_kv, max_logits
):
    my_group = lax.axis_index("dp")
    my_node = lax.axis_index("fsdp")

    terms = arrange(jnp.transpose(grad_query[0], (0, 2, 1, 3)), jnp.transpose(grad_kv[0], (0, 2, 1, 3)))
    reduced = lax.psum_scatter(terms, "dp", scatter_dimension=0, tiled=True)

    peaks = lax.pmax(max_logits, "dp")[0]
    peaks = lax.dynamic_slice_in_dim(peaks, my_group * PER_GROUP, PER_GROUP, 1).reshape(1, BLOCKS)
    peaks = jnp.concatenate([peaks, peaks], axis=1)
    q_owners = lax.dynamic_index_in_dim(owner_query.reshape(GROUPS, BLOCKS), my_group, 0, keepdims=False)
    kv_owners = lax.dynamic_index_in_dim(owner_kv.reshape(GROUPS, BLOCKS), my_group, 0, keepdims=False)
    used = jnp.stack([jnp.any(q_owners == my_node), jnp.any(kv_owners == my_node)]).astype(I32)
    q_send, q_late, q_late_back, q_back, q_over = tables(q_owners)
    kv_send, kv_late, kv_late_back, kv_back, kv_over = tables(kv_owners)

    late_in = exchange(late_message(momentum_query, momentum_kv))
    message, late_out = call(
        send_kernel,
        (shape((ROWS, MSG), BF16), shape((ROWS, MSG), BF16)),
        reduced, late_in, q_send, q_late, q_late_back, q_over, kv_send, kv_late, kv_late_back, kv_over, peaks,
    )
    arrived = exchange(message)
    outgoing, q_momentum, kv_momentum, factors = owner_step(used, arrived, momentum_query, momentum_kv, late_out)
    returned = exchange(outgoing)
    q_update, q_weight, kv_update, q_momentum, kv_momentum = finish(
        my_node.astype(I32).reshape(1),
        returned,
        q_back,
        kv_back,
        factors,
        jnp.transpose(weight_query, (0, 2, 1, 3)),
        q_momentum,
        kv_momentum,
    )
    kv_update = jnp.transpose(kv_update.reshape(KV_OWN, LAYERS, PER_GROUP, KV_COLS), (1, 2, 0, 3))
    kv_index = my_node * KV_OWN + jnp.arange(KV_OWN, dtype=I32)
    root_shrink = factors[0, :, 0].reshape(LAYERS, PER_GROUP)
    kv_factor = jnp.where(kv_index[None, None, :, None] < KN, root_shrink[:, :, None, None], 1.0)
    kv_weight = (weight_kv - LEARN_RATE * (kv_update.astype(F32) + DECAY_RATE * weight_kv)) * kv_factor
    return (
        jnp.transpose(q_update, (0, 2, 1, 3)),
        kv_update,
        jnp.transpose(q_weight, (0, 2, 1, 3)),
        kv_weight,
        q_momentum,
        kv_momentum,
    )


def solution(mesh):
    return jax.shard_map(
        on_device,
        mesh=mesh,
        in_specs=(
            P("dp", None, None, "fsdp", None),
            P("dp", None, None, "fsdp", None),
            P("dp", "fsdp", None, None, None),
            P("dp", "fsdp", None, None, None),
            P(None, "dp", "fsdp", None),
            P(None, "dp", "fsdp", None),
            P(),
            P(),
            P(("dp", "fsdp"), None, None),
        ),
        out_specs=(
            P(None, "dp", "fsdp", None),
            P(None, "dp", "fsdp", None),
            P(None, "dp", "fsdp", None),
            P(None, "dp", "fsdp", None),
            P("dp", "fsdp", None, None, None),
            P("dp", "fsdp", None, None, None),
        ),
        check_vma=False,
    )
```

time: 277 us -> 194 us (0.70); the launches traced: 272 us -> 192 us
  blocking collectives: 78.9 us -> 9.11 us
  matrix products: 45.7 us -> 0 us
  Pallas kernels: 0 us -> 33.2 us
  waiting for transfers between devices: 61.5 us -> 79.5 us
  other arithmetic: 13.1 us -> 4.73 us
  starting transfers between devices: 35.5 us -> 28.7 us
    pmax x1, blocking collectives: 78.9 us -> 9.11 us  [on_device(): peaks = lax.pmax(max_logits, 'dp')[0]]
    dot_general x34 -> x0, matrix products: 45.7 us -> none  [the longest x10 19.2 us: batched_newton(): jnp.einsum('sij,skj->sik', scaled, scaled, precision=lax.Precision.HIGHEST)]
    all_to_all x4 -> x3, waiting for transfers between devices: 36.7 us -> 74.1 us  [exchange(): lax.all_to_all(message, 'fsdp', split_axis=0, concat_axis=0, tiled=True)]
    pallas_call x0 -> x7, Pallas kernels: none -> 33.2 us  [call(): pl.pallas_call(kernel, out_shape=out_shape, compiler_params=PARAMS, **opt...]
    unnamed x3 -> x1, waiting for transfers between devices: 24.8 us -> 0.02 us
    unnamed x23 -> x58, local copies, waits for them, and re-layouts: 7.63 us -> 22.1 us
    reshape x8 -> x5, local copies, waits for them, and re-layouts: 7.61 us -> 0.45 us  [the longest x2 0.19 us: tables(): owners.reshape(BLOCKS, 1)]
    all_to_all x4 -> x3, starting transfers between devices: 35.4 us -> 28.7 us  [exchange(): lax.all_to_all(message, 'fsdp', split_axis=0, concat_axis=0, tiled=True)]
  transfers between devices with their start and end apart: 6 -> 4, of which waited for: 3 -> 4; matrix products, arithmetic and copies ran while one was open for 24% -> 2% of each run, Pallas kernels for 0% -> 3%
where the time goes in v2:
time: 194 us; the launch traced here: 192 us
  waiting for transfers between devices  79.5 us (41%)
  Pallas kernels  33.2 us (17%)
  starting transfers between devices  28.7 us (15%)
  local copies, waits for them, and re-layouts  22.8 us (12%)
  between operations  14.2 us (7%)
  blocking collectives  9.11 us (5%)
  other arithmetic  4.73 us (2%)
    all_to_all x3, waiting for transfers between devices, exchange(): lax.all_to_all(message, 'fsdp', split_axis=0, concat_axis=0, tiled=True)  74.1 us
    pallas_call x7, Pallas kernels, call(): pl.pallas_call(kernel, out_shape=out_shape, compiler_params=PARAMS, **opt...  33.2 us
    all_to_all x3, starting transfers between devices, exchange(): lax.all_to_all(message, 'fsdp', split_axis=0, concat_axis=0, tiled=True)  28.7 us
    unnamed x58, local copies, waits for them, and re-layouts  22.1 us
    pmax x1, blocking collectives, on_device(): peaks = lax.pmax(max_logits, 'dp')[0]  9.11 us
    reduce_scatter x1, waiting for transfers between devices, on_device(): reduced = lax.psum_scatter(terms, 'dp', scatter_dimension=0, tiled=True)  5.37 us
  transfers between devices with their start and end apart: 4, of which 4 were waited for; matrix products, arithmetic and copies ran while one was open for 2% of the time, Pallas kernels for 3%

profile of v2, /device:TPU:2, one launch (start us, length us, event | category | flops | bytes accessed | tf_op | source)
XLA Modules:
  0.0 192.3 jit_solution(12798744372946624353)
XLA Ops:
  7.2 1.4 copy.28
  8.7 1.7 copy-done.1
  10.3 2.7 %shard_map.136 = bf16[2048,896]{1,0:T(8,128)(2,1)} custom-call(bf16[4,3,64,1536]{3,2,1,0:T(8,128)(2,1)S(1)} %bitcast.31, bf16[4,4,64,512]{3,2,1,0:T(8,128)(2,1)S(1)} %bitcast.29), custom_call_target="tpu_custom_call" | custom-call | tf_op jit(solution)/shard_map/pallas_call | solution.py:131
  13.0 1.2 copy-done
  14.4 2.0 %shard_map.137 = bf16[512,896]{1,0:T(8,128)(2,1)} custom-call(bf16[1,1,2,192,1536]{4,3,2,1,0:T(8,128)(2,1)S(1)} %copy-done, bf16[1,1,2,256,512]{4,3,2,1,0:T(8,128)(2,1)S(1)} %copy-done.2), custom_call_target="tpu_custom_call" | custom-call | tf_op jit(solution)/shard_map/pallas_call | solution.py:131
  16.4 12.2 %all-to-all-start = ((bf16[64,8,896]{2,1,0:T(8,128)(2,1)}), bf16[64,8,896]{2,1,0:T(8,128)(2,1)S(1)}, u32[]{:S(2)}, u32[]{:S(2)}) async-start(bf16[64,8,896]{2,1,0:T(8,128)(2,1)} %bitcast.7), calls=%async_computation.1 | async-start | bytes 1835008 | tf_op jit(solution)/shard_map/all_to_all | solution.py:459
  31.4 1.5 shard_map.138
  35.7 1.5 shard_map.139
  41.3 9.1 %pmax.7 = f32[1,4,64]{2,1,0:T(4,128)S(1)} all-reduce(f32[1,4,64]{2,1,0:T(4,128)S(1)} %copy-done.27), channel_id=1, replica_groups=mesh['dp'=4,'fsdp'=64] {'dp'}, use_global_device_ids=true, to_apply=%region_3.4 | all-reduce | flops 256 | bytes 2048 | tf_op jit(solution)/shard_map/pmax | solution.py:471
  50.6 4.0 %all-to-all-done = bf16[64,8,896]{2,1,0:T(8,128)(2,1)S(1)} async-done(((bf16[64,8,896]{2,1,0:T(8,128)(2,1)}), bf16[64,8,896]{2,1,0:T(8,128)(2,1)S(1)}, u32[]{:S(2)}, u32[]{:S(2)}) %all-to-all-start) | async-done | bytes 917536 | tf_op jit(solution)/shard_map/all_to_all | solution.py:459
  54.7 5.4 %reduce-scatter.2.cloned.1.call-done.sum_ref = bf16[512,896]{1,0:T(8,128)(2,1)} async-done(((bf16[2048,896]{1,0:T(8,128)(2,1)}), bf16[512,896]{1,0:T(8,128)(2,1)}) %reduce-scatter.2.cloned.1.call-update) | async-done | bytes 917520 | tf_op jit(solution)/shard_map/reduce_scatter | solution.py:469
  60.1 1.0 copy-done.10
  66.2 4.1 %shard_map.140 = (bf16[512,896]{1,0:T(8,128)(2,1)}, bf16[512,896]{1,0:T(8,128)(2,1)S(1)}) custom-call(bf16[512,896]{1,0:T(8,128)(2,1)} %reduce-scatter.2.cloned.1.call-done.sum_ref, bf16[512,896]{1,0:T(8,128)(2,1)} %bitcast.37, bf16[512,512]{1,0:T(8,128)(2,1)S(1)} %get-tuple-element.27.q_send, bf16[512,512]{1,0:T(8,128)(2,1)S(1)} %copy-done.10, ...), custom_call_target="tpu_custom_call" | custom-call | tf_op jit(solution)/shard_map/pallas_call | solution.py:131
  70.3 10.7 %all-to-all-start.1 = ((bf16[64,8,896]{2,1,0:T(8,128)(2,1)}), bf16[64,8,896]{2,1,0:T(8,128)(2,1)S(1)}, u32[]{:S(2)}, u32[]{:S(2)}) async-start(bf16[64,8,896]{2,1,0:T(8,128)(2,1)} %bitcast.11), calls=%async_computation.2 | async-start | bytes 1835008 | tf_op jit(solution)/shard_map/all_to_all | solution.py:459
  81.0 1.3 add_convert_fusion.used_ref
  82.3 24.6 %all-to-all-done.1 = bf16[64,8,896]{2,1,0:T(8,128)(2,1)S(1)} async-done(((bf16[64,8,896]{2,1,0:T(8,128)(2,1)}), bf16[64,8,896]{2,1,0:T(8,128)(2,1)S(1)}, u32[]{:S(2)}, u32[]{:S(2)}) %all-to-all-start.1) | async-done | bytes 917536 | tf_op jit(solution)/shard_map/all_to_all | solution.py:459
  106.9 17.5 %shard_map.141 = (bf16[1024,896]{1,0:T(8,128)(2,1)S(1)}, bf16[1,1,2,192,1536]{4,3,2,1,0:T(8,128)(2,1)}, bf16[1,1,2,256,512]{4,3,2,1,0:T(8,128)(2,1)}, f32[2,64,128]{2,1,0:T(8,128)S(1)}) custom-call(s32[2]{0:T(128)S(1)} %add_convert_fusion.used_ref, bf16[512,896]{1,0:T(8,128)(2,1)S(1)} %bitcast.30, bf16[1,1,2,192,1536]{4,3,2,1,0:T(8,128)(2,1)S(1)} %copy-done, ...), custom_call_target="tpu_custom_call" | custom-call | tf_op jit(solution)/shard_map/pallas_call | solution.py:131
  124.4 1.3 copy-done.3
  126.3 5.8 %all-to-all-start.2 = ((bf16[64,16,896]{2,1,0:T(8,128)(2,1)}), bf16[64,16,896]{2,1,0:T(8,128)(2,1)S(1)}, u32[]{:S(2)}, u32[]{:S(2)}) async-start(bf16[64,16,896]{2,1,0:T(8,128)(2,1)} %bitcast.32), calls=%async_computation.3 | async-start | bytes 3670016 | tf_op jit(solution)/shard_map/all_to_all | solution.py:459
  132.4 45.4 %all-to-all-done.2 = bf16[64,16,896]{2,1,0:T(8,128)(2,1)S(1)} async-done(((bf16[64,16,896]{2,1,0:T(8,128)(2,1)}), bf16[64,16,896]{2,1,0:T(8,128)(2,1)S(1)}, u32[]{:S(2)}, u32[]{:S(2)}) %all-to-all-start.2) | async-done | bytes 1835040 | tf_op jit(solution)/shard_map/all_to_all | solution.py:459
  177.9 1.2 copy-done.6
  179.1 1.2 copy-done.8
  180.3 3.8 %shard_map.142 = (bf16[4,3,16,1536]{3,2,1,0:T(8,128)(2,1)}, f32[4,3,16,1536]{3,2,1,0:T(8,128)}, bf16[4,64,512]{2,1,0:T(8,128)(2,1)S(1)}, bf16[1,1,2,192,1536]{4,...) custom-call(s32[1]{0:T(128)} %bitcast.node_ref, ...), custom_call_target="tpu_custom_call", output_to_operand_aliasing={{3}: (6, {}), {4}: (7, {})} | custom-call | tf_op jit(solution)/shard_map/pallas_call | solution.py:131
  184.2 1.3 subtract_multiply_fusion
  (67 shorter events, 16.0 us)
Async XLA Ops:
  7.2 52.9 %reduce-scatter.2.cloned.1.call-start = ((), (), s32[]{:S(2)}) async-start(), calls=%async_computation.4 | async-start | bytes 4587520 | tf_op jit(solution)/shard_map/reduce_scatter | solution.py:469
  8.7 1.7 copy-start.1
  13.0 1.3 copy-start
  13.0 1.4 copy-start.2
  16.4 12.8 %copy-start.25 = (s32[4,4,16,1]{2,3,1,0:T(1,128)S(1)}, s32[4,4,16,1]{2,3,1,0:T(1,128)}, u32[]{:S(2)}) copy-start(s32[4,4,16,1]{2,3,1,0:T(1,128)} %param.16) | copy-start | bytes 3076
  16.4 13.5 %copy-start.26 = (s32[4,4,16,1]{2,3,1,0:T(1,128)S(1)}, s32[4,4,16,1]{2,3,1,0:T(1,128)}, u32[]{:S(2)}) copy-start(s32[4,4,16,1]{2,3,1,0:T(1,128)} %param.15) | copy-start | bytes 3076
  16.4 24.9 %copy-start.27 = (f32[1,4,64]{2,1,0:T(4,128)S(1)}, f32[1,4,64]{2,1,0:T(4,128)}, u32[]{:S(2)}) copy-start(f32[1,4,64]{2,1,0:T(4,128)} %param.17) | copy-start | bytes 3076
  16.4 38.3 %all-to-all-start = ((bf16[64,8,896]{2,1,0:T(8,128)(2,1)}), bf16[64,8,896]{2,1,0:T(8,128)(2,1)S(1)}, u32[]{:S(2)}, u32[]{:S(2)}) async-start(bf16[64,8,896]{2,1,0:T(8,128)(2,1)} %bitcast.7), calls=%async_computation.1 | async-start | bytes 1835008 | tf_op jit(solution)/shard_map/all_to_all | solution.py:459
  33.0 1.0 copy-start.5
  37.2 1.0 copy-start.7
  54.7 5.4 %copy-start.23 = (bf16[64,8,896]{2,1,0:T(8,128)(2,1)}, bf16[64,8,896]{2,1,0:T(8,128)(2,1)S(1)}, u32[]{:S(2)}) copy-start(bf16[64,8,896]{2,1,0:T(8,128)(2,1)S(1)} %all-to-all-done) | copy-start | bytes 2752516
  60.1 1.0 copy-start.10
  61.1 1.0 copy-start.12
  62.2 1.0 copy-start.14
  63.2 1.0 copy-start.16
  64.2 1.0 copy-start.18
  70.3 36.6 %all-to-all-start.1 = ((bf16[64,8,896]{2,1,0:T(8,128)(2,1)}), bf16[64,8,896]{2,1,0:T(8,128)(2,1)S(1)}, u32[]{:S(2)}, u32[]{:S(2)}) async-start(bf16[64,8,896]{2,1,0:T(8,128)(2,1)} %bitcast.11), calls=%async_computation.2 | async-start | bytes 1835008 | tf_op jit(solution)/shard_map/all_to_all | solution.py:459
  124.4 1.3 copy-start.3
  126.3 5.8 %copy-start.22 = (f32[2,64,128]{2,1,0:T(8,128)S(1)}, f32[2,64,128]{2,1,0:T(8,128)}, u32[]{:S(2)}) copy-start(f32[2,64,128]{2,1,0:T(8,128)} %copy-done.21) | copy-start | bytes 196612
  126.3 51.6 %copy-start.4 = (f32[4,16,3,1536]{3,1,2,0:T(8,128)S(1)}, f32[4,16,3,1536]{3,1,2,0:T(8,128)}, u32[]{:S(2)}) copy-start(f32[4,16,3,1536]{3,1,2,0:T(8,128)} %param.13) | copy-start | bytes 3538948
  126.3 51.6 %all-to-all-start.2 = ((bf16[64,16,896]{2,1,0:T(8,128)(2,1)}), bf16[64,16,896]{2,1,0:T(8,128)(2,1)S(1)}, u32[]{:S(2)}, u32[]{:S(2)}) async-start(bf16[64,16,896]{2,1,0:T(8,128)(2,1)} %bitcast.32), calls=%async_computation.3 | async-start | bytes 3670016 | tf_op jit(solution)/shard_map/all_to_all | solution.py:459
  177.9 1.2 copy-start.6
  179.1 1.2 copy-start.8
  180.3 3.9 %copy-start.24 = (f32[4,16,4,512]{3,2,1,0:T(4,128)S(1)}, f32[4,16,4,512]{3,2,1,0:T(4,128)}, u32[]{:S(2)}) copy-start(f32[4,16,4,512]{3,2,1,0:T(4,128)} %param.14) | copy-start | bytes 1572868
  (8 other events, 6.3 us)
Sparse Core Ops, SparseCore 0:
  13.2 46.8 reduce-scatter.1

commit v3 on v2

v3 whole, which is shorter than its diff:
```python
import math

import jax
import jax.numpy as jnp
from jax import lax
from jax.experimental import pallas as pl
from jax.experimental.pallas import tpu as pltpu
from jax.sharding import PartitionSpec as P

QN = 128
KN = 128
STEPS = 5
LAYERS = 4
HEADS = 64
GROUPS = 4
PER_GROUP = 16
NODES = 64
BLOCKS = 64
Q_ROWS, Q_COLS = 192, 1536
KV_ROWS, KV_COLS = 256, 512
Q_OWN, KV_OWN = Q_ROWS // NODES, KV_ROWS // NODES
LANE = 128
Q_TILES, KV_TILES = Q_COLS // LANE, KV_COLS // LANE
SUB = 8
MSG_COLS = 7
MSG = MSG_COLS * LANE
ROWS = NODES * SUB
HALF = ROWS // 2
EXTRA = ROWS // 4
RING = ROWS - EXTRA
PEAK_TILE = Q_OWN * Q_TILES + KV_OWN * KV_TILES
SPLIT = Q_OWN * Q_TILES // SUB
SPLIT_SUB = Q_OWN * Q_TILES % SUB

MOMENTUM_RATE = 0.95
LEARN_RATE = 0.02
DECAY_RATE = 0.1
CLIP_LEVEL = 100.0
NEWTON_FIRST = 3.4445
NEWTON_SECOND = -4.775
NEWTON_THIRD = 2.0315
EPSILON = 1e-07
Q_SCALE = 0.2 * math.sqrt(max(Q_ROWS, Q_COLS))
KV_SCALE = 0.2 * math.sqrt(max(KV_ROWS, KV_COLS))

F32 = jnp.float32
BF16 = jnp.bfloat16
I32 = jnp.int32
PARAMS = pltpu.CompilerParams(vmem_limit_bytes=24 * 1024 * 1024)


def place(tile):
    col, sub = divmod(tile, SUB)
    return slice(sub * BLOCKS, (sub + 1) * BLOCKS), slice(col * LANE, (col + 1) * LANE)


def tiles_of(kind):
    if kind == "q":
        return [(r, ct, r * Q_TILES + ct) for r in range(Q_OWN) for ct in range(Q_TILES)]
    base = Q_OWN * Q_TILES
    return [(r, ct, base + r * KV_TILES + ct) for r in range(KV_OWN) for ct in range(KV_TILES)]


def in_hbm(x):
    return pltpu.with_memory_space_constraint(x, pltpu.HBM)


def iota(shape, dim):
    return lax.broadcasted_iota(I32, shape, dim)


def dot(a, b):
    return jnp.dot(a, b, preferred_element_type=F32)


def dot_nt(a, b):
    return lax.dot_general(a, b, (((1,), (1,)), ((), ())), preferred_element_type=F32)


def one(cond):
    return jnp.where(cond, 1.0, 0.0).astype(BF16)


def pack_matrix():
    row, col = iota((ROWS, ROWS), 0), iota((ROWS, ROWS), 1)
    return one(((row >> 3) == (col & 63)) & ((row & 7) == (col >> 6)))


def unpack_matrix():
    row, col = iota((ROWS, ROWS), 0), iota((ROWS, ROWS), 1)
    return one(((row & 63) == (col >> 3)) & ((row >> 6) == (col & 7)))


def natural_matrix(own):
    size = own * NODES
    row, col = iota((size, size), 0), iota((size, size), 1)
    return one(row == (col & 63) * own + (col >> 6))


def split_matrix(own):
    size = own * NODES
    row, col = iota((size, size), 0), iota((size, size), 1)
    return one(col == (row & 63) * own + (row >> 6))


def to_message(q_natural, kv_natural, tiles_ref):
    q_split = dot(split_matrix(Q_OWN), q_natural).astype(BF16)
    kv_split = dot(split_matrix(KV_OWN), kv_natural).astype(BF16)
    tiles_ref[:, SPLIT * LANE :] = jnp.zeros((ROWS, MSG - SPLIT * LANE), BF16)
    for r, ct, tile in tiles_of("q"):
        rows, cols = place(tile)
        tiles_ref[rows, cols] = q_split[r * NODES : (r + 1) * NODES, ct * LANE : (ct + 1) * LANE]
    for r, ct, tile in tiles_of("kv"):
        rows, cols = place(tile)
        tiles_ref[rows, cols] = kv_split[r * NODES : (r + 1) * NODES, ct * LANE : (ct + 1) * LANE]
    return dot(pack_matrix(), tiles_ref[...])


def from_tiles(tiles, q_ref, kv_ref):
    for r, ct, tile in tiles_of("q"):
        rows, cols = place(tile)
        q_ref[r * NODES : (r + 1) * NODES, ct * LANE : (ct + 1) * LANE] = tiles[rows, cols]
    for r, ct, tile in tiles_of("kv"):
        rows, cols = place(tile)
        kv_ref[r * NODES : (r + 1) * NODES, ct * LANE : (ct + 1) * LANE] = tiles[rows, cols]
    return dot(natural_matrix(Q_OWN), q_ref[...]), dot(natural_matrix(KV_OWN), kv_ref[...])


def by_kind(q_matrix, kv_matrix, source, q_rows):
    edge = SPLIT * LANE
    q_part = dot(q_matrix, source[:, : edge + LANE])
    kv_part = dot(kv_matrix, source[:, edge:])
    mixed = jnp.where(q_rows, q_part[:, edge:], kv_part[:, :LANE])
    return jnp.concatenate([q_part[:, :edge], mixed, kv_part[:, LANE:]], axis=1)


def call(kernel, out_shape, *operands, **options):
    return pl.pallas_call(kernel, out_shape=out_shape, compiler_params=PARAMS, **options)(*operands)


def whole(*dims):
    return pl.BlockSpec(dims, lambda i: (0,) * len(dims))


def shape(dims, dtype):
    return jax.ShapeDtypeStruct(dims, dtype)


def parts_of(value):
    high = value.astype(BF16).astype(F32)
    middle = (value - high).astype(BF16).astype(F32)
    return high, middle, (value - high) - middle


def peak_tile(column):
    high, middle, low = parts_of(column)
    lane = iota((column.shape[0], LANE), 1)
    return jnp.where(lane == 0, high, jnp.where(lane == 1, middle, jnp.where(lane == 2, low, 0.0))).astype(BF16)


def peak_column(tile):
    lane = iota(tile.shape, 1)
    return jnp.sum(jnp.where(lane < 3, tile.astype(F32), 0.0), axis=1, keepdims=True)


def group_tiles(group, q_ref, kv_ref, peak_ref, put):
    for tile in range(PEAK_TILE + 1, MSG_COLS * SUB):
        rows, cols = place(tile)
        put(rows.start, cols, jnp.zeros((BLOCKS, LANE), BF16))
    rows, cols = place(PEAK_TILE)
    for layer in range(LAYERS):
        spread = jnp.broadcast_to(peak_ref[layer : layer + 1, :], (PER_GROUP, HEADS))
        mine = iota((PER_GROUP, HEADS), 1) == iota((PER_GROUP, HEADS), 0) + group * PER_GROUP
        column = jnp.sum(jnp.where(mine, spread, 0.0), axis=1, keepdims=True)
        put(rows.start + layer * PER_GROUP, cols, peak_tile(column))
    for kind, ref in (("q", q_ref), ("kv", kv_ref)):
        for r, ct, tile in tiles_of(kind):
            rows, cols = place(tile)
            for layer in range(LAYERS):
                put(rows.start + layer * PER_GROUP, cols, ref[layer, r, :, ct * LANE : (ct + 1) * LANE])


def window(start, size):
    return slice(start, start + size)


def first_kernel(
    group_ref, q_far, kv_far, q_next, kv_next, q_last, kv_last, peak_ref, forward_out, backward_out
):
    def put_far(start, cols, value):
        out = (forward_out, backward_out)[start // HALF]
        out[window(start % HALF, value.shape[0]), cols] = value

    def put_next(start, cols, value):
        if start >= ROWS - EXTRA:
            forward_out[window(start - ROWS + EXTRA + HALF, value.shape[0]), cols] = value

    def put_last(start, cols, value):
        if start < EXTRA:
            backward_out[window(start + HALF, value.shape[0]), cols] = value

    group_tiles(group_ref[0], q_far, kv_far, peak_ref, put_far)
    group_tiles(group_ref[1], q_next, kv_next, peak_ref, put_next)
    group_tiles(group_ref[2], q_last, kv_last, peak_ref, put_last)


def mine_kernel(group_ref, q_ref, kv_ref, peak_ref, out_ref):
    def put(start, cols, value):
        out_ref[window(start, value.shape[0]), cols] = value

    group_tiles(group_ref[0], q_ref, kv_ref, peak_ref, put)


def combine_kernel(
    group_ref, q_next, kv_next, q_last, kv_last, peak_ref, from_last, from_next, next_out, last_out
):
    def put_next(start, cols, value):
        if start >= ROWS - EXTRA:
            return
        if start < HALF:
            value = (value.astype(F32) + from_last[window(start, value.shape[0]), cols].astype(F32)).astype(BF16)
        next_out[window(start, value.shape[0]), cols] = value

    def put_last(start, cols, value):
        if start < EXTRA:
            return
        here = window(start - EXTRA, value.shape[0])
        if start >= HALF:
            far = from_next[window(start - HALF, value.shape[0]), cols]
            if window(start // BLOCKS * BLOCKS, BLOCKS) == peak_rows and cols == peak_cols:
                value = peak_tile(jnp.maximum(peak_column(value), peak_column(far)))
            else:
                value = (value.astype(F32) + far.astype(F32)).astype(BF16)
        last_out[here, cols] = value

    peak_rows, peak_cols = place(PEAK_TILE)
    group_tiles(group_ref[0], q_next, kv_next, peak_ref, put_next)
    group_tiles(group_ref[1], q_last, kv_last, peak_ref, put_last)


def arrange_call(kernel, groups, grad_query, grad_kv, peaks, extra, out_shape, hint=None):
    count = groups.shape[0]

    def at(index):
        return [
            pl.BlockSpec((LAYERS, Q_OWN, PER_GROUP, Q_COLS), lambda i, g: (0, 0, g[index], 0)),
            pl.BlockSpec((LAYERS, KV_OWN, PER_GROUP, KV_COLS), lambda i, g: (0, 0, g[index], 0)),
        ]

    def all_of(x):
        return pl.BlockSpec(x.shape, lambda i, g: (0,) * len(x.shape))

    return pl.pallas_call(
        kernel,
        out_shape=out_shape,
        grid_spec=pltpu.PrefetchScalarGridSpec(
            num_scalar_prefetch=1,
            grid=(1,),
            in_specs=sum([at(index) for index in range(count)], []) + [all_of(x) for x in (peaks, *extra)],
            out_specs=[all_of(x) for x in out_shape],
        ),
        compiler_params=PARAMS,
        cost_estimate=hint,
    )(groups, *([in_hbm(grad_query), grad_kv] * count), peaks, *extra)


SEND, LATE, SEND_BACK, LATE_BACK = range(4)


def table_kernel(group_ref, q_ref, kv_ref, table_ref, over_ref, fill_ref):
    group = group_ref[0]
    down, across = iota((NODES, BLOCKS), 0), iota((NODES, BLOCKS), 1)

    def count(cond, axis):
        return jnp.sum(jnp.where(cond, 1.0, 0.0), axis=axis, keepdims=True)

    for kind, ref in enumerate((q_ref, kv_ref)):
        owner_row = jnp.zeros((SUB, BLOCKS), F32)
        for layer in range(LAYERS):
            piece = jnp.broadcast_to(ref[group, layer].astype(F32), (SUB, PER_GROUP)).astype(BF16)
            spot = iota((PER_GROUP, BLOCKS), 1) == iota((PER_GROUP, BLOCKS), 0) + layer * PER_GROUP
            owner_row += dot(piece, one(spot))
        owner_row = owner_row[:1].astype(I32)
        spread = jnp.broadcast_to(owner_row, (BLOCKS, BLOCKS))
        owner_col = jnp.sum(jnp.where(down == across, spread, 0).astype(F32), axis=1, keepdims=True).astype(I32)
        same = owner_col == owner_row
        slot_col = count(same & (across < down), 1)
        slot_row = count(same & (down < across), 0)
        hits = down == owner_row
        hits_back = owner_col == across
        fill_col, fill_row = count(hits, 1), count(hits_back, 0)
        over_col, over_row = slot_col > 0.5, slot_row > 0.5
        free_col, free_row = fill_col < 0.5, fill_row < 0.5
        over_rank_col, over_rank_row = count(over_row & (across < down), 1), count(over_col & (down < across), 0)
        free_rank_col, free_rank_row = count(free_row & (across < down), 1), count(free_col & (down < across), 0)
        table_ref[kind, SEND] = one(
            (hits & ~over_row) | (free_col & over_row & (free_rank_col == over_rank_row))
        )
        table_ref[kind, LATE] = one(hits & over_row)
        table_ref[kind, SEND_BACK] = one(
            (hits_back & ~over_col) | (free_row & over_col & (free_rank_row == over_rank_col))
        )
        table_ref[kind, LATE_BACK] = one(hits_back & over_col)
        over_ref[kind] = jnp.broadcast_to(jnp.where(over_col, 1.0, 0.0), (BLOCKS, LANE))
        fill_ref[kind] = jnp.broadcast_to(fill_col, (BLOCKS, LANE))


def tables(group, owner_query, owner_kv):
    return call(
        table_kernel,
        (shape((2, 4, NODES, BLOCKS), BF16), shape((2, BLOCKS, LANE), F32), shape((2, NODES, LANE), F32)),
        group,
        jnp.transpose(owner_query, (0, 1, 3, 2)),
        jnp.transpose(owner_kv, (0, 1, 3, 2)),
        in_specs=[pl.BlockSpec(memory_space=pltpu.SMEM)] + [pl.BlockSpec(memory_space=pltpu.VMEM)] * 2,
    )


def to_peers(table):
    rows = one((iota((ROWS, NODES), 0) >> 3) == iota((ROWS, NODES), 1))
    cols = one(iota((BLOCKS, ROWS), 0) == (iota((BLOCKS, ROWS), 1) & 63))
    wide = dot(dot(rows, table).astype(BF16), cols)
    row, col = iota((ROWS, ROWS), 0), iota((ROWS, ROWS), 1)
    return jnp.where((row & 7) == (col >> 6), wide, 0.0).astype(BF16)


def to_tiles(table):
    rows = one((iota((ROWS, BLOCKS), 0) & 63) == iota((ROWS, BLOCKS), 1))
    cols = one(iota((NODES, ROWS), 0) == (iota((NODES, ROWS), 1) >> 3))
    wide = dot(dot(rows, table).astype(BF16), cols)
    row, col = iota((ROWS, ROWS), 0), iota((ROWS, ROWS), 1)
    return jnp.where((row >> 6) == (col & 7), wide, 0.0).astype(BF16)


def late_kernel(q_ref, kv_ref, out_ref, tiles_ref):
    out_ref[...] = to_message(q_ref[0, 0, 0], kv_ref[0, 0, 0], tiles_ref).astype(BF16)


def late_message(momentum_query, momentum_kv):
    return call(
        late_kernel,
        pltpu.HBM((ROWS, MSG), BF16),
        in_hbm(momentum_query),
        in_hbm(momentum_kv),
        grid=(1,),
        in_specs=[
            pl.BlockSpec((1, 1, 1, Q_ROWS, Q_COLS), lambda i: (0, 0, 1, 0, 0)),
            pl.BlockSpec((1, 1, 1, KV_ROWS, KV_COLS), lambda i: (0, 0, 1, 0, 0)),
        ],
        out_specs=pl.BlockSpec((ROWS, MSG), lambda i: (0, 0)),
        scratch_shapes=[pltpu.VMEM((ROWS, MSG), BF16)],
    )


def earlier_kernel(late_in_ref, table_ref, out_ref):
    tile_rows = iota((ROWS, LANE), 0) < SPLIT_SUB * BLOCKS
    q_matrix, kv_matrix = to_tiles(table_ref[0, LATE_BACK]), to_tiles(table_ref[1, LATE_BACK])
    out_ref[...] = by_kind(q_matrix, kv_matrix, late_in_ref[...], tile_rows).astype(BF16)


def send_kernel(
    mine_ref, last_ref, next_ref, first_last, first_next, earlier_ref, table_ref, over_ref, out_hbm, carried_hbm,
    chosen, carried, message, sems,
):
    row = iota((ROWS, LANE), 0)
    q_over = jnp.concatenate([over_ref[0]] * SUB, axis=0)
    kv_over = jnp.concatenate([over_ref[1]] * SUB, axis=0)
    for col in range(MSG_COLS):
        lanes = slice(col * LANE, (col + 1) * LANE)
        last = jnp.concatenate([last_ref[:, lanes], first_last[HALF:, lanes]], axis=0).astype(F32)
        following = jnp.concatenate([first_next[HALF:, lanes], next_ref[:, lanes]], axis=0).astype(F32)
        reduced = mine_ref[:, lanes].astype(F32) + (last + following)
        reduced = reduced.astype(BF16).astype(F32)
        moved = MOMENTUM_RATE * earlier_ref[:, lanes].astype(F32) + reduced
        carried[:, lanes] = moved.astype(BF16)
        if col < SPLIT:
            mask = q_over
        elif col == SPLIT:
            mask = jnp.where(row < SPLIT_SUB * BLOCKS, q_over, kv_over)
        else:
            mask = kv_over
        chosen[:, lanes] = jnp.where(mask > 0.5, reduced + MOMENTUM_RATE * moved, reduced).astype(BF16)
    carried_copy = pltpu.make_async_copy(carried, carried_hbm, sems.at[0])
    carried_copy.start()
    edge = SPLIT * LANE
    q_part = dot(to_peers(table_ref[0, SEND]), chosen[:, : edge + LANE])
    message[:, :edge] = q_part[:, :edge].astype(BF16)
    q_copy = pltpu.make_async_copy(message.at[:, :edge], out_hbm.at[:, :edge], sems.at[1])
    q_copy.start()
    kv_part = dot(to_peers(table_ref[1, SEND]), chosen[:, edge:])
    peer_rows = (row & 7) < SPLIT_SUB
    message[:, edge : edge + LANE] = jnp.where(peer_rows, q_part[:, edge:], kv_part[:, :LANE]).astype(BF16)
    rows, cols = place(PEAK_TILE)
    peak = jnp.maximum(peak_column(mine_ref[rows, cols]), peak_column(last_ref[rows, cols]))
    peak = jnp.maximum(peak, peak_column(next_ref[rows.start - EXTRA : rows.stop - EXTRA, cols]))
    spot = iota((BLOCKS, LANE), 0) == (iota((BLOCKS, LANE), 1) & 63)
    peak = jnp.sum(jnp.where(spot, jnp.broadcast_to(peak, (BLOCKS, LANE)), 0.0), axis=0, keepdims=True)
    high, middle, low = parts_of(peak)
    sub = PEAK_TILE % SUB
    first_half = iota((ROWS, LANE), 1) < LANE // 2
    last = kv_part[:, cols.start - edge :]
    last = jnp.where((row & 7) == sub, jnp.where(first_half, high, middle), last)
    last = jnp.where((row & 7) == sub + 1, jnp.where(first_half, low, 0.0), last)
    message[:, edge + LANE : cols.start] = kv_part[:, LANE : cols.start - edge].astype(BF16)
    message[:, cols] = last.astype(BF16)
    kv_copy = pltpu.make_async_copy(message.at[:, edge:], out_hbm.at[:, edge:], sems.at[2])
    kv_copy.start()
    carried_copy.wait()
    q_copy.wait()
    kv_copy.wait()


def late_out_kernel(carried_ref, table_ref, out_ref):
    peer_rows = (iota((ROWS, LANE), 0) & 7) < SPLIT_SUB
    q_matrix, kv_matrix = to_peers(table_ref[0, LATE]), to_peers(table_ref[1, LATE])
    out_ref[...] = by_kind(q_matrix, kv_matrix, carried_ref[...], peer_rows).astype(BF16)


def halves(x):
    high = x.astype(BF16)
    return high, (x - high.astype(F32)).astype(BF16)


def product(a, b, op):
    return op(a[0], b[0]) + (op(a[0], b[1]) + op(a[1], b[0]))


def newton_step(x_ref):
    x = x_ref[...]
    parts = halves(x)
    square = product(parts, parts, dot_nt)
    square_parts = halves(square)
    polynomial = NEWTON_SECOND * square + NEWTON_THIRD * product(square_parts, square_parts, dot)
    x_ref[...] = NEWTON_FIRST * x + product(halves(polynomial), parts, dot)


def owner_kernel(
    node_ref, in_ref, q_mom, kv_mom, fill_ref, out_ref, q_new, kv_new, q_x, kv_x, q_half, kv_half, tiles_ref
):
    node = node_ref[0]
    received = dot(unpack_matrix(), in_ref[...])
    arrived = from_tiles(received.astype(BF16), q_half, kv_half)
    for kind, gradient, mom, new, x_ref in (
        (0, arrived[0], q_mom, q_new, q_x),
        (1, arrived[1], kv_mom, kv_new, kv_x),
    ):
        used = fill_ref[kind, pl.ds(node, 1), :1] > 0.5
        carried = MOMENTUM_RATE * mom[0, 0, 0].astype(F32) + gradient
        new[0, 0, 0] = jnp.where(used, carried, 0.0).astype(BF16)
        direction = jnp.where(used, gradient + MOMENTUM_RATE * carried, gradient)
        norm = jnp.sqrt(jnp.sum(direction * direction)) + EPSILON
        x_ref[...] = direction / norm

    def body(_, carry):
        newton_step(q_x)
        newton_step(kv_x)
        return carry

    lax.fori_loop(0, STEPS, body, 0)
    outgoing = to_message((q_x[...] * Q_SCALE).astype(BF16), (kv_x[...] * KV_SCALE).astype(BF16), tiles_ref)
    out_ref[...] = outgoing.astype(BF16)


def owner_step(node, arrived, momentum_query, momentum_kv, fill):
    q_slot = pl.BlockSpec((1, 1, 1, Q_ROWS, Q_COLS), lambda i: (0, 0, 0, 0, 0))
    kv_slot = pl.BlockSpec((1, 1, 1, KV_ROWS, KV_COLS), lambda i: (0, 0, 0, 0, 0))
    return call(
        owner_kernel,
        (
            pltpu.HBM((ROWS, MSG), BF16),
            pltpu.HBM((1, 1, 2, Q_ROWS, Q_COLS), BF16),
            pltpu.HBM((1, 1, 2, KV_ROWS, KV_COLS), BF16),
        ),
        node,
        arrived,
        in_hbm(momentum_query),
        in_hbm(momentum_kv),
        fill,
        grid=(1,),
        in_specs=[pl.BlockSpec(memory_space=pltpu.SMEM), whole(ROWS, MSG), q_slot, kv_slot, whole(2, NODES, LANE)],
        out_specs=[whole(ROWS, MSG), q_slot, kv_slot],
        scratch_shapes=[
            pltpu.VMEM((Q_ROWS, Q_COLS), F32),
            pltpu.VMEM((KV_ROWS, KV_COLS), F32),
            pltpu.VMEM((Q_ROWS, Q_COLS), BF16),
            pltpu.VMEM((KV_ROWS, KV_COLS), BF16),
            pltpu.VMEM((ROWS, MSG), BF16),
        ],
    )


def settle_kernel(in_ref, arrived_ref, q_old, kv_old, q_new, kv_new, factor_ref, q_half, kv_half):
    matrix = unpack_matrix()
    late = dot(matrix, in_ref[...]).astype(BF16)
    q_late, kv_late = from_tiles(late, q_half, kv_half)
    q_new[0, 0, 0] = q_late.astype(BF16)
    kv_new[0, 0, 0] = kv_late.astype(BF16)

    rows, cols = place(PEAK_TILE)
    parts = dot(matrix, arrived_ref[:, cols])
    top, bottom = parts[rows], parts[place(PEAK_TILE + 1)[0]]
    peaks = jnp.max((top[:, :BLOCKS] + top[:, BLOCKS:]) + bottom[:, :BLOCKS], axis=0, keepdims=True)
    diagonal = iota((BLOCKS, BLOCKS), 0) == iota((BLOCKS, BLOCKS), 1)
    peak_col = jnp.sum(jnp.where(diagonal, jnp.broadcast_to(peaks, (BLOCKS, BLOCKS)), 0.0), axis=1, keepdims=True)
    shrink = jnp.minimum(1.0, CLIP_LEVEL / peak_col)
    factor_ref[0] = jnp.broadcast_to(jnp.sqrt(shrink), (BLOCKS, LANE))
    factor_ref[1] = jnp.broadcast_to(shrink, (BLOCKS, LANE))


def settle(late, arrived, q_momentum, kv_momentum):
    anywhere = pl.BlockSpec(memory_space=pl.ANY)
    return call(
        settle_kernel,
        (
            shape((1, 1, 2, Q_ROWS, Q_COLS), BF16),
            shape((1, 1, 2, KV_ROWS, KV_COLS), BF16),
            shape((2, BLOCKS, LANE), F32),
        ),
        late,
        arrived,
        q_momentum,
        kv_momentum,
        grid=(1,),
        in_specs=[whole(ROWS, MSG), whole(ROWS, MSG), anywhere, anywhere],
        out_specs=[
            pl.BlockSpec((1, 1, 1, Q_ROWS, Q_COLS), lambda i: (0, 0, 1, 0, 0)),
            pl.BlockSpec((1, 1, 1, KV_ROWS, KV_COLS), lambda i: (0, 0, 1, 0, 0)),
            whole(2, BLOCKS, LANE),
        ],
        scratch_shapes=[pltpu.VMEM((Q_ROWS, Q_COLS), BF16), pltpu.VMEM((KV_ROWS, KV_COLS), BF16)],
        input_output_aliases={2: 0, 3: 1},
    )


def finish_kernel(
    node_ref, in_ref, table_ref, factor_ref, weight_hbm, update_hbm, weight_new_hbm, kv_update_ref,
    weight, update, sems,
):
    fetch = pltpu.make_async_copy(weight_hbm, weight, sems.at[0])
    fetch.start()
    edge = SPLIT * LANE
    kv_rows = dot(to_tiles(table_ref[1, SEND_BACK]), in_ref[:, edge:])
    for r, ct, tile in tiles_of("kv"):
        rows, cols = place(tile)
        lanes = slice(cols.start - edge, cols.stop - edge)
        kv_update_ref[r, :, ct * LANE : (ct + 1) * LANE] = kv_rows[rows, lanes].astype(BF16)
    q_rows = dot(to_tiles(table_ref[0, SEND_BACK]), in_ref[:, : edge + LANE])
    fetch.wait()
    copies = []
    for r in range(Q_OWN):
        factor = jnp.where(node_ref[0] * Q_OWN + r < QN, factor_ref[0], factor_ref[1])
        factor = factor.reshape(LAYERS, PER_GROUP, LANE)
        for ct in range(Q_TILES):
            rows, cols = place(r * Q_TILES + ct)
            lanes = slice(ct * LANE, (ct + 1) * LANE)
            step = q_rows[rows, cols].reshape(LAYERS, PER_GROUP, LANE)
            update[:, r, :, lanes] = step.astype(BF16)
            old = weight[:, r, :, lanes]
            weight[:, r, :, lanes] = (old - LEARN_RATE * (step + DECAY_RATE * old)) * factor
        copies.append(pltpu.make_async_copy(update.at[:, r], update_hbm.at[:, r], sems.at[1 + 2 * r]))
        copies.append(pltpu.make_async_copy(weight.at[:, r], weight_new_hbm.at[:, r], sems.at[2 + 2 * r]))
        copies[-2].start()
        copies[-1].start()
    for copy in copies:
        copy.wait()


def finish(node, returned, table, factors, weight_query):
    q_dims = (LAYERS, Q_OWN, PER_GROUP, Q_COLS)
    kv_dims = (KV_OWN, BLOCKS, KV_COLS)
    outside = pl.BlockSpec(memory_space=pltpu.HBM)
    return call(
        finish_kernel,
        (pltpu.HBM(q_dims, BF16), pltpu.HBM(q_dims, F32), shape(kv_dims, BF16)),
        node,
        returned,
        table,
        factors,
        in_hbm(weight_query),
        grid=(1,),
        in_specs=[
            pl.BlockSpec(memory_space=pltpu.SMEM),
            whole(ROWS, MSG),
            whole(2, 4, NODES, BLOCKS),
            whole(2, BLOCKS, LANE),
            outside,
        ],
        out_specs=[outside, outside, whole(*kv_dims)],
        scratch_shapes=[
            pltpu.VMEM(q_dims, F32),
            pltpu.VMEM(q_dims, BF16),
            pltpu.SemaphoreType.DMA((1 + 2 * Q_OWN,)),
        ],
    )


def exchange(message):
    return lax.all_to_all(message, "fsdp", split_axis=0, concat_axis=0, tiled=True)


def on_device(
    grad_query, grad_kv, momentum_query, momentum_kv, weight_query, weight_kv, owner_query, owner_kv, max_logits
):
    my_group = lax.axis_index("dp")
    my_node = lax.axis_index("fsdp")

    node = my_node.astype(I32).reshape(1)
    forward = [(i, (i + 1) % GROUPS) for i in range(GROUPS)]
    backward = [(i, (i + 3) % GROUPS) for i in range(GROUPS)]

    def turn(*steps):
        return (my_group.astype(I32) + jnp.asarray(steps, I32)) % GROUPS

    q_grads = jnp.transpose(grad_query[0], (0, 2, 1, 3))
    kv_grads = jnp.transpose(grad_kv[0], (0, 2, 1, 3))
    peaks = max_logits[0]
    ring_shape = (shape((RING, MSG), BF16),) * 2
    to_next, to_last = arrange_call(first_kernel, turn(2, 1, 3), q_grads, kv_grads, peaks, (), ring_shape)
    to_next, to_last, momentum_query, momentum_kv = lax.optimization_barrier(
        (to_next, to_last, momentum_query, momentum_kv)
    )
    from_last = lax.ppermute(to_next, "dp", forward)
    from_next = lax.ppermute(to_last, "dp", backward)
    late_in = exchange(late_message(momentum_query, momentum_kv))
    table, over, fill = tables(turn(0), owner_query, owner_kv)
    hint = pl.CostEstimate(flops=10**12, bytes_accessed=10**10, transcendentals=0)
    to_next, to_last = arrange_call(
        combine_kernel, turn(1, 3), q_grads, kv_grads, peaks, (from_last, from_next),
        ring_shape, hint,
    )
    sum_last = lax.ppermute(to_next, "dp", forward)
    sum_next = lax.ppermute(to_last, "dp", backward)
    (mine,) = arrange_call(mine_kernel, turn(0), q_grads, kv_grads, peaks, (), (pltpu.HBM((ROWS, MSG), BF16),))
    earlier = call(earlier_kernel, shape((ROWS, MSG), BF16), late_in, table)

    outside = pl.BlockSpec(memory_space=pltpu.HBM)
    message, carried = call(
        send_kernel,
        (pltpu.HBM((ROWS, MSG), BF16), pltpu.HBM((ROWS, MSG), BF16)),
        mine, sum_last, sum_next, from_last, from_next, earlier, table, over,
        grid=(1,),
        in_specs=[whole(ROWS, MSG)] + [whole(RING, MSG)] * 4 + [whole(ROWS, MSG)]
        + [whole(2, 4, NODES, BLOCKS), whole(2, BLOCKS, LANE)],
        out_specs=[outside, outside],
        scratch_shapes=[pltpu.VMEM((ROWS, MSG), BF16)] * 3 + [pltpu.SemaphoreType.DMA((3,))],
    )
    late_out = call(late_out_kernel, pltpu.HBM((ROWS, MSG), BF16), carried, table)
    arrived, late_out = lax.optimization_barrier((exchange(message), late_out))
    late = exchange(late_out)
    outgoing, q_momentum, kv_momentum = owner_step(node, arrived, momentum_query, momentum_kv, fill)
    late, outgoing = lax.optimization_barrier((late, outgoing))
    returned = exchange(outgoing)
    q_momentum, kv_momentum, factors = settle(late, arrived, q_momentum, kv_momentum)
    q_update, q_weight, kv_update = finish(
        node, returned, table, factors, jnp.transpose(weight_query, (0, 2, 1, 3))
    )
    kv_update = jnp.transpose(kv_update.reshape(KV_OWN, LAYERS, PER_GROUP, KV_COLS), (1, 2, 0, 3))
    kv_index = my_node * KV_OWN + jnp.arange(KV_OWN, dtype=I32)
    root_shrink = factors[0, :, 0].reshape(LAYERS, PER_GROUP)
    kv_factor = jnp.where(kv_index[None, None, :, None] < KN, root_shrink[:, :, None, None], 1.0)
    kv_weight = (weight_kv - LEARN_RATE * (kv_update.astype(F32) + DECAY_RATE * weight_kv)) * kv_factor
    return (
        jnp.transpose(q_update, (0, 2, 1, 3)),
        kv_update,
        jnp.transpose(q_weight, (0, 2, 1, 3)),
        kv_weight,
        q_momentum,
        kv_momentum,
    )


def solution(mesh):
    return jax.shard_map(
        on_device,
        mesh=mesh,
        in_specs=(
            P("dp", None, None, "fsdp", None),
            P("dp", None, None, "fsdp", None),
            P("dp", "fsdp", None, None, None),
            P("dp", "fsdp", None, None, None),
            P(None, "dp", "fsdp", None),
            P(None, "dp", "fsdp", None),
            P(),
            P(),
            P(("dp", "fsdp"), None, None),
        ),
        out_specs=(
            P(None, "dp", "fsdp", None),
            P(None, "dp", "fsdp", None),
            P(None, "dp", "fsdp", None),
            P(None, "dp", "fsdp", None),
            P("dp", "fsdp", None, None, None),
            P("dp", "fsdp", None, None, None),
        ),
        check_vma=False,
    )
```

time: 194 us -> 158 us (0.81)
  local copies, waits for them, and re-layouts: 22.8 us -> 1.67 us
  Pallas kernels: 33.2 us -> 46.6 us
  between operations: 14.2 us -> 0.84 us
  blocking collectives: 9.11 us -> 0 us
  waiting for transfers between devices: 79.5 us -> 72.1 us
  starting transfers between devices: 28.7 us -> 33.7 us
  other arithmetic: 4.73 us -> 1.4 us
    unnamed x58 -> x17, local copies, waits for them, and re-layouts: 22.1 us -> 1.48 us
    pmax x1 -> x0, blocking collectives: 9.11 us -> none  [on_device(): peaks = lax.pmax(max_logits, 'dp')[0]]
    pallas_call x0 -> x3, Pallas kernels: none -> 8.39 us  [arrange_call(): pl.pallas_call(kernel, out_shape=out_shape, grid_spec=pltpu.PrefetchScala...]
    reduce_scatter x1 -> x0, waiting for transfers between devices: 5.37 us -> none  [on_device(): reduced = lax.psum_scatter(terms, 'dp', scatter_dimension=0, tiled=True)]
    pallas_call x7 -> x8, Pallas kernels: 33.2 us -> 38.2 us  [call(): pl.pallas_call(kernel, out_shape=out_shape, compiler_params=PARAMS, **opt...]
    ppermute x0 -> x4, starting transfers between devices: none -> 4.3 us  [the longest x1 1.49 us: on_device(): from_last = lax.ppermute(to_next, 'dp', forward)]
    all_to_all x3 -> x4, waiting for transfers between devices: 74.1 us -> 71.3 us  [exchange(): lax.all_to_all(message, 'fsdp', split_axis=0, concat_axis=0, tiled=True)]
    all_to_all x3 -> x4, starting transfers between devices: 28.7 us -> 29.4 us  [exchange(): lax.all_to_all(message, 'fsdp', split_axis=0, concat_axis=0, tiled=True)]
  transfers between devices with their start and end apart: 4 -> 8, of which waited for: 4 -> 5; matrix products, arithmetic and copies ran while one was open for 2% -> 0% of each run, Pallas kernels for 3% -> 23%
where the time goes in v3:
time: 158 us; the launch traced here: 156 us
  waiting for transfers between devices  72.1 us (46%)
  Pallas kernels  46.6 us (29%)
  starting transfers between devices  33.7 us (21%)
  local copies, waits for them, and re-layouts  1.67 us (1%)
    all_to_all x4, waiting for transfers between devices, exchange(): lax.all_to_all(message, 'fsdp', split_axis=0, concat_axis=0, tiled=True)  71.3 us
    pallas_call x8, Pallas kernels, call(): pl.pallas_call(kernel, out_shape=out_shape, compiler_params=PARAMS, **opt...  38.2 us
    all_to_all x4, starting transfers between devices, exchange(): lax.all_to_all(message, 'fsdp', split_axis=0, concat_axis=0, tiled=True)  29.4 us
    pallas_call x3, Pallas kernels, arrange_call(): pl.pallas_call(kernel, out_shape=out_shape, grid_spec=pltpu.PrefetchScala...  8.39 us
  transfers between devices with their start and end apart: 8, of which 5 were waited for; matrix products, arithmetic and copies ran while one was open for 0% of the time, Pallas kernels for 23%

profile of v3, /device:TPU:2, one launch (start us, length us, event | category | flops | bytes accessed | tf_op | source)
XLA Modules:
  0.0 156.3 jit_solution(11463262665876336188)
XLA Ops:
  0.7 1.4 copy.28
  2.1 3.1 %shard_map.173 = (bf16[384,896]{1,0:T(8,128)(2,1)}, bf16[384,896]{1,0:T(8,128)(2,1)S(1)}) custom-call(s32[3]{0:T(128)S(1)} %and_select_fusion.group_ref, bf16[4,3,64,1536]{3,2,1,0:T(8,128)(2,1)} %bitcast.44, bf16[4,4,64,512]{3,2,1,0:T(8,128)(2,1)S(1)} %bitcast.28, bf16[4,3,64,1536]{3,2,1,0:T(8,128)(2,1)} %bitcast.45, bf16[4,4,64,512]{3,2,1,0:T(8,128)(2,1)S(1)} %bitcast.29, ...), custom_call_target="tpu_custom_call" | custom-call | tf_op jit(solution)/shard_map/pallas_call | solution.py:253
  5.2 1.5 collective-permute-start
  6.7 0.8 collective-permute-start.1
  7.5 3.1 %shard_map.175 = bf16[512,896]{1,0:T(8,128)(2,1)} custom-call(bf16[1,1,2,192,1536]{4,3,2,1,0:T(8,128)(2,1)} %q_mom, bf16[1,1,2,256,512]{4,3,2,1,0:T(8,128)(2,1)} %kv_mom), custom_call_target="tpu_custom_call" | custom-call | tf_op jit(solution)/shard_map/pallas_call | solution.py:138
  10.6 12.2 %all-to-all-start = ((bf16[64,8,896]{2,1,0:T(8,128)(2,1)}), bf16[64,8,896]{2,1,0:T(8,128)(2,1)}, u32[]{:S(2)}, u32[]{:S(2)}) async-start(bf16[64,8,896]{2,1,0:T(8,128)(2,1)} %bitcast.50), calls=%async_computation | async-start | bytes 1835008 | tf_op jit(solution)/shard_map/all_to_all | solution.py:598
  23.6 3.2 %shard_map.174 = (bf16[384,896]{1,0:T(8,128)(2,1)}, bf16[384,896]{1,0:T(8,128)(2,1)}) custom-call(s32[2]{0:T(128)S(1)} %and_select_fusion.1.group_ref, bf16[4,3,64,1536]{3,2,1,0:T(8,128)(2,1)} %bitcast.47, bf16[4,4,64,512]{3,2,1,0:T(8,128)(2,1)S(1)} %bitcast.31, bf16[4,3,64,1536]{3,2,1,0:T(8,128)(2,1)} %bitcast.48, bf16[4,4,64,512]{3,2,1,0:T(8,128)(2,1)S(1)} %bitcast.32, ...), custom_call_target="tpu_custom_call" | custom-call | flops 999999995904 | bytes 10000000000 | tf_op jit(solution)/shard_map/pallas_call | solution.py:253
  26.8 1.2 collective-permute-start.2
  28.0 0.8 collective-permute-start.3
  28.8 2.2 %shard_map.172.mine_ref = bf16[512,896]{1,0:T(8,128)(2,1)} custom-call(s32[1]{0:T(128)S(6)} %select_n.32.group_ref, bf16[4,3,64,1536]{3,2,1,0:T(8,128)(2,1)} %bitcast.49, bf16[4,4,64,512]{3,2,1,0:T(8,128)(2,1)S(1)} %bitcast.33, f32[4,64]{1,0:T(4,128)S(1)} %bitcast.43), custom_call_target="tpu_custom_call" | custom-call | tf_op jit(solution)/shard_map/pallas_call | solution.py:253
  31.4 17.4 %all-to-all-done = bf16[64,8,896]{2,1,0:T(8,128)(2,1)} async-done(((bf16[64,8,896]{2,1,0:T(8,128)(2,1)}), bf16[64,8,896]{2,1,0:T(8,128)(2,1)}, u32[]{:S(2)}, u32[]{:S(2)}) %all-to-all-start) | async-done | bytes 917536 | tf_op jit(solution)/shard_map/all_to_all | solution.py:598
  48.8 2.8 %shard_map.177.earlier_ref = bf16[512,896]{1,0:T(8,128)(2,1)S(1)} custom-call(bf16[512,896]{1,0:T(8,128)(2,1)} %bitcast.10.late_in_ref, bf16[2,4,64,64]{3,2,1,0:T(8,128)(2,1)S(1)} %get-tuple-element.40.table_ref), custom_call_target="tpu_custom_call" | custom-call | tf_op jit(solution)/shard_map/pallas_call | solution.py:138
  51.6 4.1 %shard_map.178 = (bf16[512,896]{1,0:T(8,128)(2,1)}, bf16[512,896]{1,0:T(8,128)(2,1)}) custom-call(bf16[512,896]{1,0:T(8,128)(2,1)S(1)} %copy-done, bf16[384,896]{1,0:T(8,128)(2,1)} %collective-permute-done.2.last_ref, bf16[384,896]{1,0:T(8,128)(2,1)} %collective-permute-done.3.next_ref, bf16[384,896]{1,0:T(8,128)(2,1)S(1)} %collective-permute-done.from_last.first_last, ...), custom_call_target="tpu_custom_call" | custom-call | tf_op jit(solution)/shard_map/pallas_call | solution.py:138
  55.7 5.8 %all-to-all-start.1 = ((bf16[64,8,896]{2,1,0:T(8,128)(2,1)}), bf16[64,8,896]{2,1,0:T(8,128)(2,1)S(1)}, u32[]{:S(2)}, u32[]{:S(2)}) async-start(bf16[64,8,896]{2,1,0:T(8,128)(2,1)} %bitcast.54), calls=%async_computation.1 | async-start | bytes 1835008 | tf_op jit(solution)/shard_map/all_to_all | solution.py:598
  61.5 2.6 %shard_map.179 = bf16[512,896]{1,0:T(8,128)(2,1)} custom-call(bf16[512,896]{1,0:T(8,128)(2,1)S(1)} %copy-done.1, bf16[2,4,64,64]{3,2,1,0:T(8,128)(2,1)S(1)} %get-tuple-element.40.table_ref), custom_call_target="tpu_custom_call" | custom-call | tf_op jit(solution)/shard_map/pallas_call | solution.py:138
  64.1 23.5 %all-to-all-done.1 = bf16[64,8,896]{2,1,0:T(8,128)(2,1)S(1)} async-done(((bf16[64,8,896]{2,1,0:T(8,128)(2,1)}), bf16[64,8,896]{2,1,0:T(8,128)(2,1)S(1)}, u32[]{:S(2)}, u32[]{:S(2)}) %all-to-all-start.1) | async-done | bytes 917536 | tf_op jit(solution)/shard_map/all_to_all | solution.py:598
  87.6 5.7 %all-to-all-start.2 = ((bf16[64,8,896]{2,1,0:T(8,128)(2,1)}), bf16[64,8,896]{2,1,0:T(8,128)(2,1)S(1)}, u32[]{:S(2)}, u32[]{:S(2)}) async-start(bf16[64,8,896]{2,1,0:T(8,128)(2,1)} %bitcast.51), calls=%async_computation.2 | async-start | bytes 1835008 | tf_op jit(solution)/shard_map/all_to_all | solution.py:598
  93.3 19.3 %shard_map.180 = (bf16[512,896]{1,0:T(8,128)(2,1)}, bf16[1,1,2,192,1536]{4,3,2,1,0:T(8,128)(2,1)}, bf16[1,1,2,256,512]{4,3,2,1,0:T(8,128)(2,1)}) custom-call(s32[1]{0:T(128)} %bitcast.node_ref, bf16[512,896]{1,0:T(8,128)(2,1)S(1)} %bitcast.34, bf16[1,1,2,192,1536]{4,3,2,1,0:T(8,128)(2,1)} %q_mom, bf16[1,1,2,256,512]{4,3,2,1,0:T(8,128)(2,1)} %kv_mom, ...), custom_call_target="tpu_custom_call" | custom-call | tf_op jit(solution)/shard_map/pallas_call | solution.py:138
  112.5 6.8 %all-to-all-done.2 = bf16[64,8,896]{2,1,0:T(8,128)(2,1)S(1)} async-done(((bf16[64,8,896]{2,1,0:T(8,128)(2,1)}), bf16[64,8,896]{2,1,0:T(8,128)(2,1)S(1)}, u32[]{:S(2)}, u32[]{:S(2)}) %all-to-all-start.2) | async-done | bytes 917536 | tf_op jit(solution)/shard_map/all_to_all | solution.py:598
  119.3 5.7 %all-to-all-start.3 = ((bf16[64,8,896]{2,1,0:T(8,128)(2,1)}), bf16[64,8,896]{2,1,0:T(8,128)(2,1)S(1)}, u32[]{:S(2)}, u32[]{:S(2)}) async-start(bf16[64,8,896]{2,1,0:T(8,128)(2,1)} %bitcast.53), calls=%async_computation.3 | async-start | bytes 1835008 | tf_op jit(solution)/shard_map/all_to_all | solution.py:598
  125.0 2.2 %shard_map.181 = (bf16[1,1,2,192,1536]{4,3,2,1,0:T(8,128)(2,1)}, bf16[1,1,2,256,512]{4,3,2,1,0:T(8,128)(2,1)}, f32[2,64,128]{2,1,0:T(8,128)S(1)}) custom-call(bf16[512,896]{1,0:T(8,128)(2,1)S(1)} %bitcast.37, bf16[512,896]{1,0:T(8,128)(2,1)S(1)} %bitcast.35, ...), custom_call_target="tpu_custom_call", output_to_operand_aliasing={{0}: (2, {}), {1}: (3, {})} | custom-call | tf_op jit(solution)/shard_map/pallas_call | solution.py:138
  127.5 23.6 %all-to-all-done.3 = bf16[64,8,896]{2,1,0:T(8,128)(2,1)S(1)} async-done(((bf16[64,8,896]{2,1,0:T(8,128)(2,1)}), bf16[64,8,896]{2,1,0:T(8,128)(2,1)S(1)}, u32[]{:S(2)}, u32[]{:S(2)}) %all-to-all-start.3) | async-done | bytes 917536 | tf_op jit(solution)/shard_map/all_to_all | solution.py:598
  151.1 3.9 %shard_map.182 = (bf16[4,3,16,1536]{3,2,1,0:T(8,128)(2,1)}, f32[4,3,16,1536]{3,2,1,0:T(8,128)}, bf16[4,64,512]{2,1,0:T(8,128)(2,1)S(1)}) custom-call(s32[1]{0:T(128)} %bitcast.node_ref, bf16[512,896]{1,0:T(8,128)(2,1)S(1)} %bitcast.36, bf16[2,4,64,64]{3,2,1,0:T(8,128)(2,1)S(1)} %get-tuple-element.40.table_ref, ...), custom_call_target="tpu_custom_call" | custom-call | tf_op jit(solution)/shard_map/pallas_call | solution.py:138
  155.0 1.3 subtract_multiply_fusion
  (27 shorter events, 1.5 us)
Async XLA Ops:
  0.6 1.5 copy-start.7
  0.6 1.5 copy-start.4
  5.2 17.6 %collective-permute-start = (bf16[384,896]{1,0:T(8,128)(2,1)}, bf16[384,896]{1,0:T(8,128)(2,1)S(1)}, u32[]{:S(2)}, u32[]{:S(2)}) collective-permute-start(bf16[384,896]{1,0:T(8,128)(2,1)} %get-tuple-element.34), channel_id=1, source_target_pairs={{0,64},{64,128},{128,192},{192,0},{1,65},{65,129},{129,193},{193,1... | collective-permute-start | bytes 2064392 | tf_op jit(solution)/shard_map/ppermute | solution.py:622
  6.7 16.9 %collective-permute-start.1 = (bf16[384,896]{1,0:T(8,128)(2,1)S(1)}, bf16[384,896]{1,0:T(8,128)(2,1)S(1)}, u32[]{:S(2)}, u32[]{:S(2)}) collective-permute-start(bf16[384,896]{1,0:T(8,128)(2,1)S(1)} %get-tuple-element.35), channel_id=1, source_target_pairs={{0,192},{64,0},{128,64},{192,128},{1,193},{65,1},{129,65},{193,129... | collective-permute-start | bytes 2064392 | tf_op jit(solution)/shard_map/ppermute | solution.py:623
  10.6 12.2 %copy-start.6 = (s32[2]{0:T(128)S(1)}, s32[2]{0:T(128)}, u32[]{:S(2)}) copy-start(s32[2]{0:T(128)} %constant.70.clone) | copy-start | bytes 28
  10.6 38.2 %all-to-all-start = ((bf16[64,8,896]{2,1,0:T(8,128)(2,1)}), bf16[64,8,896]{2,1,0:T(8,128)(2,1)}, u32[]{:S(2)}, u32[]{:S(2)}) async-start(bf16[64,8,896]{2,1,0:T(8,128)(2,1)} %bitcast.50), calls=%async_computation | async-start | bytes 1835008 | tf_op jit(solution)/shard_map/all_to_all | solution.py:598
  26.8 24.8 %collective-permute-start.2 = (bf16[384,896]{1,0:T(8,128)(2,1)}, bf16[384,896]{1,0:T(8,128)(2,1)}, u32[]{:S(2)}, u32[]{:S(2)}) collective-permute-start(bf16[384,896]{1,0:T(8,128)(2,1)} %get-tuple-element.36), channel_id=1, source_target_pairs={{0,64},{64,128},{128,192},{192,0},{1,65},{65,129},{129,193},{193,1... | collective-permute-start | bytes 2064392 | tf_op jit(solution)/shard_map/ppermute | solution.py:631
  28.0 23.6 %collective-permute-start.3 = (bf16[384,896]{1,0:T(8,128)(2,1)}, bf16[384,896]{1,0:T(8,128)(2,1)}, u32[]{:S(2)}, u32[]{:S(2)}) collective-permute-start(bf16[384,896]{1,0:T(8,128)(2,1)} %get-tuple-element.37), channel_id=1, source_target_pairs={{0,192},{64,0},{128,64},{192,128},{1,193},{65,1},{129,65},{193,129... | collective-permute-start | bytes 2064392 | tf_op jit(solution)/shard_map/ppermute | solution.py:632
  28.8 2.2 %copy-start.2 = (s32[4,4,16,1]{2,3,1,0:T(1,128)S(1)}, s32[4,4,16,1]{2,3,1,0:T(1,128)}, u32[]{:S(2)}) copy-start(s32[4,4,16,1]{2,3,1,0:T(1,128)} %param.19) | copy-start | bytes 3076
  28.8 2.2 %copy-start.3 = (s32[4,4,16,1]{2,3,1,0:T(1,128)S(1)}, s32[4,4,16,1]{2,3,1,0:T(1,128)}, u32[]{:S(2)}) copy-start(s32[4,4,16,1]{2,3,1,0:T(1,128)} %param.20) | copy-start | bytes 3076
  31.0 20.6 %copy-start = (bf16[512,896]{1,0:T(8,128)(2,1)S(1)}, bf16[512,896]{1,0:T(8,128)(2,1)}, u32[]{:S(2)}) copy-start(bf16[512,896]{1,0:T(8,128)(2,1)} %shard_map.172.mine_ref) | copy-start | bytes 2752516
  55.7 5.8 %copy-start.1 = (bf16[512,896]{1,0:T(8,128)(2,1)S(1)}, bf16[512,896]{1,0:T(8,128)(2,1)}, u32[]{:S(2)}) copy-start(bf16[512,896]{1,0:T(8,128)(2,1)} %get-tuple-element.43.carried_ref) | copy-start | bytes 2752516
  55.7 31.9 %all-to-all-start.1 = ((bf16[64,8,896]{2,1,0:T(8,128)(2,1)}), bf16[64,8,896]{2,1,0:T(8,128)(2,1)S(1)}, u32[]{:S(2)}, u32[]{:S(2)}) async-start(bf16[64,8,896]{2,1,0:T(8,128)(2,1)} %bitcast.54), calls=%async_computation.1 | async-start | bytes 1835008 | tf_op jit(solution)/shard_map/all_to_all | solution.py:598
  87.6 31.8 %all-to-all-start.2 = ((bf16[64,8,896]{2,1,0:T(8,128)(2,1)}), bf16[64,8,896]{2,1,0:T(8,128)(2,1)S(1)}, u32[]{:S(2)}, u32[]{:S(2)}) async-start(bf16[64,8,896]{2,1,0:T(8,128)(2,1)} %bitcast.51), calls=%async_computation.2 | async-start | bytes 1835008 | tf_op jit(solution)/shard_map/all_to_all | solution.py:598
  119.3 31.8 %all-to-all-start.3 = ((bf16[64,8,896]{2,1,0:T(8,128)(2,1)}), bf16[64,8,896]{2,1,0:T(8,128)(2,1)S(1)}, u32[]{:S(2)}, u32[]{:S(2)}) async-start(bf16[64,8,896]{2,1,0:T(8,128)(2,1)} %bitcast.53), calls=%async_computation.3 | async-start | bytes 1835008 | tf_op jit(solution)/shard_map/all_to_all | solution.py:598
  127.2 27.8 %copy-start.5 = (f32[4,16,4,512]{3,2,1,0:T(4,128)S(1)}, f32[4,16,4,512]{3,2,1,0:T(4,128)}, u32[]{:S(2)}) copy-start(f32[4,16,4,512]{3,2,1,0:T(4,128)} %param.18) | copy-start | bytes 1572868

commit v4 on v3

--- a/solution.py
+++ b/solution.py
@@ -29,6 +29,8 @@
 EXTRA = ROWS // 4
 RING = ROWS - EXTRA
 PEAK_TILE = Q_OWN * Q_TILES + KV_OWN * KV_TILES
+LATE_MSG = MSG - LANE
+REST = KV_TILES
 SPLIT = Q_OWN * Q_TILES // SUB
 SPLIT_SUB = Q_OWN * Q_TILES % SUB
 
@@ -140,6 +142,9 @@
 
 def whole(*dims):
     return pl.BlockSpec(dims, lambda i: (0,) * len(dims))
+
+
+HERE = pl.BlockSpec(memory_space=pltpu.VMEM)
 
 
 def shape(dims, dtype):
@@ -256,8 +261,8 @@
         grid_spec=pltpu.PrefetchScalarGridSpec(
             num_scalar_prefetch=1,
             grid=(1,),
-            in_specs=sum([at(index) for index in range(count)], []) + [all_of(x) for x in (peaks, *extra)],
-            out_specs=[all_of(x) for x in out_shape],
+            in_specs=sum([at(index) for index in range(count)], []) + [all_of(peaks)] + [HERE] * len(extra),
+            out_specs=[all_of(x) if hint is None and count == 1 else HERE for x in out_shape],
         ),
         compiler_params=PARAMS,
         cost_estimate=hint,
@@ -332,6 +337,17 @@
     return jnp.where((row >> 6) == (col & 7), wide, 0.0).astype(BF16)
 
 
+def expand_kernel(table_ref, send_ref, late_back_ref, back_ref):
+    for kind in range(2):
+        send_ref[kind] = to_peers(table_ref[kind, SEND])
+        late_back_ref[kind] = to_tiles(table_ref[kind, LATE_BACK])
+        back_ref[kind] = to_tiles(table_ref[kind, SEND_BACK])
+
+
+def expand(table):
+    return call(expand_kernel, (pltpu.HBM((2, ROWS, ROWS), BF16),) * 3, table)
+
+
 def late_kernel(q_ref, kv_ref, out_ref, tiles_ref):
     out_ref[...] = to_message(q_ref[0, 0, 0], kv_ref[0, 0, 0], tiles_ref).astype(BF16)
 
@@ -352,14 +368,13 @@
     )
 
 
-def earlier_kernel(late_in_ref, table_ref, out_ref):
+def earlier_kernel(late_in_ref, matrix_ref, out_ref):
     tile_rows = iota((ROWS, LANE), 0) < SPLIT_SUB * BLOCKS
-    q_matrix, kv_matrix = to_tiles(table_ref[0, LATE_BACK]), to_tiles(table_ref[1, LATE_BACK])
-    out_ref[...] = by_kind(q_matrix, kv_matrix, late_in_ref[...], tile_rows).astype(BF16)
+    out_ref[...] = by_kind(matrix_ref[0], matrix_ref[1], late_in_ref[...], tile_rows).astype(BF16)
 
 
 def send_kernel(
-    mine_ref, last_ref, next_ref, first_last, first_next, earlier_ref, table_ref, over_ref, out_hbm, carried_hbm,
+    mine_ref, last_ref, next_ref, first_last, first_next, earlier_ref, matrix_ref, over_ref, out_hbm, carried_hbm,
     chosen, carried, message, sems,
 ):
     row = iota((ROWS, LANE), 0)
@@ -367,8 +382,8 @@
     kv_over = jnp.concatenate([over_ref[1]] * SUB, axis=0)
     for col in range(MSG_COLS):
         lanes = slice(col * LANE, (col + 1) * LANE)
-        last = jnp.concatenate([last_ref[:, lanes], first_last[HALF:, lanes]], axis=0).astype(F32)
-        following = jnp.concatenate([first_next[HALF:, lanes], next_ref[:, lanes]], axis=0).astype(F32)
+        last = jnp.concatenate([last_ref[:, lanes], first_last[:, lanes]], axis=0).astype(F32)
+        following = jnp.concatenate([first_next[:, lanes], next_ref[:, lanes]], axis=0).astype(F32)
         reduced = mine_ref[:, lanes].astype(F32) + (last + following)
         reduced = reduced.astype(BF16).astype(F32)
         moved = MOMENTUM_RATE * earlier_ref[:, lanes].astype(F32) + reduced
@@ -383,11 +398,11 @@
     carried_copy = pltpu.make_async_copy(carried, carried_hbm, sems.at[0])
     carried_copy.start()
     edge = SPLIT * LANE
-    q_part = dot(to_peers(table_ref[0, SEND]), chosen[:, : edge + LANE])
+    q_part = dot(matrix_ref[0], chosen[:, : edge + LANE])
     message[:, :edge] = q_part[:, :edge].astype(BF16)
     q_copy = pltpu.make_async_copy(message.at[:, :edge], out_hbm.at[:, :edge], sems.at[1])
     q_copy.start()
-    kv_part = dot(to_peers(table_ref[1, SEND]), chosen[:, edge:])
+    kv_part = dot(matrix_ref[1], chosen[:, edge:])
     peer_rows = (row & 7) < SPLIT_SUB
     message[:, edge : edge + LANE] = jnp.where(peer_rows, q_part[:, edge:], kv_part[:, :LANE]).astype(BF16)
     rows, cols = place(PEAK_TILE)
@@ -410,10 +425,13 @@
     kv_copy.wait()
 
 
-def late_out_kernel(carried_ref, table_ref, out_ref):
-    peer_rows = (iota((ROWS, LANE), 0) & 7) < SPLIT_SUB
+def late_out_kernel(carried_ref, table_ref, out_ref, rest_ref):
+    row = iota((ROWS, LANE), 0)
     q_matrix, kv_matrix = to_peers(table_ref[0, LATE]), to_peers(table_ref[1, LATE])
-    out_ref[...] = by_kind(q_matrix, kv_matrix, carried_ref[...], peer_rows).astype(BF16)
+    placed = by_kind(q_matrix, kv_matrix, carried_ref[...], (row & 7) < SPLIT_SUB)
+    out_ref[...] = placed[:, :LATE_MSG].astype(BF16)
+    moved = pltpu.roll(placed[:, LATE_MSG:], REST, 0)
+    rest_ref[...] = jnp.where((row & 7) >= REST, moved, 0.0).astype(BF16)
 
 
 def halves(x):
@@ -422,20 +440,25 @@
 
 
 def product(a, b, op):
-    return op(a[0], b[0]) + (op(a[0], b[1]) + op(a[1], b[0]))
-
-
-def newton_step(x_ref):
-    x = x_ref[...]
-    parts = halves(x)
-    square = product(parts, parts, dot_nt)
-    square_parts = halves(square)
-    polynomial = NEWTON_SECOND * square + NEWTON_THIRD * product(square_parts, square_parts, dot)
-    x_ref[...] = NEWTON_FIRST * x + product(halves(polynomial), parts, dot)
+    size = a[0].shape[0]
+    both = op(jnp.concatenate(a, axis=0), b[0])
+    return both[:size] + (both[size:] + op(a[0], b[1]))
+
+
+def newton_step(refs):
+    values = [ref[...] for ref in refs]
+    parts = [halves(x) for x in values]
+    squares = [product(h, h, dot_nt) for h in parts]
+    square_parts = [halves(square) for square in squares]
+    polynomials = [
+        NEWTON_SECOND * square + NEWTON_THIRD * product(h, h, dot) for square, h in zip(squares, square_parts)
+    ]
+    for ref, x, h, polynomial in zip(refs, values, parts, polynomials):
+        ref[...] = NEWTON_FIRST * x + product(halves(polynomial), h, dot)
 
 
 def owner_kernel(
-    node_ref, in_ref, q_mom, kv_mom, fill_ref, out_ref, q_new, kv_new, q_x, kv_x, q_half, kv_half, tiles_ref
+    node_ref, in_ref, q_mom, kv_mom, fill_ref, rest_ref, out_ref, q_new, kv_new, q_x, kv_x, q_half, kv_half, tiles_ref
 ):
     node = node_ref[0]
     received = dot(unpack_matrix(), in_ref[...])
@@ -452,16 +475,16 @@
         x_ref[...] = direction / norm
 
     def body(_, carry):
-        newton_step(q_x)
-        newton_step(kv_x)
+        newton_step((q_x, kv_x))
         return carry
 
     lax.fori_loop(0, STEPS, body, 0)
     outgoing = to_message((q_x[...] * Q_SCALE).astype(BF16), (kv_x[...] * KV_SCALE).astype(BF16), tiles_ref)
-    out_ref[...] = outgoing.astype(BF16)
-
-
-def owner_step(node, arrived, momentum_query, momentum_kv, fill):
+    out_ref[:, :LATE_MSG] = outgoing[:, :LATE_MSG].astype(BF16)
+    out_ref[:, LATE_MSG:] = (outgoing[:, LATE_MSG:] + rest_ref[...].astype(F32)).astype(BF16)
+
+
+def owner_step(node, arrived, momentum_query, momentum_kv, fill, rest):
     q_slot = pl.BlockSpec((1, 1, 1, Q_ROWS, Q_COLS), lambda i: (0, 0, 0, 0, 0))
     kv_slot = pl.BlockSpec((1, 1, 1, KV_ROWS, KV_COLS), lambda i: (0, 0, 0, 0, 0))
     return call(
@@ -476,8 +499,9 @@
         in_hbm(momentum_query),
         in_hbm(momentum_kv),
         fill,
+        in_hbm(rest),
         grid=(1,),
-        in_specs=[pl.BlockSpec(memory_space=pltpu.SMEM), whole(ROWS, MSG), q_slot, kv_slot, whole(2, NODES, LANE)],
+        in_specs=[pl.BlockSpec(memory_space=pltpu.SMEM), HERE, q_slot, kv_slot, whole(2, NODES, LANE), whole(ROWS, LANE)],
         out_specs=[whole(ROWS, MSG), q_slot, kv_slot],
         scratch_shapes=[
             pltpu.VMEM((Q_ROWS, Q_COLS), F32),
@@ -489,12 +513,19 @@
     )
 
 
-def settle_kernel(in_ref, arrived_ref, q_old, kv_old, q_new, kv_new, factor_ref, q_half, kv_half):
+def settle_kernel(in_ref, arrived_ref, q_old, q_new, kv_part, factor_ref, q_half, kv_half):
     matrix = unpack_matrix()
     late = dot(matrix, in_ref[...]).astype(BF16)
-    q_late, kv_late = from_tiles(late, q_half, kv_half)
-    q_new[0, 0, 0] = q_late.astype(BF16)
-    kv_new[0, 0, 0] = kv_late.astype(BF16)
+    for kind, half in (("q", q_half), ("kv", kv_half)):
+        for r, ct, tile in tiles_of(kind):
+            rows, cols = place(tile)
+            here = slice(r * NODES, (r + 1) * NODES), slice(ct * LANE, (ct + 1) * LANE)
+            if cols.start < LATE_MSG:
+                half[here] = late[rows, cols]
+            else:
+                half[here] = jnp.zeros((NODES, LANE), BF16)
+    q_new[0, 0, 0] = dot(natural_matrix(Q_OWN), q_half[...]).astype(BF16)
+    kv_part[...] = dot(natural_matrix(KV_OWN), kv_half[...]).astype(BF16)
 
     rows, cols = place(PEAK_TILE)
     parts = dot(matrix, arrived_ref[:, cols])
@@ -507,44 +538,39 @@
     factor_ref[1] = jnp.broadcast_to(shrink, (BLOCKS, LANE))
 
 
-def settle(late, arrived, q_momentum, kv_momentum):
-    anywhere = pl.BlockSpec(memory_space=pl.ANY)
+def settle(late, arrived, q_momentum):
     return call(
         settle_kernel,
         (
             shape((1, 1, 2, Q_ROWS, Q_COLS), BF16),
-            shape((1, 1, 2, KV_ROWS, KV_COLS), BF16),
+            pltpu.HBM((KV_ROWS, KV_COLS), BF16),
             shape((2, BLOCKS, LANE), F32),
         ),
         late,
         arrived,
         q_momentum,
-        kv_momentum,
         grid=(1,),
-        in_specs=[whole(ROWS, MSG), whole(ROWS, MSG), anywhere, anywhere],
+        in_specs=[HERE, whole(ROWS, MSG), pl.BlockSpec(memory_space=pl.ANY)],
         out_specs=[
             pl.BlockSpec((1, 1, 1, Q_ROWS, Q_COLS), lambda i: (0, 0, 1, 0, 0)),
-            pl.BlockSpec((1, 1, 1, KV_ROWS, KV_COLS), lambda i: (0, 0, 1, 0, 0)),
+            whole(KV_ROWS, KV_COLS),
             whole(2, BLOCKS, LANE),
         ],
         scratch_shapes=[pltpu.VMEM((Q_ROWS, Q_COLS), BF16), pltpu.VMEM((KV_ROWS, KV_COLS), BF16)],
-        input_output_aliases={2: 0, 3: 1},
+        input_output_aliases={2: 0},
     )
 
 
 def finish_kernel(
-    node_ref, in_ref, table_ref, factor_ref, weight_hbm, update_hbm, weight_new_hbm, kv_update_ref,
-    weight, update, sems,
+    node_ref, in_ref, matrix_ref, factor_ref, weight_hbm, part_hbm, kv_old, update_hbm, weight_new_hbm, kv_update_ref,
+    kv_new_hbm, weight, update, part, kv_new, sems,
 ):
     fetch = pltpu.make_async_copy(weight_hbm, weight, sems.at[0])
     fetch.start()
+    part_fetch = pltpu.make_async_copy(part_hbm, part, sems.at[1])
+    part_fetch.start()
     edge = SPLIT * LANE
-    kv_rows = dot(to_tiles(table_ref[1, SEND_BACK]), in_ref[:, edge:])
-    for r, ct, tile in tiles_of("kv"):
-        rows, cols = place(tile)
-        lanes = slice(cols.start - edge, cols.stop - edge)
-        kv_update_ref[r, :, ct * LANE : (ct + 1) * LANE] = kv_rows[rows, lanes].astype(BF16)
-    q_rows = dot(to_tiles(table_ref[0, SEND_BACK]), in_ref[:, : edge + LANE])
+    q_rows = dot(matrix_ref[0], in_ref[:, : edge + LANE])
     fetch.wait()
     copies = []
     for r in range(Q_OWN):
@@ -557,39 +583,65 @@
             update[:, r, :, lanes] = step.astype(BF16)
             old = weight[:, r, :, lanes]
             weight[:, r, :, lanes] = (old - LEARN_RATE * (step + DECAY_RATE * old)) * factor
-        copies.append(pltpu.make_async_copy(update.at[:, r], update_hbm.at[:, r], sems.at[1 + 2 * r]))
-        copies.append(pltpu.make_async_copy(weight.at[:, r], weight_new_hbm.at[:, r], sems.at[2 + 2 * r]))
+        copies.append(pltpu.make_async_copy(update.at[:, r], update_hbm.at[:, r], sems.at[2 + 2 * r]))
+        copies.append(pltpu.make_async_copy(weight.at[:, r], weight_new_hbm.at[:, r], sems.at[3 + 2 * r]))
         copies[-2].start()
         copies[-1].start()
+    row, col = iota((KV_TILES * NODES, ROWS), 0), iota((KV_TILES * NODES, ROWS), 1)
+    rest_matrix = one(((row & 63) == (col >> 3)) & ((row >> 6) + REST == (col & 7)))
+    rest = dot(rest_matrix, in_ref[:, LATE_MSG:]).astype(BF16)
+    rest = jnp.concatenate([rest[ct * NODES : (ct + 1) * NODES] for ct in range(KV_TILES)], axis=1)
+    spread = one(iota((KV_ROWS, NODES), 0) == iota((KV_ROWS, NODES), 1) * KV_OWN + (KV_OWN - 1))
+    part_fetch.wait()
+    kv_new[...] = (part[...].astype(F32) + dot(spread, rest)).astype(BF16)
+    copies.append(pltpu.make_async_copy(kv_new, kv_new_hbm.at[0, 0, 1], sems.at[2 + 2 * Q_OWN]))
+    copies[-1].start()
+    kv_rows = dot(matrix_ref[1], in_ref[:, edge:])
+    for r, ct, tile in tiles_of("kv"):
+        rows, cols = place(tile)
+        lanes = slice(cols.start - edge, cols.stop - edge)
+        kv_update_ref[r, :, ct * LANE : (ct + 1) * LANE] = kv_rows[rows, lanes].astype(BF16)
     for copy in copies:
         copy.wait()
 
 
-def finish(node, returned, table, factors, weight_query):
+def finish(node, returned, matrix, factors, weight_query, kv_part, kv_momentum):
     q_dims = (LAYERS, Q_OWN, PER_GROUP, Q_COLS)
     kv_dims = (KV_OWN, BLOCKS, KV_COLS)
     outside = pl.BlockSpec(memory_space=pltpu.HBM)
     return call(
         finish_kernel,
-        (pltpu.HBM(q_dims, BF16), pltpu.HBM(q_dims, F32), shape(kv_dims, BF16)),
+        (
+            pltpu.HBM(q_dims, BF16),
+            pltpu.HBM(q_dims, F32),
+            shape(kv_dims, BF16),
+            pltpu.HBM((1, 1, 2, KV_ROWS, KV_COLS), BF16),
+        ),
         node,
         returned,
-        table,
+        in_hbm(matrix),
         factors,
         in_hbm(weight_query),
+        in_hbm(kv_part),
+        in_hbm(kv_momentum),
         grid=(1,),
         in_specs=[
             pl.BlockSpec(memory_space=pltpu.SMEM),
-            whole(ROWS, MSG),
-            whole(2, 4, NODES, BLOCKS),
+            HERE,
+            whole(2, ROWS, ROWS),
             whole(2, BLOCKS, LANE),
             outside,
+            outside,
+            outside,
         ],
-        out_specs=[outside, outside, whole(*kv_dims)],
+        out_specs=[outside, outside, HERE, outside],
+        input_output_aliases={6: 3},
         scratch_shapes=[
             pltpu.VMEM(q_dims, F32),
             pltpu.VMEM(q_dims, BF16),
-            pltpu.SemaphoreType.DMA((1 + 2 * Q_OWN,)),
+            pltpu.VMEM((KV_ROWS, KV_COLS), BF16),
+            pltpu.VMEM((KV_ROWS, KV_COLS), BF16),
+            pltpu.SemaphoreType.DMA((3 + 2 * Q_OWN,)),
         ],
     )
 
@@ -623,6 +675,7 @@
     from_next = lax.ppermute(to_last, "dp", backward)
     late_in = exchange(late_message(momentum_query, momentum_kv))
     table, over, fill = tables(turn(0), owner_query, owner_kv)
+    send_matrix, late_back, back_matrix = expand(table)
     hint = pl.CostEstimate(flops=10**12, bytes_accessed=10**10, transcendentals=0)
     to_next, to_last = arrange_call(
         combine_kernel, turn(1, 3), q_grads, kv_grads, peaks, (from_last, from_next),
@@ -631,28 +684,30 @@
     sum_last = lax.ppermute(to_next, "dp", forward)
     sum_next = lax.ppermute(to_last, "dp", backward)
     (mine,) = arrange_call(mine_kernel, turn(0), q_grads, kv_grads, peaks, (), (pltpu.HBM((ROWS, MSG), BF16),))
-    earlier = call(earlier_kernel, shape((ROWS, MSG), BF16), late_in, table)
+    earlier = call(earlier_kernel, shape((ROWS, MSG), BF16), in_hbm(late_in), in_hbm(late_back))
 
     outside = pl.BlockSpec(memory_space=pltpu.HBM)
     message, carried = call(
         send_kernel,
         (pltpu.HBM((ROWS, MSG), BF16), pltpu.HBM((ROWS, MSG), BF16)),
-        mine, sum_last, sum_next, from_last, from_next, earlier, table, over,
+        mine, sum_last, sum_next, from_last, from_next, earlier, in_hbm(send_matrix), over,
         grid=(1,),
-        in_specs=[whole(ROWS, MSG)] + [whole(RING, MSG)] * 4 + [whole(ROWS, MSG)]
-        + [whole(2, 4, NODES, BLOCKS), whole(2, BLOCKS, LANE)],
+        in_specs=[whole(ROWS, MSG), HERE, HERE] + [pl.BlockSpec((EXTRA, MSG), lambda i: (2, 0))] * 2 + [HERE]
+        + [whole(2, ROWS, ROWS), whole(2, BLOCKS, LANE)],
         out_specs=[outside, outside],
         scratch_shapes=[pltpu.VMEM((ROWS, MSG), BF16)] * 3 + [pltpu.SemaphoreType.DMA((3,))],
     )
-    late_out = call(late_out_kernel, pltpu.HBM((ROWS, MSG), BF16), carried, table)
+    late_out, rest = call(
+        late_out_kernel, (pltpu.HBM((ROWS, LATE_MSG), BF16), pltpu.HBM((ROWS, LANE), BF16)), carried, table
+    )
     arrived, late_out = lax.optimization_barrier((exchange(message), late_out))
     late = exchange(late_out)
-    outgoing, q_momentum, kv_momentum = owner_step(node, arrived, momentum_query, momentum_kv, fill)
+    outgoing, q_momentum, kv_momentum = owner_step(node, arrived, momentum_query, momentum_kv, fill, rest)
     late, outgoing = lax.optimization_barrier((late, outgoing))
     returned = exchange(outgoing)
-    q_momentum, kv_momentum, factors = settle(late, arrived, q_momentum, kv_momentum)
-    q_update, q_weight, kv_update = finish(
-        node, returned, table, factors, jnp.transpose(weight_query, (0, 2, 1, 3))
+    q_momentum, kv_part, factors = settle(late, arrived, q_momentum)
+    q_update, q_weight, kv_update, kv_momentum = finish(
+        node, returned, back_matrix, factors, jnp.transpose(weight_query, (0, 2, 1, 3)), kv_part, kv_momentum
     )
     kv_update = jnp.transpose(kv_update.reshape(KV_OWN, LAYERS, PER_GROUP, KV_COLS), (1, 2, 0, 3))
     kv_index = my_node * KV_OWN + jnp.arange(KV_OWN, dtype=I32)

time: 158 us -> 156 us (0.987)
  Pallas kernels: 46.6 us -> 45 us
    pallas_call x8 -> x9, Pallas kernels: 38.2 us -> 36.6 us  [call(): pl.pallas_call(kernel, out_shape=out_shape, compiler_params=PARAMS, **opt...]
  transfers between devices with their start and end apart: 8 -> 8, of which waited for: 5 -> 5; matrix products, arithmetic and copies ran while one was open for 0% -> 0% of each run, Pallas kernels for 23% -> 22%
where the time goes in v4:
time: 156 us; the launch traced here: 153 us
  waiting for transfers between devices  70.7 us (45%)
  Pallas kernels  45 us (29%)
  starting transfers between devices  33.9 us (22%)
  local copies, waits for them, and re-layouts  1.66 us (1%)
    all_to_all x4, waiting for transfers between devices, exchange(): lax.all_to_all(message, 'fsdp', split_axis=0, concat_axis=0, tiled=True)  69.9 us
    pallas_call x9, Pallas kernels, call(): pl.pallas_call(kernel, out_shape=out_shape, compiler_params=PARAMS, **opt...  36.6 us
    all_to_all x4, starting transfers between devices, exchange(): lax.all_to_all(message, 'fsdp', split_axis=0, concat_axis=0, tiled=True)  29.6 us
    pallas_call x3, Pallas kernels, arrange_call(): pl.pallas_call(kernel, out_shape=out_shape, grid_spec=pltpu.PrefetchScala...  8.43 us
  transfers between devices with their start and end apart: 8, of which 5 were waited for; matrix products, arithmetic and copies ran while one was open for 0% of the time, Pallas kernels for 22%

profile of v4, /device:TPU:2, one launch (start us, length us, event | category | flops | bytes accessed | tf_op | source)
XLA Modules:
  0.0 153.5 jit_solution(16543321386315517238)
XLA Ops:
  0.7 1.4 copy.28
  2.1 3.1 %shard_map.173 = (bf16[384,896]{1,0:T(8,128)(2,1)}, bf16[384,896]{1,0:T(8,128)(2,1)S(1)}) custom-call(s32[3]{0:T(128)S(1)} %and_select_fusion.group_ref, bf16[4,3,64,1536]{3,2,1,0:T(8,128)(2,1)} %bitcast.44, bf16[4,4,64,512]{3,2,1,0:T(8,128)(2,1)S(1)} %bitcast.28, bf16[4,3,64,1536]{3,2,1,0:T(8,128)(2,1)} %bitcast.45, bf16[4,4,64,512]{3,2,1,0:T(8,128)(2,1)S(1)} %bitcast.29, ...), custom_call_target="tpu_custom_call" | custom-call | tf_op jit(solution)/shard_map/pallas_call | solution.py:258
  5.2 1.5 collective-permute-start
  7.5 3.1 %shard_map.175 = bf16[512,896]{1,0:T(8,128)(2,1)} custom-call(bf16[1,1,2,192,1536]{4,3,2,1,0:T(8,128)(2,1)} %q_mom, bf16[1,1,2,256,512]{4,3,2,1,0:T(8,128)(2,1)} %kv_mom), custom_call_target="tpu_custom_call" | custom-call | tf_op jit(solution)/shard_map/pallas_call | solution.py:140
  10.6 12.2 %all-to-all-start = ((bf16[64,8,896]{2,1,0:T(8,128)(2,1)}), bf16[64,8,896]{2,1,0:T(8,128)(2,1)}, u32[]{:S(2)}, u32[]{:S(2)}) async-start(bf16[64,8,896]{2,1,0:T(8,128)(2,1)} %bitcast.50), calls=%async_computation | async-start | bytes 1835008 | tf_op jit(solution)/shard_map/all_to_all | solution.py:650
  23.6 3.2 %shard_map.174 = (bf16[384,896]{1,0:T(8,128)(2,1)}, bf16[384,896]{1,0:T(8,128)(2,1)}) custom-call(s32[2]{0:T(128)S(1)} %and_select_fusion.1.group_ref, bf16[4,3,64,1536]{3,2,1,0:T(8,128)(2,1)} %bitcast.47, bf16[4,4,64,512]{3,2,1,0:T(8,128)(2,1)S(1)} %bitcast.31, bf16[4,3,64,1536]{3,2,1,0:T(8,128)(2,1)} %bitcast.48, bf16[4,4,64,512]{3,2,1,0:T(8,128)(2,1)S(1)} %bitcast.32, ...), custom_call_target="tpu_custom_call" | custom-call | flops 999999995904 | bytes 10000000000 | tf_op jit(solution)/shard_map/pallas_call | solution.py:258
  26.8 1.2 collective-permute-start.2
  28.0 0.8 collective-permute-start.3
  28.8 2.2 %shard_map.172.mine_ref = bf16[512,896]{1,0:T(8,128)(2,1)} custom-call(s32[1]{0:T(128)S(6)} %select_n.32.group_ref, bf16[4,3,64,1536]{3,2,1,0:T(8,128)(2,1)} %bitcast.49, bf16[4,4,64,512]{3,2,1,0:T(8,128)(2,1)S(1)} %bitcast.33, f32[4,64]{1,0:T(4,128)S(1)} %bitcast.43), custom_call_target="tpu_custom_call" | custom-call | tf_op jit(solution)/shard_map/pallas_call | solution.py:258
  31.4 2.9 %shard_map.177 = (bf16[2,512,512]{2,1,0:T(8,128)(2,1)}, bf16[2,512,512]{2,1,0:T(8,128)(2,1)}, bf16[2,512,512]{2,1,0:T(8,128)(2,1)}) custom-call(bf16[2,4,64,64]{3,2,1,0:T(8,128)(2,1)S(1)} %get-tuple-element.46.table_ref), custom_call_target="tpu_custom_call" | custom-call | tf_op jit(solution)/shard_map/pallas_call | solution.py:140
  34.4 14.4 %all-to-all-done = bf16[64,8,896]{2,1,0:T(8,128)(2,1)} async-done(((bf16[64,8,896]{2,1,0:T(8,128)(2,1)}), bf16[64,8,896]{2,1,0:T(8,128)(2,1)}, u32[]{:S(2)}, u32[]{:S(2)}) %all-to-all-start) | async-done | bytes 917536 | tf_op jit(solution)/shard_map/all_to_all | solution.py:650
  48.8 2.4 %shard_map.178.earlier_ref = bf16[512,896]{1,0:T(8,128)(2,1)S(1)} custom-call(bf16[512,896]{1,0:T(8,128)(2,1)} %bitcast.10.late_in_ref, bf16[2,512,512]{2,1,0:T(8,128)(2,1)} %get-tuple-element.47.matrix_ref), custom_call_target="tpu_custom_call" | custom-call | tf_op jit(solution)/shard_map/pallas_call | solution.py:140
  51.2 3.9 %shard_map.179 = (bf16[512,896]{1,0:T(8,128)(2,1)}, bf16[512,896]{1,0:T(8,128)(2,1)}) custom-call(bf16[512,896]{1,0:T(8,128)(2,1)S(1)} %copy-done, bf16[384,896]{1,0:T(8,128)(2,1)S(1)} %collective-permute-done.2.last_ref, bf16[384,896]{1,0:T(8,128)(2,1)} %collective-permute-done.3.next_ref, bf16[384,896]{1,0:T(8,128)(2,1)S(1)} %collective-permute-done.from_last.first_last, ...), custom_call_target="tpu_custom_call" | custom-call | tf_op jit(solution)/shard_map/pallas_call | solution.py:140
  55.1 5.8 %all-to-all-start.1 = ((bf16[64,8,896]{2,1,0:T(8,128)(2,1)}), bf16[64,8,896]{2,1,0:T(8,128)(2,1)S(1)}, u32[]{:S(2)}, u32[]{:S(2)}) async-start(bf16[64,8,896]{2,1,0:T(8,128)(2,1)} %bitcast.53), calls=%async_computation.1 | async-start | bytes 1835008 | tf_op jit(solution)/shard_map/all_to_all | solution.py:650
  60.9 2.3 %shard_map.180 = (bf16[512,768]{1,0:T(8,128)(2,1)}, bf16[512,128]{1,0:T(8,128)(2,1)}) custom-call(bf16[512,896]{1,0:T(8,128)(2,1)S(1)} %copy-done.1, bf16[2,4,64,64]{3,2,1,0:T(8,128)(2,1)S(1)} %get-tuple-element.46.table_ref), custom_call_target="tpu_custom_call" | custom-call | tf_op jit(solution)/shard_map/pallas_call | solution.py:140
  63.2 23.8 %all-to-all-done.1 = bf16[64,8,896]{2,1,0:T(8,128)(2,1)S(1)} async-done(((bf16[64,8,896]{2,1,0:T(8,128)(2,1)}), bf16[64,8,896]{2,1,0:T(8,128)(2,1)S(1)}, u32[]{:S(2)}, u32[]{:S(2)}) %all-to-all-start.1) | async-done | bytes 917536 | tf_op jit(solution)/shard_map/all_to_all | solution.py:650
  87.0 5.9 %all-to-all-start.2 = ((bf16[64,8,768]{2,1,0:T(8,128)(2,1)}), bf16[64,8,768]{2,1,0:T(8,128)(2,1)S(1)}, u32[]{:S(2)}, u32[]{:S(2)}) async-start(bf16[64,8,768]{2,1,0:T(8,128)(2,1)} %bitcast.54), calls=%async_computation.2 | async-start | bytes 1572864 | tf_op jit(solution)/shard_map/all_to_all | solution.py:650
  92.9 15.5 %shard_map.181 = (bf16[512,896]{1,0:T(8,128)(2,1)}, bf16[1,1,2,192,1536]{4,3,2,1,0:T(8,128)(2,1)}, bf16[1,1,2,256,512]{4,3,2,1,0:T(8,128)(2,1)}) custom-call(s32[1]{0:T(128)} %bitcast.node_ref, bf16[512,896]{1,0:T(8,128)(2,1)S(1)} %bitcast.34, bf16[1,1,2,192,1536]{4,3,2,1,0:T(8,128)(2,1)} %q_mom, bf16[1,1,2,256,512]{4,3,2,1,0:T(8,128)(2,1)} %kv_mom, ...), custom_call_target="tpu_custom_call" | custom-call | tf_op jit(solution)/shard_map/pallas_call | solution.py:140
  108.4 7.7 %all-to-all-done.2 = bf16[64,8,768]{2,1,0:T(8,128)(2,1)S(1)} async-done(((bf16[64,8,768]{2,1,0:T(8,128)(2,1)}), bf16[64,8,768]{2,1,0:T(8,128)(2,1)S(1)}, u32[]{:S(2)}, u32[]{:S(2)}) %all-to-all-start.2) | async-done | bytes 786464 | tf_op jit(solution)/shard_map/all_to_all | solution.py:650
  116.2 5.7 %all-to-all-start.3 = ((bf16[64,8,896]{2,1,0:T(8,128)(2,1)}), bf16[64,8,896]{2,1,0:T(8,128)(2,1)S(1)}, u32[]{:S(2)}, u32[]{:S(2)}) async-start(bf16[64,8,896]{2,1,0:T(8,128)(2,1)} %bitcast.52), calls=%async_computation.3 | async-start | bytes 1835008 | tf_op jit(solution)/shard_map/all_to_all | solution.py:650
  121.9 1.8 %shard_map.182 = (bf16[1,1,2,192,1536]{4,3,2,1,0:T(8,128)(2,1)}, bf16[256,512]{1,0:T(8,128)(2,1)}, f32[2,64,128]{2,1,0:T(8,128)S(1)}) custom-call(bf16[512,768]{1,0:T(8,128)(2,1)S(1)} %bitcast.37, bf16[512,896]{1,0:T(8,128)(2,1)S(1)} %bitcast.35, bf16[1,1,2,192,1536]{4,3,2,1,0:T(8,128)(2,1)} %get-tuple-element.61.q_old), custom_call_target="tpu_custom_call", output_to_operand_aliasing={{0}: (2, {})} | custom-call | tf_op jit(solution)/shard_map/pallas_call | solution.py:140
  124.0 24.0 %all-to-all-done.3 = bf16[64,8,896]{2,1,0:T(8,128)(2,1)S(1)} async-done(((bf16[64,8,896]{2,1,0:T(8,128)(2,1)}), bf16[64,8,896]{2,1,0:T(8,128)(2,1)S(1)}, u32[]{:S(2)}, u32[]{:S(2)}) %all-to-all-start.3) | async-done | bytes 917536 | tf_op jit(solution)/shard_map/all_to_all | solution.py:650
  148.0 4.2 %shard_map.183 = (bf16[4,3,16,1536]{3,2,1,0:T(8,128)(2,1)}, f32[4,3,16,1536]{3,2,1,0:T(8,128)}, bf16[4,64,512]{2,1,0:T(8,128)(2,1)S(1)}, bf16[1,1,2,256,512]{4,3,2,1,0:T(8,128)(2,1)}) custom-call(s32[1]{0:T(128)} %bitcast.node_ref, bf16[512,896]{1,0:T(8,128)(2,1)S(1)} %bitcast.36, ...), custom_call_target="tpu_custom_call", output_to_operand_aliasing={{3}: (6, {})} | custom-call | tf_op jit(solution)/shard_map/pallas_call | solution.py:140
  152.2 1.3 subtract_multiply_fusion
  (28 shorter events, 2.3 us)
Async XLA Ops:
  0.6 1.5 copy-start.7
  0.6 1.5 copy-start.4
  5.2 17.6 %collective-permute-start = (bf16[384,896]{1,0:T(8,128)(2,1)}, bf16[384,896]{1,0:T(8,128)(2,1)S(1)}, u32[]{:S(2)}, u32[]{:S(2)}) collective-permute-start(bf16[384,896]{1,0:T(8,128)(2,1)} %get-tuple-element.40), channel_id=1, source_target_pairs={{0,64},{64,128},{128,192},{192,0},{1,65},{65,129},{129,193},{193,1... | collective-permute-start | bytes 2064392 | tf_op jit(solution)/shard_map/ppermute | solution.py:674
  6.7 16.9 %collective-permute-start.1 = (bf16[384,896]{1,0:T(8,128)(2,1)S(1)}, bf16[384,896]{1,0:T(8,128)(2,1)S(1)}, u32[]{:S(2)}, u32[]{:S(2)}) collective-permute-start(bf16[384,896]{1,0:T(8,128)(2,1)S(1)} %get-tuple-element.41), channel_id=1, source_target_pairs={{0,192},{64,0},{128,64},{192,128},{1,193},{65,1},{129,65},{193,129... | collective-permute-start | bytes 2064392 | tf_op jit(solution)/shard_map/ppermute | solution.py:675
  10.6 12.2 %copy-start.6 = (s32[2]{0:T(128)S(1)}, s32[2]{0:T(128)}, u32[]{:S(2)}) copy-start(s32[2]{0:T(128)} %constant.70.clone) | copy-start | bytes 28
  10.6 38.2 %all-to-all-start = ((bf16[64,8,896]{2,1,0:T(8,128)(2,1)}), bf16[64,8,896]{2,1,0:T(8,128)(2,1)}, u32[]{:S(2)}, u32[]{:S(2)}) async-start(bf16[64,8,896]{2,1,0:T(8,128)(2,1)} %bitcast.50), calls=%async_computation | async-start | bytes 1835008 | tf_op jit(solution)/shard_map/all_to_all | solution.py:650
  26.8 24.4 %collective-permute-start.2 = (bf16[384,896]{1,0:T(8,128)(2,1)}, bf16[384,896]{1,0:T(8,128)(2,1)S(1)}, u32[]{:S(2)}, u32[]{:S(2)}) collective-permute-start(bf16[384,896]{1,0:T(8,128)(2,1)} %get-tuple-element.42), channel_id=1, source_target_pairs={{0,64},{64,128},{128,192},{192,0},{1,65},{65,129},{129,193},{193,1... | collective-permute-start | bytes 2064392 | tf_op jit(solution)/shard_map/ppermute | solution.py:684
  28.0 23.2 %collective-permute-start.3 = (bf16[384,896]{1,0:T(8,128)(2,1)}, bf16[384,896]{1,0:T(8,128)(2,1)}, u32[]{:S(2)}, u32[]{:S(2)}) collective-permute-start(bf16[384,896]{1,0:T(8,128)(2,1)} %get-tuple-element.43), channel_id=1, source_target_pairs={{0,192},{64,0},{128,64},{192,128},{1,193},{65,1},{129,65},{193,129... | collective-permute-start | bytes 2064392 | tf_op jit(solution)/shard_map/ppermute | solution.py:685
  28.8 2.2 %copy-start.2 = (s32[4,4,16,1]{2,3,1,0:T(1,128)S(1)}, s32[4,4,16,1]{2,3,1,0:T(1,128)}, u32[]{:S(2)}) copy-start(s32[4,4,16,1]{2,3,1,0:T(1,128)} %param.19) | copy-start | bytes 3076
  28.8 2.2 %copy-start.3 = (s32[4,4,16,1]{2,3,1,0:T(1,128)S(1)}, s32[4,4,16,1]{2,3,1,0:T(1,128)}, u32[]{:S(2)}) copy-start(s32[4,4,16,1]{2,3,1,0:T(1,128)} %param.20) | copy-start | bytes 3076
  48.8 2.5 %copy-start = (bf16[512,896]{1,0:T(8,128)(2,1)S(1)}, bf16[512,896]{1,0:T(8,128)(2,1)}, u32[]{:S(2)}) copy-start(bf16[512,896]{1,0:T(8,128)(2,1)} %shard_map.172.mine_ref) | copy-start | bytes 2752516
  55.1 5.8 %copy-start.1 = (bf16[512,896]{1,0:T(8,128)(2,1)S(1)}, bf16[512,896]{1,0:T(8,128)(2,1)}, u32[]{:S(2)}) copy-start(bf16[512,896]{1,0:T(8,128)(2,1)} %get-tuple-element.51.carried_ref) | copy-start | bytes 2752516
  55.1 31.9 %all-to-all-start.1 = ((bf16[64,8,896]{2,1,0:T(8,128)(2,1)}), bf16[64,8,896]{2,1,0:T(8,128)(2,1)S(1)}, u32[]{:S(2)}, u32[]{:S(2)}) async-start(bf16[64,8,896]{2,1,0:T(8,128)(2,1)} %bitcast.53), calls=%async_computation.1 | async-start | bytes 1835008 | tf_op jit(solution)/shard_map/all_to_all | solution.py:650
  87.0 29.1 %all-to-all-start.2 = ((bf16[64,8,768]{2,1,0:T(8,128)(2,1)}), bf16[64,8,768]{2,1,0:T(8,128)(2,1)S(1)}, u32[]{:S(2)}, u32[]{:S(2)}) async-start(bf16[64,8,768]{2,1,0:T(8,128)(2,1)} %bitcast.54), calls=%async_computation.2 | async-start | bytes 1572864 | tf_op jit(solution)/shard_map/all_to_all | solution.py:650
  116.2 31.8 %all-to-all-start.3 = ((bf16[64,8,896]{2,1,0:T(8,128)(2,1)}), bf16[64,8,896]{2,1,0:T(8,128)(2,1)S(1)}, u32[]{:S(2)}, u32[]{:S(2)}) async-start(bf16[64,8,896]{2,1,0:T(8,128)(2,1)} %bitcast.52), calls=%async_computation.3 | async-start | bytes 1835008 | tf_op jit(solution)/shard_map/all_to_all | solution.py:650
  148.0 4.2 %copy-start.5 = (f32[4,16,4,512]{3,2,1,0:T(4,128)S(1)}, f32[4,16,4,512]{3,2,1,0:T(4,128)}, u32[]{:S(2)}) copy-start(f32[4,16,4,512]{3,2,1,0:T(4,128)} %param.18) | copy-start | bytes 1572868

commit v5 on v4

--- a/solution.py
+++ b/solution.py
@@ -562,14 +562,20 @@
 
 
 def finish_kernel(
-    node_ref, in_ref, matrix_ref, factor_ref, weight_hbm, part_hbm, kv_old, update_hbm, weight_new_hbm, kv_update_ref,
-    kv_new_hbm, weight, update, part, kv_new, sems,
+    node_ref, in_ref, matrix_hbm, factor_ref, weight_hbm, part_hbm, kv_old, update_hbm, weight_new_hbm, kv_update_ref,
+    kv_new_hbm, weight, update, part, kv_new, matrix_ref, sems,
 ):
+    matrices = [
+        pltpu.make_async_copy(matrix_hbm.at[kind], matrix_ref.at[kind], sems.at[3 + 2 * Q_OWN + kind]) for kind in range(2)
+    ]
+    matrices[0].start()
     fetch = pltpu.make_async_copy(weight_hbm, weight, sems.at[0])
     fetch.start()
+    matrices[1].start()
     part_fetch = pltpu.make_async_copy(part_hbm, part, sems.at[1])
     part_fetch.start()
     edge = SPLIT * LANE
+    matrices[0].wait()
     q_rows = dot(matrix_ref[0], in_ref[:, : edge + LANE])
     fetch.wait()
     copies = []
@@ -596,6 +602,7 @@
     kv_new[...] = (part[...].astype(F32) + dot(spread, rest)).astype(BF16)
     copies.append(pltpu.make_async_copy(kv_new, kv_new_hbm.at[0, 0, 1], sems.at[2 + 2 * Q_OWN]))
     copies[-1].start()
+    matrices[1].wait()
     kv_rows = dot(matrix_ref[1], in_ref[:, edge:])
     for r, ct, tile in tiles_of("kv"):
         rows, cols = place(tile)
@@ -628,7 +635,7 @@
         in_specs=[
             pl.BlockSpec(memory_space=pltpu.SMEM),
             HERE,
-            whole(2, ROWS, ROWS),
+            outside,
             whole(2, BLOCKS, LANE),
             outside,
             outside,
@@ -641,7 +648,8 @@
             pltpu.VMEM(q_dims, BF16),
             pltpu.VMEM((KV_ROWS, KV_COLS), BF16),
             pltpu.VMEM((KV_ROWS, KV_COLS), BF16),
-            pltpu.SemaphoreType.DMA((3 + 2 * Q_OWN,)),
+            pltpu.VMEM((2, ROWS, ROWS), BF16),
+            pltpu.SemaphoreType.DMA((5 + 2 * Q_OWN,)),
         ],
     )
 
@@ -684,7 +692,10 @@
     sum_last = lax.ppermute(to_next, "dp", forward)
     sum_next = lax.ppermute(to_last, "dp", backward)
     (mine,) = arrange_call(mine_kernel, turn(0), q_grads, kv_grads, peaks, (), (pltpu.HBM((ROWS, MSG), BF16),))
-    earlier = call(earlier_kernel, shape((ROWS, MSG), BF16), in_hbm(late_in), in_hbm(late_back))
+    earlier = call(
+        earlier_kernel, shape((ROWS, MSG), BF16), late_in, in_hbm(late_back),
+        in_specs=[HERE, HERE], out_specs=HERE,
+    )
 
     outside = pl.BlockSpec(memory_space=pltpu.HBM)
     message, carried = call(

time: 156 us -> 155 us (level)
  no operation moved by 1% of the time
where the time goes in v5:
time: 155 us; the launch traced here: 153 us
  waiting for transfers between devices  70.7 us (46%)
  Pallas kernels  44.3 us (29%)
  starting transfers between devices  33.9 us (22%)
  local copies, waits for them, and re-layouts  1.66 us (1%)
    all_to_all x4, waiting for transfers between devices, exchange(): lax.all_to_all(message, 'fsdp', split_axis=0, concat_axis=0, tiled=True)  69.9 us
    pallas_call x9, Pallas kernels, call(): pl.pallas_call(kernel, out_shape=out_shape, compiler_params=PARAMS, **opt...  35.8 us
    all_to_all x4, starting transfers between devices, exchange(): lax.all_to_all(message, 'fsdp', split_axis=0, concat_axis=0, tiled=True)  29.6 us
    pallas_call x3, Pallas kernels, arrange_call(): pl.pallas_call(kernel, out_shape=out_shape, grid_spec=pltpu.PrefetchScala...  8.43 us
  transfers between devices with their start and end apart: 8, of which 5 were waited for; matrix products, arithmetic and copies ran while one was open for 0% of the time, Pallas kernels for 22%

profile of v5, /device:TPU:2, one launch (start us, length us, event | category | flops | bytes accessed | tf_op | source)
XLA Modules:
  0.0 152.7 jit_solution(16041338170117274847)
XLA Ops:
  0.7 1.4 copy.28
  2.1 3.1 %shard_map.173 = (bf16[384,896]{1,0:T(8,128)(2,1)}, bf16[384,896]{1,0:T(8,128)(2,1)S(1)}) custom-call(s32[3]{0:T(128)S(1)} %and_select_fusion.group_ref, bf16[4,3,64,1536]{3,2,1,0:T(8,128)(2,1)} %bitcast.44, bf16[4,4,64,512]{3,2,1,0:T(8,128)(2,1)S(1)} %bitcast.28, bf16[4,3,64,1536]{3,2,1,0:T(8,128)(2,1)} %bitcast.45, bf16[4,4,64,512]{3,2,1,0:T(8,128)(2,1)S(1)} %bitcast.29, ...), custom_call_target="tpu_custom_call" | custom-call | tf_op jit(solution)/shard_map/pallas_call | solution.py:258
  5.2 1.5 collective-permute-start
  7.5 3.1 %shard_map.175 = bf16[512,896]{1,0:T(8,128)(2,1)} custom-call(bf16[1,1,2,192,1536]{4,3,2,1,0:T(8,128)(2,1)} %q_mom, bf16[1,1,2,256,512]{4,3,2,1,0:T(8,128)(2,1)} %kv_mom), custom_call_target="tpu_custom_call" | custom-call | tf_op jit(solution)/shard_map/pallas_call | solution.py:140
  10.6 12.2 %all-to-all-start = ((bf16[64,8,896]{2,1,0:T(8,128)(2,1)}), bf16[64,8,896]{2,1,0:T(8,128)(2,1)}, u32[]{:S(2)}, u32[]{:S(2)}) async-start(bf16[64,8,896]{2,1,0:T(8,128)(2,1)} %bitcast.50), calls=%async_computation | async-start | bytes 1835008 | tf_op jit(solution)/shard_map/all_to_all | solution.py:658
  23.6 3.2 %shard_map.174 = (bf16[384,896]{1,0:T(8,128)(2,1)}, bf16[384,896]{1,0:T(8,128)(2,1)}) custom-call(s32[2]{0:T(128)S(1)} %and_select_fusion.1.group_ref, bf16[4,3,64,1536]{3,2,1,0:T(8,128)(2,1)} %bitcast.47, bf16[4,4,64,512]{3,2,1,0:T(8,128)(2,1)S(1)} %bitcast.31, bf16[4,3,64,1536]{3,2,1,0:T(8,128)(2,1)} %bitcast.48, bf16[4,4,64,512]{3,2,1,0:T(8,128)(2,1)S(1)} %bitcast.32, ...), custom_call_target="tpu_custom_call" | custom-call | flops 999999995904 | bytes 10000000000 | tf_op jit(solution)/shard_map/pallas_call | solution.py:258
  26.8 1.2 collective-permute-start.2
  28.0 0.8 collective-permute-start.3
  28.8 2.2 %shard_map.172.mine_ref = bf16[512,896]{1,0:T(8,128)(2,1)} custom-call(s32[1]{0:T(128)S(6)} %select_n.32.group_ref, bf16[4,3,64,1536]{3,2,1,0:T(8,128)(2,1)} %bitcast.49, bf16[4,4,64,512]{3,2,1,0:T(8,128)(2,1)S(1)} %bitcast.33, f32[4,64]{1,0:T(4,128)S(1)} %bitcast.43), custom_call_target="tpu_custom_call" | custom-call | tf_op jit(solution)/shard_map/pallas_call | solution.py:258
  31.4 2.9 %shard_map.177 = (bf16[2,512,512]{2,1,0:T(8,128)(2,1)}, bf16[2,512,512]{2,1,0:T(8,128)(2,1)}, bf16[2,512,512]{2,1,0:T(8,128)(2,1)}) custom-call(bf16[2,4,64,64]{3,2,1,0:T(8,128)(2,1)S(1)} %get-tuple-element.46.table_ref), custom_call_target="tpu_custom_call" | custom-call | tf_op jit(solution)/shard_map/pallas_call | solution.py:140
  34.4 14.4 %all-to-all-done = bf16[64,8,896]{2,1,0:T(8,128)(2,1)} async-done(((bf16[64,8,896]{2,1,0:T(8,128)(2,1)}), bf16[64,8,896]{2,1,0:T(8,128)(2,1)}, u32[]{:S(2)}, u32[]{:S(2)}) %all-to-all-start) | async-done | bytes 917536 | tf_op jit(solution)/shard_map/all_to_all | solution.py:658
  48.8 2.4 %shard_map.178.earlier_ref = bf16[512,896]{1,0:T(8,128)(2,1)S(1)} custom-call(bf16[512,896]{1,0:T(8,128)(2,1)} %bitcast.10.late_in_ref, bf16[2,512,512]{2,1,0:T(8,128)(2,1)} %get-tuple-element.47.matrix_ref), custom_call_target="tpu_custom_call" | custom-call | tf_op jit(solution)/shard_map/pallas_call | solution.py:140
  51.2 3.9 %shard_map.179 = (bf16[512,896]{1,0:T(8,128)(2,1)}, bf16[512,896]{1,0:T(8,128)(2,1)}) custom-call(bf16[512,896]{1,0:T(8,128)(2,1)S(1)} %copy-done, bf16[384,896]{1,0:T(8,128)(2,1)S(1)} %collective-permute-done.2.last_ref, bf16[384,896]{1,0:T(8,128)(2,1)} %collective-permute-done.3.next_ref, bf16[384,896]{1,0:T(8,128)(2,1)S(1)} %collective-permute-done.from_last.first_last, ...), custom_call_target="tpu_custom_call" | custom-call | tf_op jit(solution)/shard_map/pallas_call | solution.py:140
  55.1 5.8 %all-to-all-start.1 = ((bf16[64,8,896]{2,1,0:T(8,128)(2,1)}), bf16[64,8,896]{2,1,0:T(8,128)(2,1)S(1)}, u32[]{:S(2)}, u32[]{:S(2)}) async-start(bf16[64,8,896]{2,1,0:T(8,128)(2,1)} %bitcast.53), calls=%async_computation.1 | async-start | bytes 1835008 | tf_op jit(solution)/shard_map/all_to_all | solution.py:658
  60.9 2.3 %shard_map.180 = (bf16[512,768]{1,0:T(8,128)(2,1)}, bf16[512,128]{1,0:T(8,128)(2,1)}) custom-call(bf16[512,896]{1,0:T(8,128)(2,1)S(1)} %copy-done.1, bf16[2,4,64,64]{3,2,1,0:T(8,128)(2,1)S(1)} %get-tuple-element.46.table_ref), custom_call_target="tpu_custom_call" | custom-call | tf_op jit(solution)/shard_map/pallas_call | solution.py:140
  63.2 23.8 %all-to-all-done.1 = bf16[64,8,896]{2,1,0:T(8,128)(2,1)S(1)} async-done(((bf16[64,8,896]{2,1,0:T(8,128)(2,1)}), bf16[64,8,896]{2,1,0:T(8,128)(2,1)S(1)}, u32[]{:S(2)}, u32[]{:S(2)}) %all-to-all-start.1) | async-done | bytes 917536 | tf_op jit(solution)/shard_map/all_to_all | solution.py:658
  87.0 5.9 %all-to-all-start.2 = ((bf16[64,8,768]{2,1,0:T(8,128)(2,1)}), bf16[64,8,768]{2,1,0:T(8,128)(2,1)S(1)}, u32[]{:S(2)}, u32[]{:S(2)}) async-start(bf16[64,8,768]{2,1,0:T(8,128)(2,1)} %bitcast.54), calls=%async_computation.2 | async-start | bytes 1572864 | tf_op jit(solution)/shard_map/all_to_all | solution.py:658
  92.9 15.5 %shard_map.181 = (bf16[512,896]{1,0:T(8,128)(2,1)}, bf16[1,1,2,192,1536]{4,3,2,1,0:T(8,128)(2,1)}, bf16[1,1,2,256,512]{4,3,2,1,0:T(8,128)(2,1)}) custom-call(s32[1]{0:T(128)} %bitcast.node_ref, bf16[512,896]{1,0:T(8,128)(2,1)S(1)} %bitcast.34, bf16[1,1,2,192,1536]{4,3,2,1,0:T(8,128)(2,1)} %q_mom, bf16[1,1,2,256,512]{4,3,2,1,0:T(8,128)(2,1)} %kv_mom, ...), custom_call_target="tpu_custom_call" | custom-call | tf_op jit(solution)/shard_map/pallas_call | solution.py:140
  108.4 7.7 %all-to-all-done.2 = bf16[64,8,768]{2,1,0:T(8,128)(2,1)S(1)} async-done(((bf16[64,8,768]{2,1,0:T(8,128)(2,1)}), bf16[64,8,768]{2,1,0:T(8,128)(2,1)S(1)}, u32[]{:S(2)}, u32[]{:S(2)}) %all-to-all-start.2) | async-done | bytes 786464 | tf_op jit(solution)/shard_map/all_to_all | solution.py:658
  116.2 5.7 %all-to-all-start.3 = ((bf16[64,8,896]{2,1,0:T(8,128)(2,1)}), bf16[64,8,896]{2,1,0:T(8,128)(2,1)S(1)}, u32[]{:S(2)}, u32[]{:S(2)}) async-start(bf16[64,8,896]{2,1,0:T(8,128)(2,1)} %bitcast.52), calls=%async_computation.3 | async-start | bytes 1835008 | tf_op jit(solution)/shard_map/all_to_all | solution.py:658
  121.9 1.8 %shard_map.182 = (bf16[1,1,2,192,1536]{4,3,2,1,0:T(8,128)(2,1)}, bf16[256,512]{1,0:T(8,128)(2,1)}, f32[2,64,128]{2,1,0:T(8,128)S(1)}) custom-call(bf16[512,768]{1,0:T(8,128)(2,1)S(1)} %bitcast.37, bf16[512,896]{1,0:T(8,128)(2,1)S(1)} %bitcast.35, bf16[1,1,2,192,1536]{4,3,2,1,0:T(8,128)(2,1)} %get-tuple-element.61.q_old), custom_call_target="tpu_custom_call", output_to_operand_aliasing={{0}: (2, {})} | custom-call | tf_op jit(solution)/shard_map/pallas_call | solution.py:140
  124.0 24.0 %all-to-all-done.3 = bf16[64,8,896]{2,1,0:T(8,128)(2,1)S(1)} async-done(((bf16[64,8,896]{2,1,0:T(8,128)(2,1)}), bf16[64,8,896]{2,1,0:T(8,128)(2,1)S(1)}, u32[]{:S(2)}, u32[]{:S(2)}) %all-to-all-start.3) | async-done | bytes 917536 | tf_op jit(solution)/shard_map/all_to_all | solution.py:658
  148.0 3.5 %shard_map.183 = (bf16[4,3,16,1536]{3,2,1,0:T(8,128)(2,1)}, f32[4,3,16,1536]{3,2,1,0:T(8,128)}, bf16[4,64,512]{2,1,0:T(8,128)(2,1)S(1)}, bf16[1,1,2,256,512]{4,3,2,1,0:T(8,128)(2,1)}) custom-call(s32[1]{0:T(128)} %bitcast.node_ref, bf16[512,896]{1,0:T(8,128)(2,1)S(1)} %bitcast.36, ...), custom_call_target="tpu_custom_call", output_to_operand_aliasing={{3}: (6, {})} | custom-call | tf_op jit(solution)/shard_map/pallas_call | solution.py:140
  151.4 1.3 subtract_multiply_fusion
  (28 shorter events, 2.3 us)
Async XLA Ops:
  0.6 1.5 copy-start.7
  0.6 1.5 copy-start.4
  5.2 17.6 %collective-permute-start = (bf16[384,896]{1,0:T(8,128)(2,1)}, bf16[384,896]{1,0:T(8,128)(2,1)S(1)}, u32[]{:S(2)}, u32[]{:S(2)}) collective-permute-start(bf16[384,896]{1,0:T(8,128)(2,1)} %get-tuple-element.40), channel_id=1, source_target_pairs={{0,64},{64,128},{128,192},{192,0},{1,65},{65,129},{129,193},{193,1... | collective-permute-start | bytes 2064392 | tf_op jit(solution)/shard_map/ppermute | solution.py:682
  6.7 16.9 %collective-permute-start.1 = (bf16[384,896]{1,0:T(8,128)(2,1)S(1)}, bf16[384,896]{1,0:T(8,128)(2,1)S(1)}, u32[]{:S(2)}, u32[]{:S(2)}) collective-permute-start(bf16[384,896]{1,0:T(8,128)(2,1)S(1)} %get-tuple-element.41), channel_id=1, source_target_pairs={{0,192},{64,0},{128,64},{192,128},{1,193},{65,1},{129,65},{193,129... | collective-permute-start | bytes 2064392 | tf_op jit(solution)/shard_map/ppermute | solution.py:683
  10.6 12.2 %copy-start.6 = (s32[2]{0:T(128)S(1)}, s32[2]{0:T(128)}, u32[]{:S(2)}) copy-start(s32[2]{0:T(128)} %constant.70.clone) | copy-start | bytes 28
  10.6 38.2 %all-to-all-start = ((bf16[64,8,896]{2,1,0:T(8,128)(2,1)}), bf16[64,8,896]{2,1,0:T(8,128)(2,1)}, u32[]{:S(2)}, u32[]{:S(2)}) async-start(bf16[64,8,896]{2,1,0:T(8,128)(2,1)} %bitcast.50), calls=%async_computation | async-start | bytes 1835008 | tf_op jit(solution)/shard_map/all_to_all | solution.py:658
  26.8 24.4 %collective-permute-start.2 = (bf16[384,896]{1,0:T(8,128)(2,1)}, bf16[384,896]{1,0:T(8,128)(2,1)S(1)}, u32[]{:S(2)}, u32[]{:S(2)}) collective-permute-start(bf16[384,896]{1,0:T(8,128)(2,1)} %get-tuple-element.42), channel_id=1, source_target_pairs={{0,64},{64,128},{128,192},{192,0},{1,65},{65,129},{129,193},{193,1... | collective-permute-start | bytes 2064392 | tf_op jit(solution)/shard_map/ppermute | solution.py:692
  28.0 23.2 %collective-permute-start.3 = (bf16[384,896]{1,0:T(8,128)(2,1)}, bf16[384,896]{1,0:T(8,128)(2,1)}, u32[]{:S(2)}, u32[]{:S(2)}) collective-permute-start(bf16[384,896]{1,0:T(8,128)(2,1)} %get-tuple-element.43), channel_id=1, source_target_pairs={{0,192},{64,0},{128,64},{192,128},{1,193},{65,1},{129,65},{193,129... | collective-permute-start | bytes 2064392 | tf_op jit(solution)/shard_map/ppermute | solution.py:693
  28.8 2.2 %copy-start.2 = (s32[4,4,16,1]{2,3,1,0:T(1,128)S(1)}, s32[4,4,16,1]{2,3,1,0:T(1,128)}, u32[]{:S(2)}) copy-start(s32[4,4,16,1]{2,3,1,0:T(1,128)} %param.19) | copy-start | bytes 3076
  28.8 2.2 %copy-start.3 = (s32[4,4,16,1]{2,3,1,0:T(1,128)S(1)}, s32[4,4,16,1]{2,3,1,0:T(1,128)}, u32[]{:S(2)}) copy-start(s32[4,4,16,1]{2,3,1,0:T(1,128)} %param.20) | copy-start | bytes 3076
  48.8 2.5 %copy-start = (bf16[512,896]{1,0:T(8,128)(2,1)S(1)}, bf16[512,896]{1,0:T(8,128)(2,1)}, u32[]{:S(2)}) copy-start(bf16[512,896]{1,0:T(8,128)(2,1)} %shard_map.172.mine_ref) | copy-start | bytes 2752516
  55.1 5.8 %copy-start.1 = (bf16[512,896]{1,0:T(8,128)(2,1)S(1)}, bf16[512,896]{1,0:T(8,128)(2,1)}, u32[]{:S(2)}) copy-start(bf16[512,896]{1,0:T(8,128)(2,1)} %get-tuple-element.51.carried_ref) | copy-start | bytes 2752516
  55.1 31.9 %all-to-all-start.1 = ((bf16[64,8,896]{2,1,0:T(8,128)(2,1)}), bf16[64,8,896]{2,1,0:T(8,128)(2,1)S(1)}, u32[]{:S(2)}, u32[]{:S(2)}) async-start(bf16[64,8,896]{2,1,0:T(8,128)(2,1)} %bitcast.53), calls=%async_computation.1 | async-start | bytes 1835008 | tf_op jit(solution)/shard_map/all_to_all | solution.py:658
  87.0 29.1 %all-to-all-start.2 = ((bf16[64,8,768]{2,1,0:T(8,128)(2,1)}), bf16[64,8,768]{2,1,0:T(8,128)(2,1)S(1)}, u32[]{:S(2)}, u32[]{:S(2)}) async-start(bf16[64,8,768]{2,1,0:T(8,128)(2,1)} %bitcast.54), calls=%async_computation.2 | async-start | bytes 1572864 | tf_op jit(solution)/shard_map/all_to_all | solution.py:658
  116.2 31.8 %all-to-all-start.3 = ((bf16[64,8,896]{2,1,0:T(8,128)(2,1)}), bf16[64,8,896]{2,1,0:T(8,128)(2,1)S(1)}, u32[]{:S(2)}, u32[]{:S(2)}) async-start(bf16[64,8,896]{2,1,0:T(8,128)(2,1)} %bitcast.52), calls=%async_computation.3 | async-start | bytes 1835008 | tf_op jit(solution)/shard_map/all_to_all | solution.py:658
  148.0 3.5 %copy-start.5 = (f32[4,16,4,512]{3,2,1,0:T(4,128)S(1)}, f32[4,16,4,512]{3,2,1,0:T(4,128)}, u32[]{:S(2)}) copy-start(f32[4,16,4,512]{3,2,1,0:T(4,128)} %param.18) | copy-start | bytes 1572868
